TPU v7x, 32 devices: a whole 2x2x4 slice. The times are simulated.
32 devices in a mesh: rows: 4 (over z), hid: 4 (over x, core), wid: 2 (over y).
Axes of the slice: x: 2, y: 2, z: 4, core: 2. Of those that a mesh axis runs over, the one named last changes fastest.
Arguments:
- inputs: bfloat16 [2, 8, 512, 1536], P(None, 'rows', 'hid', 'wid'), may hold values from -6 to 6
- starts: int32 [2, 8, 4], P(None, 'rows'), may hold values from 0 to 511, as said below
- norm_one: float32 [1536], P('wid'), may hold values from 0.5 to 1.5
- w_query: bfloat16 [1536, 1536], P('wid', 'hid'), may hold values from -0.15625 to 0.15625
- w_key: bfloat16 [1536, 1536], P('wid', 'hid'), may hold values from -0.15625 to 0.15625
- w_value: bfloat16 [1536, 1536], P('wid', 'hid'), may hold values from -0.15625 to 0.15625
- w_house: bfloat16 [1536, 1536], P('wid', 'hid'), may hold values from -0.15625 to 0.15625
- strength_weight: bfloat16 [1536, 12], P('wid', 'hid'), may hold values from -0.15625 to 0.15625
- b_beta: float32 [12], P('hid'), may hold values from -3 to 3
- w_out: bfloat16 [1536, 1536], P('hid', 'wid'), may hold values from -0.625 to 0.625
- norm_two: float32 [1536], P('wid'), may hold values from 0.5 to 1.5
- gate_weight: bfloat16 [1536, 4096], P('wid', 'hid'), may hold values from -0.15625 to 0.15625
- up_weight: bfloat16 [1536, 4096], P('wid', 'hid'), may hold values from -0.15625 to 0.15625
- w_down: bfloat16 [4096, 1536], P('hid', 'wid'), may hold values from -0.09375 to 0.09375
- cotangent: bfloat16 [2, 8, 512, 1536], P(None, 'rows', 'hid', 'wid'), may hold values from -6 to 6
Outputs:
- output: bfloat16 [2, 8, 512, 1536], P(None, 'rows', 'hid', 'wid')
- grad_input: float32 [2, 8, 512, 1536], P(None, 'rows', 'hid', 'wid')
- grad_norm_one: float32 [1536], P('wid')
- grad_query: float32 [1536, 1536], P('wid', 'hid')
- grad_key: float32 [1536, 1536], P('wid', 'hid')
- grad_value: float32 [1536, 1536], P('wid', 'hid')
- grad_house: float32 [1536, 1536], P('wid', 'hid')
- grad_beta_weight: float32 [1536, 12], P('wid', 'hid')
- grad_beta_bias: float32 [12], P('hid')
- grad_out: float32 [1536, 1536], P('hid', 'wid')
- grad_norm_two: float32 [1536], P('wid')
- grad_gate: float32 [1536, 4096], P('wid', 'hid')
- grad_up: float32 [1536, 4096], P('wid', 'hid')
- grad_down: float32 [4096, 1536], P('hid', 'wid')
Inputs may be any that keep to these rules, and one draw needn't show every extreme that they name: In each packed row the 4 starts rise strictly and the first is 0.
All inputs are finite; a program needn't handle non-finite values.
Results may differ from a plain program's by a relative error of at most 0.02.
Values may be sent and summed in bfloat16 or wider, within the bound.
No kernel may reach another device: no remote copies, remote signals or barrier semaphores. Data moves between devices by JAX's collectives and lax.ppermute only.
A program may use at most 256 MiB of HBM per device.

v0:
```python
import jax
import jax.numpy as jnp
from jax import lax
from jax.sharding import PartitionSpec as P

EPS = 1e-06


def households(query, keys, values, house, braw, row_starts):
    length = query.shape[0]
    heads = braw.shape[1]
    high = lax.Precision.HIGHEST

    def split(arr):
        return arr.reshape(length, heads, -1).transpose(1, 0, 2)

    qh, kh, vh, uh = (split(query), split(keys), split(values), split(house))
    wdir = uh * lax.rsqrt(jnp.sum(uh * uh, -1, keepdims=True) + EPS)
    beta = 2.0 * jax.nn.sigmoid(braw).T
    place = jnp.arange(length)
    docs = jnp.sum((place[:, None] >= row_starts[None, :]).astype(jnp.int32), 1)
    below = place[:, None] > place[None, :]
    upto = place[:, None] >= place[None, :]
    allowed = upto & (docs[:, None] == docs[None, :])
    mixing = jnp.einsum("hid,hjd->hij", wdir, wdir, precision=high)
    system = jnp.eye(length, dtype=query.dtype) + jnp.where(below, mixing, 0.0) * beta[:, None, :]
    right = jnp.where(below, jnp.einsum("hid,hjd->hij", wdir, kh, precision=high), 0.0)
    coeff = jax.scipy.linalg.solve_triangular(system, right, lower=True, unit_diagonal=True)
    direct = jnp.where(upto, jnp.einsum("hid,hjd->hij", qh, kh, precision=high), 0.0)
    cross = (
        jnp.where(upto, jnp.einsum("hid,hjd->hij", qh, wdir, precision=high), 0.0)
        * beta[:, None, :]
    )
    scores = (direct - jnp.einsum("hit,htj->hij", cross, coeff, precision=high)) / jnp.sqrt(
        float(qh.shape[-1])
    )
    scores = jnp.where(allowed, scores, -1e30)
    top = jnp.max(scores, -1, keepdims=True)
    weights = jnp.exp(scores - top)
    weights = weights / jnp.sum(weights, -1, keepdims=True)
    result = jnp.einsum("hij,hjd->hid", weights, vh, precision=high)
    return result.transpose(1, 0, 2).reshape(length, -1)


def width_sum(value):
    return lax.psum(jnp.sum(value, -1), "wid")


def rms_scale(hidden, width):
    return lax.rsqrt(width_sum(hidden * hidden) / width + EPS)[..., None]


def rms_back(hidden, gain, scale, grad, width):
    inner = width_sum(hidden * gain * grad)[..., None]
    return scale * gain * grad - hidden * scale * scale * scale * inner / width


def gather_rows(normed):
    return lax.all_gather(normed, "hid", axis=1, tiled=True)


def project_sum(first, second):
    return (
        lax.psum_scatter(first, "wid", scatter_dimension=0, tiled=True),
        lax.psum_scatter(second, "wid", scatter_dimension=0, tiled=True),
    )


def project_grads(first, second):
    return (
        lax.all_gather(first, "wid", axis=0, tiled=True),
        lax.all_gather(second, "wid", axis=0, tiled=True),
    )


def branch_forward(values, weight_matrix):
    complete_rows = lax.all_gather(values, "wid", axis=0, tiled=True)
    part = jnp.einsum(
        "act,tx->acx", complete_rows, weight_matrix, preferred_element_type=jnp.float32
    )
    return (complete_rows, lax.psum_scatter(part, "hid", scatter_dimension=1, tiled=True))


def branch_backward(grad_low, complete_rows, weight_matrix):
    gradient_whole = lax.all_gather(grad_low, "hid", axis=1, tiled=True)
    weight_gradient = jnp.einsum(
        "yxw,yxf->wf", complete_rows, gradient_whole, preferred_element_type=jnp.float32
    )
    part = jnp.einsum(
        "wfp,op->wfo", gradient_whole, weight_matrix, preferred_element_type=jnp.float32
    )
    return (weight_gradient, lax.psum_scatter(part, "wid", scatter_dimension=0, tiled=True))


def norm_grad_sum(part):
    return lax.psum_scatter(part, "hid", scatter_dimension=1, tiled=True)


def on_device(
    inputs,
    starts,
    norm_one,
    w_query,
    w_key,
    w_value,
    w_house,
    strength_weight,
    b_beta,
    w_out,
    norm_two,
    gate_weight,
    up_weight,
    w_down,
    cotangent,
):
    width = inputs.shape[-1] * lax.axis_size("wid")
    head_cols = w_query.shape[1]
    head_weight_matrix = jnp.concatenate([w_query, w_key, w_value, w_house], 1)
    place = lax.axis_index("wid")
    single_float = jnp.float32
    totals = None
    gain_one_grad = jnp.zeros(norm_one.shape, single_float)
    gain_two_grad = jnp.zeros(norm_two.shape, single_float)
    results, input_grads = ([], [])
    for micro in range(inputs.shape[0]):
        start = inputs[micro].astype(single_float)
        row_starts = lax.dynamic_index_in_dim(starts[micro], place, 0, keepdims=False)
        scale_one = rms_scale(start, width)
        normed = (start * scale_one * norm_one).astype(jnp.bfloat16)
        normalized_whole = gather_rows(normed)
        head_portion = jnp.einsum(
            "act,tx->acx", normalized_whole, head_weight_matrix, preferred_element_type=single_float
        )
        strength_portion = jnp.einsum(
            "act,tx->acx", normalized_whole, strength_weight, preferred_element_type=single_float
        )
        head_sum, beta_sum = project_sum(head_portion, strength_portion)
        head_proj = head_sum[0]
        beta_proj = beta_sum[0]
        beta_raw = beta_proj + b_beta
        query = head_proj[:, :head_cols]
        keys = head_proj[:, head_cols : 2 * head_cols]
        values = head_proj[:, 2 * head_cols : 3 * head_cols]
        house = head_proj[:, 3 * head_cols :]
        attn, attn_pull = jax.vjp(
            lambda a, b, c, d, e: households(a, b, c, d, e, row_starts),
            query,
            keys,
            values,
            house,
            beta_raw,
        )
        attn_full, branch = branch_forward(attn.astype(jnp.bfloat16)[None], w_out)
        middle = start + branch
        scale_two = rms_scale(middle, width)
        normed_two = (middle * scale_two * norm_two).astype(jnp.bfloat16)
        second_normalized_whole = gather_rows(normed_two)
        gate_portion = jnp.einsum(
            "act,tx->acx", second_normalized_whole, gate_weight, preferred_element_type=single_float
        )
        up_portion = jnp.einsum(
            "act,tx->acx", second_normalized_whole, up_weight, preferred_element_type=single_float
        )
        gate, upper = project_sum(gate_portion, up_portion)
        sigma = jax.nn.sigmoid(gate)
        swish = gate * sigma
        act_full, feed = branch_forward((swish * upper).astype(jnp.bfloat16), w_down)
        results.append((middle + feed).astype(jnp.bfloat16))
        grad_out = cotangent[micro]
        down_grad, d_act = branch_backward(grad_out, act_full, w_down)
        d_gate = (d_act * upper * sigma * (1.0 + gate * (1.0 - sigma))).astype(jnp.bfloat16)
        d_up = (d_act * swish).astype(jnp.bfloat16)
        gate_gradient_whole, up_gradient_whole = project_grads(d_gate, d_up)
        gate_grad = jnp.einsum(
            "yxw,yxf->wf",
            second_normalized_whole,
            gate_gradient_whole,
            preferred_element_type=single_float,
        )
        up_gradient = jnp.einsum(
            "yxw,yxf->wf",
            second_normalized_whole,
            up_gradient_whole,
            preferred_element_type=single_float,
        )
        d_normed_two = norm_grad_sum(
            jnp.einsum(
                "wfp,op->wfo", gate_gradient_whole, gate_weight, preferred_element_type=single_float
            )
            + jnp.einsum(
                "wfp,op->wfo", up_gradient_whole, up_weight, preferred_element_type=single_float
            )
        )
        gain_two_grad = gain_two_grad + jnp.sum(d_normed_two * middle * scale_two, (0, 1))
        d_middle = grad_out.astype(single_float) + rms_back(
            middle, norm_two, scale_two, d_normed_two, width
        )
        out_grad, d_attn = branch_backward(d_middle.astype(jnp.bfloat16), attn_full, w_out)
        d_query, d_keys, d_values, d_house, d_beta = attn_pull(d_attn[0])
        d_heads = jnp.concatenate([d_query, d_keys, d_values, d_house], -1).astype(jnp.bfloat16)[
            None
        ]
        d_beta_low = d_beta.astype(jnp.bfloat16)[None]
        head_gradient_whole, strength_gradient_whole = project_grads(d_heads, d_beta_low)
        heads_grad = jnp.einsum(
            "yxw,yxf->wf",
            normalized_whole,
            head_gradient_whole,
            preferred_element_type=single_float,
        )
        strength_gradient = jnp.einsum(
            "yxw,yxf->wf",
            normalized_whole,
            strength_gradient_whole,
            preferred_element_type=single_float,
        )
        bias_grad = jnp.sum(strength_gradient_whole.astype(single_float), (0, 1))
        d_normed = norm_grad_sum(
            jnp.einsum(
                "wfp,op->wfo",
                head_gradient_whole,
                head_weight_matrix,
                preferred_element_type=single_float,
            )
            + jnp.einsum(
                "wfp,op->wfo",
                strength_gradient_whole,
                strength_weight,
                preferred_element_type=single_float,
            )
        )
        gain_one_grad = gain_one_grad + jnp.sum(d_normed * start * scale_one, (0, 1))
        input_grads.append(d_middle + rms_back(start, norm_one, scale_one, d_normed, width))
        current = [
            heads_grad,
            strength_gradient,
            bias_grad,
            out_grad,
            gate_grad,
            up_gradient,
            down_grad,
        ]
        totals = current if totals is None else [a + b for a, b in zip(totals, current)]
    totals = list(
        (
            lax.psum(totals[0].astype(jnp.bfloat16), "rows").astype(jnp.float32),
            lax.psum(totals[1].astype(jnp.bfloat16), "rows").astype(jnp.float32),
            lax.psum(totals[2].astype(jnp.bfloat16), "rows").astype(jnp.float32),
            lax.psum(totals[3].astype(jnp.bfloat16), "rows").astype(jnp.float32),
            lax.psum(totals[4].astype(jnp.bfloat16), "rows").astype(jnp.float32),
            lax.psum(totals[5].astype(jnp.bfloat16), "rows").astype(jnp.float32),
            lax.psum(totals[6].astype(jnp.bfloat16), "rows").astype(jnp.float32),
        )
    )
    gain_one_total, gain_two_total = lax.psum((gain_one_grad, gain_two_grad), ("rows", "hid"))
    heads_total = totals[0]
    return (
        jnp.stack(results),
        jnp.stack(input_grads),
        gain_one_total,
        heads_total[:, :head_cols],
        heads_total[:, head_cols : 2 * head_cols],
        heads_total[:, 2 * head_cols : 3 * head_cols],
        heads_total[:, 3 * head_cols :],
        totals[1],
        totals[2],
        totals[3],
        gain_two_total,
        totals[4],
        totals[5],
        totals[6],
    )


def solution(mesh):
    return jax.shard_map(
        on_device,
        mesh=mesh,
        in_specs=(
            P(None, "rows", "hid", "wid"),
            P(None, "rows", None),
            P("wid"),
            P("wid", "hid"),
            P("wid", "hid"),
            P("wid", "hid"),
            P("wid", "hid"),
            P("wid", "hid"),
            P("hid"),
            P("hid", "wid"),
            P("wid"),
            P("wid", "hid"),
            P("wid", "hid"),
            P("hid", "wid"),
            P(None, "rows", "hid", "wid"),
        ),
        out_specs=(
            P(None, "rows", "hid", "wid"),
            P(None, "rows", "hid", "wid"),
            P("wid"),
            P("wid", "hid"),
            P("wid", "hid"),
            P("wid", "hid"),
            P("wid", "hid"),
            P("wid", "hid"),
            P("hid"),
            P("hid", "wid"),
            P("wid"),
            P("wid", "hid"),
            P("wid", "hid"),
            P("hid", "wid"),
        ),
        check_vma=False,
    )
```

profile of v0, /device:TPU:0, one launch (start us, length us, event | category | flops | bytes accessed | tf_op | source)
XLA Modules:
  0.0 2224.7 jit_solution(6756981037784477710)
XLA Ops:
  83.2 57.2 %reduce-scatter.29.cloned.1.call-done = f32[1,512,1536]{2,1,0:T(8,128)} async-done(((f32[2,512,1536]{2,1,0:T(8,128)}), f32[1,512,1536]{2,1,0:T(8,128)}) %reduce-scatter.29.cloned.1.call-update) | async-done | bytes 3145744 | tf_op jit(solution)/shard_map/reduce_scatter | solution.py:64
  173.9 45.9 %reduce-scatter.19.cloned.1.call-done = f32[1,512,1536]{2,1,0:T(8,128)} async-done(((f32[2,512,1536]{2,1,0:T(8,128)}), f32[1,512,1536]{2,1,0:T(8,128)}) %reduce-scatter.19.cloned.1.call-update) | async-done | bytes 3145744 | tf_op jit(solution)/shard_map/reduce_scatter | solution.py:64
  249.1 119.4 %custom-call.13 = f32[3,4,128,128]{2,3,1,0:T(8,128)} custom-call(f32[3,4,128,128]{3,2,1,0:T(8,128)} %bitcast.539), custom_call_target="InvertDiagBlocksLowerTriangular" | custom-call | tf_op jit(solution)/shard_map/jvp(jit(_solve_triangular))/vmap()/triangular_solve | solution.py:28
  448.1 119.5 %custom-call.12 = f32[3,4,128,128]{2,3,1,0:T(8,128)} custom-call(f32[3,4,128,128]{3,2,1,0:T(8,128)} %bitcast.538), custom_call_target="InvertDiagBlocksLowerTriangular" | custom-call | tf_op jit(solution)/shard_map/jvp(jit(_solve_triangular))/vmap()/triangular_solve | solution.py:28
  625.9 36.0 %reduce-scatter.21.cloned.1.call-done = f32[2,128,768]{2,1,0:T(8,128)} async-done(((f32[2,512,768]{2,1,0:T(8,128)}), f32[2,128,768]{2,1,0:T(8,128)}) %reduce-scatter.21.cloned.1.call-update) | async-done | bytes 786448 | tf_op jit(solution)/shard_map/reduce_scatter | solution.py:81
  716.6 45.7 %reduce-scatter.39.cloned.1.call-done = f32[1,512,1024]{2,1,0:T(8,128)} async-done(((f32[2,512,1024]{2,1,0:T(8,128)}), f32[1,512,1024]{2,1,0:T(8,128)}) %reduce-scatter.39.cloned.1.call-update) | async-done | bytes 2097168 | tf_op jit(solution)/shard_map/reduce_scatter | solution.py:92
  762.3 56.6 %reduce-scatter.25.cloned.1.call-done = f32[1,512,1024]{2,1,0:T(8,128)} async-done(((f32[2,512,1024]{2,1,0:T(8,128)}), f32[1,512,1024]{2,1,0:T(8,128)}) %reduce-scatter.25.cloned.1.call-update) | async-done | bytes 2097168 | tf_op jit(solution)/shard_map/reduce_scatter | solution.py:65
  818.8 56.7 %reduce-scatter.23.cloned.1.call-done = f32[1,512,1024]{2,1,0:T(8,128)} async-done(((f32[2,512,1024]{2,1,0:T(8,128)}), f32[1,512,1024]{2,1,0:T(8,128)}) %reduce-scatter.23.cloned.1.call-update) | async-done | bytes 2097168 | tf_op jit(solution)/shard_map/reduce_scatter | solution.py:64
  882.6 32.5 %all-gather.33.cloned.1.call-done = bf16[2,512,1024]{2,1,0:T(8,128)(2,1)} async-done(((bf16[1,512,1024]{2,1,0:T(8,128)(2,1)}), bf16[2,512,1024]{2,1,0:T(8,128)(2,1)}) %all-gather.33.cloned.1.call-update) | async-done | bytes 2097168 | tf_op jit(solution)/shard_map/all_gather | solution.py:71
  920.1 30.3 %all-gather.35.cloned.1.call-done = bf16[2,512,1024]{2,1,0:T(8,128)(2,1)} async-done(((bf16[1,512,1024]{2,1,0:T(8,128)(2,1)}), bf16[2,512,1024]{2,1,0:T(8,128)(2,1)}) %all-gather.35.cloned.1.call-update) | async-done | bytes 2097168 | tf_op jit(solution)/shard_map/all_gather | solution.py:72
  957.5 37.4 %reduce-scatter.41.cloned.1.call-done = f32[2,128,768]{2,1,0:T(8,128)} async-done(((f32[2,512,768]{2,1,0:T(8,128)}), f32[2,128,768]{2,1,0:T(8,128)}) %reduce-scatter.41.cloned.1.call-update) | async-done | bytes 786448 | tf_op jit(solution)/shard_map/reduce_scatter | solution.py:96
  1049.8 45.0 %reduce-scatter.47.cloned.1.call-done = f32[1,512,1024]{2,1,0:T(8,128)} async-done(((f32[2,512,1024]{2,1,0:T(8,128)}), f32[1,512,1024]{2,1,0:T(8,128)}) %reduce-scatter.47.cloned.1.call-update) | async-done | bytes 2097168 | tf_op jit(solution)/shard_map/reduce_scatter | solution.py:92
  1094.8 56.6 %reduce-scatter.35.cloned.1.call-done = f32[1,512,1024]{2,1,0:T(8,128)} async-done(((f32[2,512,1024]{2,1,0:T(8,128)}), f32[1,512,1024]{2,1,0:T(8,128)}) %reduce-scatter.35.cloned.1.call-update) | async-done | bytes 2097168 | tf_op jit(solution)/shard_map/reduce_scatter | solution.py:65
  1151.4 56.6 %reduce-scatter.33.cloned.1.call-done = f32[1,512,1024]{2,1,0:T(8,128)} async-done(((f32[2,512,1024]{2,1,0:T(8,128)}), f32[1,512,1024]{2,1,0:T(8,128)}) %reduce-scatter.33.cloned.1.call-update) | async-done | bytes 2097168 | tf_op jit(solution)/shard_map/reduce_scatter | solution.py:64
  1215.9 31.7 %all-gather.41.cloned.1.call-done = bf16[2,512,1024]{2,1,0:T(8,128)(2,1)} async-done(((bf16[1,512,1024]{2,1,0:T(8,128)(2,1)}), bf16[2,512,1024]{2,1,0:T(8,128)(2,1)}) %all-gather.41.cloned.1.call-update) | async-done | bytes 2097168 | tf_op jit(solution)/shard_map/all_gather | solution.py:71
  1252.7 30.3 %all-gather.43.cloned.1.call-done = bf16[2,512,1024]{2,1,0:T(8,128)(2,1)} async-done(((bf16[1,512,1024]{2,1,0:T(8,128)(2,1)}), bf16[2,512,1024]{2,1,0:T(8,128)(2,1)}) %all-gather.43.cloned.1.call-update) | async-done | bytes 2097168 | tf_op jit(solution)/shard_map/all_gather | solution.py:72
  1289.5 28.8 %all-gather.31.cloned.1.call-done = bf16[2,512,1024]{2,1,0:T(8,128)(2,1)} async-done(((bf16[1,512,1024]{2,1,0:T(8,128)(2,1)}), bf16[2,512,1024]{2,1,0:T(8,128)(2,1)}) %all-gather.31.cloned.1.call-update) | async-done | bytes 2097168 | tf_op jit(solution)/shard_map/all_gather | solution.py:77
  1323.4 35.6 %reduce-scatter.49.cloned.1.call-done = f32[2,128,768]{2,1,0:T(8,128)} async-done(((f32[2,512,768]{2,1,0:T(8,128)}), f32[2,128,768]{2,1,0:T(8,128)}) %reduce-scatter.49.cloned.1.call-update) | async-done | bytes 786448 | tf_op jit(solution)/shard_map/reduce_scatter | solution.py:96
  1365.8 33.5 %reduce-scatter.37.cloned.1.call-done = f32[2,128,768]{2,1,0:T(8,128)} async-done(((f32[2,512,768]{2,1,0:T(8,128)}), f32[2,128,768]{2,1,0:T(8,128)}) %reduce-scatter.37.cloned.1.call-update) | async-done | bytes 786448 | tf_op jit(solution)/shard_map/reduce_scatter | solution.py:81
  1739.1 35.1 %all-gather.39.cloned.1.call-done = bf16[2,512,1536]{2,1,0:T(8,128)(2,1)} async-done(((bf16[1,512,1536]{2,1,0:T(8,128)(2,1)}), bf16[2,512,1536]{2,1,0:T(8,128)(2,1)}) %all-gather.39.cloned.1.call-update) | async-done | bytes 3145744 | tf_op jit(solution)/shard_map/all_gather | solution.py:71
  1781.7 27.8 %all-gather.25.cloned.1.call-done = bf16[2,512,1024]{2,1,0:T(8,128)(2,1)} async-done(((bf16[1,512,1024]{2,1,0:T(8,128)(2,1)}), bf16[2,512,1024]{2,1,0:T(8,128)(2,1)}) %all-gather.25.cloned.1.call-update) | async-done | bytes 2097168 | tf_op jit(solution)/shard_map/all_gather | solution.py:77
  1861.9 29.9 %reduce-scatter.45.cloned.1.call-done = f32[2,128,768]{2,1,0:T(8,128)} async-done(((f32[2,512,768]{2,1,0:T(8,128)}), f32[2,128,768]{2,1,0:T(8,128)}) %reduce-scatter.45.cloned.1.call-update) | async-done | bytes 786448 | tf_op jit(solution)/shard_map/reduce_scatter | solution.py:96
  1899.4 32.7 %all-reduce.2 = (f32[768]{0:T(1024)}, f32[768]{0:T(1024)}) all-reduce(f32[768]{0:T(1024)S(1)} %add.278, f32[768]{0:T(1024)S(1)} %add.283), channel_id=1, replica_groups=mesh['rows'=4,'hid'=4,'wid'=2] {'rows','hid'}, use_global_device_ids=true, to_apply=%region_58.61 | all-reduce | flops 1536 | bytes 12288 | tf_op jit(solution)/shard_map/psum | solution.py:255
  1939.1 266.7 %all-reduce.12.cloned.1.call-done = (bf16[768,1536]{1,0:T(8,128)(2,1)}, bf16[384,768]{1,0:T(8,128)(2,1)}, bf16[768,1024]{1,0:T(8,128)(2,1)}, bf16[768,1024]{1,0:T(8,128)(2,1)}, bf16[1024,768]{1,0:T(8,128)(2,1)}) async-done(((bf16[768,1536]{1,0:T(8,128)(2,1)}, bf16[384,768]{1,0:T(8,128)(2,1)}, bf16[768,1024]{1,0:T(8,128)(2,1)}, bf16[768,1024]{1,0:T(8,128)(2,1)}, bf16[1024,768]{1,0:T(8,128)(2,1)}), ...) | async-done | bytes 7667728 | tf_op jit(solution)/shard_map/psum | solution.py:246
  (662 shorter events, 890.1 us)
Async XLA Ops:
  17.7 122.8 %reduce-scatter.29.cloned.1.call-start = ((), (), s32[]{:S(2)}) async-start(), calls=%async_computation.27 | async-start | bytes 9437184 | tf_op jit(solution)/shard_map/reduce_scatter | solution.py:64
  45.5 174.3 %reduce-scatter.19.cloned.1.call-start = ((), (), s32[]{:S(2)}) async-start(), calls=%async_computation.19 | async-start | bytes 9437184 | tf_op jit(solution)/shard_map/reduce_scatter | solution.py:64
  67.4 558.5 %reduce-scatter.31.cloned.1.call-start = ((), (), s32[]{:S(2)}) async-start(), calls=%async_computation.28 | async-start | bytes 3932160 | tf_op jit(solution)/shard_map/reduce_scatter | solution.py:81
  417.3 244.7 %reduce-scatter.21.cloned.1.call-start = ((), (), s32[]{:S(2)}) async-start(), calls=%async_computation.20 | async-start | bytes 3932160 | tf_op jit(solution)/shard_map/reduce_scatter | solution.py:81
  689.5 129.3 %reduce-scatter.25.cloned.1.call-start = ((), (), s32[]{:S(2)}) async-start(), calls=%async_computation.23 | async-start | bytes 6291456 | tf_op jit(solution)/shard_map/reduce_scatter | solution.py:65
  711.3 164.1 %reduce-scatter.23.cloned.1.call-start = ((), (), s32[]{:S(2)}) async-start(), calls=%async_computation.22 | async-start | bytes 6291456 | tf_op jit(solution)/shard_map/reduce_scatter | solution.py:64
  716.5 198.5 %all-gather.33.cloned.1.call-start = ((), (), s32[]{:S(2)}) async-start(), calls=%async_computation.35 | async-start | bytes 3145728 | tf_op jit(solution)/shard_map/all_gather | solution.py:71
  882.5 112.4 %reduce-scatter.41.cloned.1.call-start = ((), (), s32[]{:S(2)}) async-start(), calls=%async_computation.37 | async-start | bytes 3932160 | tf_op jit(solution)/shard_map/reduce_scatter | solution.py:96
  998.2 96.6 %reduce-scatter.47.cloned.1.call-start = ((), (), s32[]{:S(2)}) async-start(), calls=%async_computation.42 | async-start | bytes 6291456 | tf_op jit(solution)/shard_map/reduce_scatter | solution.py:92
  1022.4 129.0 %reduce-scatter.35.cloned.1.call-start = ((), (), s32[]{:S(2)}) async-start(), calls=%async_computation.31 | async-start | bytes 6291456 | tf_op jit(solution)/shard_map/reduce_scatter | solution.py:65
  1044.1 163.9 %reduce-scatter.33.cloned.1.call-start = ((), (), s32[]{:S(2)}) async-start(), calls=%async_computation.30 | async-start | bytes 6291456 | tf_op jit(solution)/shard_map/reduce_scatter | solution.py:64
  1049.8 197.8 %all-gather.41.cloned.1.call-start = ((), (), s32[]{:S(2)}) async-start(), calls=%async_computation.43 | async-start | bytes 3145728 | tf_op jit(solution)/shard_map/all_gather | solution.py:71
  1215.1 103.2 %all-gather.31.cloned.1.call-start = ((), (), s32[]{:S(2)}) async-start(), calls=%async_computation.32 | async-start | bytes 3145728 | tf_op jit(solution)/shard_map/all_gather | solution.py:77
  1215.8 143.2 %reduce-scatter.49.cloned.1.call-start = ((), (), s32[]{:S(2)}) async-start(), calls=%async_computation.45 | async-start | bytes 3932160 | tf_op jit(solution)/shard_map/reduce_scatter | solution.py:96
  1289.5 109.9 %reduce-scatter.37.cloned.1.call-start = ((), (), s32[]{:S(2)}) async-start(), calls=%async_computation.33 | async-start | bytes 3932160 | tf_op jit(solution)/shard_map/reduce_scatter | solution.py:81
  1323.3 99.3 %all-gather.45.cloned.1.call-start = ((), (), s32[]{:S(2)}) async-start(), calls=%async_computation.46 | async-start | bytes 1966080 | tf_op jit(solution)/shard_map/all_gather | solution.py:85
  1426.3 115.3 %reduce-scatter.43.cloned.1.call-start = ((), (), s32[]{:S(2)}) async-start(), calls=%async_computation.39 | async-start | bytes 2359296 | tf_op jit(solution)/shard_map/reduce_scatter | solution.py:92
  1447.9 279.2 %all-gather.47.cloned.1.call-start = ((), (), s32[]{:S(2)}) async-start(), calls=%async_computation.48 | async-start | bytes 4718592 | tf_op jit(solution)/shard_map/all_gather | solution.py:71
  1680.8 93.4 %all-gather.39.cloned.1.call-start = ((), (), s32[]{:S(2)}) async-start(), calls=%async_computation.40 | async-start | bytes 4718592 | tf_op jit(solution)/shard_map/all_gather | solution.py:71
  1707.5 102.1 %all-gather.25.cloned.1.call-start = ((), (), s32[]{:S(2)}) async-start(), calls=%async_computation.24 | async-start | bytes 3145728 | tf_op jit(solution)/shard_map/all_gather | solution.py:77
  1708.2 153.7 %reduce-scatter.53.cloned.1.call-start = ((), (), s32[]{:S(2)}) async-start(), calls=%async_computation.49 | async-start | bytes 3932160 | tf_op jit(solution)/shard_map/reduce_scatter | solution.py:96
  1734.7 157.1 %reduce-scatter.45.cloned.1.call-start = ((), (), s32[]{:S(2)}) async-start(), calls=%async_computation.41 | async-start | bytes 3932160 | tf_op jit(solution)/shard_map/reduce_scatter | solution.py:96
  1781.7 152.0 %reduce-scatter.27.cloned.1.call-start = ((), (), s32[]{:S(2)}) async-start(), calls=%async_computation.25 | async-start | bytes 3932160 | tf_op jit(solution)/shard_map/reduce_scatter | solution.py:81
  1814.6 391.2 %all-reduce.12.cloned.1.call-start = ((), (), s32[]{:S(2)}) async-start(), calls=%async_computation.52 | async-start | bytes 15335424 | tf_op jit(solution)/shard_map/psum | solution.py:246
  (174 other events, 4692.3 us)
Sparse Core Ops, SparseCore 0:
  62.7 77.7 reduce-scatter.28
  142.7 77.0 reduce-scatter.18
  417.4 37.9 reduce-scatter.30
  623.8 38.0 reduce-scatter.20
  707.9 54.3 reduce-scatter.38
  764.5 54.2 reduce-scatter.24
  821.1 54.3 reduce-scatter.22
  917.2 33.1 all-gather.34
  957.0 37.9 reduce-scatter.40
  1040.5 54.3 reduce-scatter.46
  1097.1 54.2 reduce-scatter.34
  1153.7 54.3 reduce-scatter.32
  1214.4 33.0 all-gather.40
  1249.8 33.1 all-gather.42
  1285.1 33.1 all-gather.30
  1321.0 37.9 reduce-scatter.48
  1361.4 37.9 reduce-scatter.36
  1680.9 46.2 all-gather.46
  1729.2 44.9 all-gather.38
  1776.4 33.1 all-gather.24
  1812.8 37.9 reduce-scatter.52
  1853.8 37.9 reduce-scatter.44
  1895.0 38.6 reduce-scatter.26
  1937.0 268.6 all-reduce.11
  (11 shorter events, 243.7 us)
where the time goes:
time: 2230 us; the launch traced here: 2220 us
  waiting for transfers between devices  1250 us (56%)
  matrix products  420 us (19%)
  other arithmetic  313 us (14%)
  local copies, waits for them, and re-layouts  107 us (5%)
  blocking collectives  106 us (5%)
    psum x1, waiting for transfers between devices, on_device(): lax.psum(totals[0].astype(jnp.bfloat16), 'rows').astype(jnp.float32)  267 us
    another operation x5, other arithmetic, households(): jax.scipy.linalg.solve_triangular(system, right, lower=True, unit_diagona...  240 us
    reduce_scatter x4, waiting for transfers between devices, project_sum(): lax.psum_scatter(first, 'wid', scatter_dimension=0, tiled=True)  216 us
    reduce_scatter x4, waiting for transfers between devices, branch_backward(): lax.psum_scatter(part, 'wid', scatter_dimension=0, tiled=True)  115 us
    reduce_scatter x2, waiting for transfers between devices, project_sum(): lax.psum_scatter(second, 'wid', scatter_dimension=0, tiled=True)  113 us
    all_gather x4, waiting for transfers between devices, project_grads(): lax.all_gather(first, 'wid', axis=0, tiled=True)  109 us
    reduce_scatter x4, waiting for transfers between devices, norm_grad_sum(): return lax.psum_scatter(part, 'hid', scatter_dimension=1, tiled=True)  103 us
    another operation x42, matrix products, households(): jax.scipy.linalg.solve_triangular(system, right, lower=True, unit_diagona...  82.6 us
  transfers between devices with their start and end apart: 35, of which 32 were waited for; matrix products, arithmetic and copies ran while one was open for 21% of the time, Pallas kernels for 0%

commit v1 on v0

v1 whole, which is shorter than its diff:
```python
import jax
import jax.numpy as jnp
from jax import lax
from jax.experimental import pallas as pl
from jax.experimental.pallas import tpu as pltpu
from jax.sharding import PartitionSpec as P

EPS = 1e-06
F32 = jnp.float32
BF = jnp.bfloat16


def mul(a, b):
    return lax.dot_general(a, b, (((1,), (0,)), ((), ())), preferred_element_type=F32)


def mul_t(a, b):
    return lax.dot_general(a, b, (((1,), (1,)), ((), ())), preferred_element_type=F32)


def parts_of(a):
    high = a.astype(BF)
    return high, (a - high.astype(F32)).astype(BF)


def mul_fine(a, b):
    ah, al = parts_of(a)
    bh, bl = parts_of(b)
    return mul(jnp.concatenate([ah, al], 1), jnp.concatenate([bh, bh], 0)) + mul(ah, bl)


def grid_of(rows, cols, row0, col0):
    return (
        lax.broadcasted_iota(jnp.int32, (rows, cols), 0) + row0,
        lax.broadcasted_iota(jnp.int32, (rows, cols), 1) + col0,
    )


def first_of(place, starts_ref):
    begin = jnp.zeros_like(place)
    for n in range(starts_ref.shape[0]):
        begin = jnp.where(place >= starts_ref[n], starts_ref[n], begin)
    return begin


def directions(u, braw):
    scale = lax.rsqrt(jnp.sum(u * u, -1, keepdims=True) + EPS)
    wdir = u * scale
    beta = 2.0 * jax.nn.sigmoid(braw)
    return scale, wdir, beta


def unit_inverses(tiles):
    size = tiles[0].shape[0]
    row, col = grid_of(size, size, 0, 0)
    eye = jnp.where(row == col, 1.0, 0.0)
    near = (row // 8) == (col // 8)
    base = [jnp.where(near, n, 0.0) for n in tiles]
    two = [mul_fine(n, n) for n in base]
    three = [mul_fine(n, m) for n, m in zip(base, two)]
    four = [mul_fine(m, m) for m in two]
    low = [eye + a + b + c for a, b, c in zip(base, two, three)]
    done = [p + mul_fine(p, f) for p, f in zip(low, four)]
    span = 8
    while span < size:
        cross = ((row // (2 * span)) == (col // (2 * span))) & ((row // span) != (col // span))
        part = [mul_fine(jnp.where(cross, n, 0.0), d) for n, d in zip(tiles, done)]
        done = [d + mul_fine(d, p) for d, p in zip(done, part)]
        span *= 2
    return done


def forward_kernel(starts_ref, q_ref, k_ref, v_ref, u_ref, b_ref, o_ref, p_ref, c_ref, t_ref):
    length = q_ref.shape[0]
    heads = b_ref.shape[1]
    dim = q_ref.shape[1] // heads
    half, tile = length // 2, length // 4
    soft = dim ** -0.5
    row, col = grid_of(length, half, 0, 0)
    row1, col1 = grid_of(half, half, half, half)
    begin = first_of(lax.broadcasted_iota(jnp.int32, (length, 1), 0), starts_ref)
    from_doc = col >= begin
    strict_a = from_doc & (col < row)
    upto_a = from_doc & (col <= row)
    strict_b = (col1 >= begin[half:]) & (col1 < row1)
    upto_b = (col1 >= begin[half:]) & (col1 <= row1)

    state = []
    tiles = []
    for h in range(heads):
        at = slice(h * dim, (h + 1) * dim)
        _, wdir, beta = directions(u_ref[:, at], b_ref[:, h : h + 1])
        wd, wb = wdir.astype(BF), (wdir * beta).astype(BF)
        la = jnp.where(strict_a, mul_t(wd, wb[:half]), 0.0)
        lb = jnp.where(strict_b, mul_t(wd[half:], wb[half:]), 0.0)
        state.append((wd, wb, la, lb))
        tiles += [-la[:tile, :tile], -la[tile:half, tile:], -lb[:tile, :tile], -lb[tile:, tile:]]
    done = unit_inverses(tiles)
    for h in range(heads):
        at = slice(h * dim, (h + 1) * dim)
        wd, wb, la, lb = state[h]
        whole = []
        for n, lower in enumerate((la[:half], lb)):
            d0, d1 = done[4 * h + 2 * n], done[4 * h + 2 * n + 1]
            d10 = -mul_fine(d1, mul_fine(lower[tile:, :tile], d0))
            t = jnp.concatenate(
                [jnp.concatenate([d0, jnp.zeros_like(d0)], 1), jnp.concatenate([d10, d1], 1)], 0
            )
            t_ref[h, n] = t.T.astype(BF)
            whole.append(t.astype(BF))
        k = k_ref[:, at]
        q = q_ref[:, at]
        ra = jnp.where(strict_a, mul_t(wd, k[:half]), 0.0)
        rb = jnp.where(strict_b, mul_t(wd[half:], k[half:]), 0.0)
        c00 = mul(whole[0], ra[:half].astype(BF)).astype(BF)
        g10 = ra[half:] - mul(la[half:].astype(BF), c00)
        c1 = mul(whole[1], jnp.concatenate([g10, rb], 1).astype(BF)).astype(BF)
        c_ref[h, :half, :half] = c00
        c_ref[h, half:, :] = c1
        xa = jnp.where(upto_a, mul_t(q, wb[:half]), 0.0).astype(BF)
        xb = jnp.where(upto_b, mul_t(q[half:], wb[half:]), 0.0).astype(BF)
        sa = mul_t(q, k[:half]) - mul(xa, c00)
        s0 = jnp.where(upto_a[:half], sa[:half], -1e30)
        low = mul(xb, c1)
        s10 = jnp.where(from_doc[half:], sa[half:] - low[:, :half], -1e30)
        s11 = jnp.where(upto_b, mul_t(q[half:], k[half:]) - low[:, half:], -1e30)
        top = jnp.max(s0, -1, keepdims=True)
        w = jnp.exp((s0 - top) * soft)
        w = (w * (1.0 / jnp.sum(w, -1, keepdims=True))).astype(BF)
        p_ref[h, :half, :half] = w
        v = v_ref[:, at]
        o_ref[:half, at] = mul(w, v[:half]).astype(BF)
        s1 = jnp.concatenate([s10, s11], 1)
        top = jnp.max(s1, -1, keepdims=True)
        w = jnp.exp((s1 - top) * soft)
        w = (w * (1.0 / jnp.sum(w, -1, keepdims=True))).astype(BF)
        p_ref[h, half:, :] = w
        o_ref[half:, at] = mul(w, v).astype(BF)


def backward_kernel(
    starts_ref, q_ref, k_ref, v_ref, u_ref, b_ref, do_ref, p_ref, c_ref, t_ref, dqv_ref, duk_ref, db_ref
):
    length = q_ref.shape[0]
    heads = b_ref.shape[1]
    dim = q_ref.shape[1] // heads
    half = length // 2
    soft = dim ** -0.5
    row, col = grid_of(length, half, 0, 0)
    row1, col1 = grid_of(half, half, half, half)
    begin = first_of(lax.broadcasted_iota(jnp.int32, (length, 1), 0), starts_ref)
    from_doc = col >= begin
    strict_a = from_doc & (col < row)
    upto_a = from_doc & (col <= row)
    strict_b = (col1 >= begin[half:]) & (col1 < row1)
    upto_b = (col1 >= begin[half:]) & (col1 <= row1)
    early, late = grid_of(half, length, 0, 0)
    begin_t = first_of(lax.broadcasted_iota(jnp.int32, (1, length), 1), starts_ref)
    from_doc_t = early >= begin_t
    upto_a_t = from_doc_t & (early <= late)
    early1, late1 = grid_of(half, half, half, half)
    upto_b_t = (early1 >= begin_t[:, half:]) & (early1 <= late1)
    for h in range(heads):
        at = slice(h * dim, (h + 1) * dim)
        scale, wdir, beta = directions(u_ref[:, at], b_ref[:, h : h + 1])
        wd, wb = wdir.astype(BF), (wdir * beta).astype(BF)
        q, k, v, do = q_ref[:, at], k_ref[:, at], v_ref[:, at], do_ref[:, at]
        qt, wdt, dot_ = q.T, wd.T, do.T
        p0, p1 = p_ref[h, :half, :half], p_ref[h, half:, :]
        c00, c1 = c_ref[h, :half, :half], c_ref[h, half:, :]
        t0, t1 = t_ref[h, 0], t_ref[h, 1]
        p0f, p1f = p0.astype(F32), p1.astype(F32)
        dp0 = mul_t(do[:half], v[:half])
        dp1 = mul_t(do[half:], v)
        ds0 = p0f * (dp0 - jnp.sum(p0f * dp0, -1, keepdims=True)) * soft
        ds1 = p1f * (dp1 - jnp.sum(p1f * dp1, -1, keepdims=True)) * soft
        ds0, ds1 = ds0.astype(BF), ds1.astype(BF)
        dsa = jnp.concatenate([ds0, ds1[:, :half]], 0)
        dxa = jnp.where(upto_a, mul_t(dsa, c00), 0.0).astype(BF)
        dxb = jnp.where(upto_b, mul_t(ds1, c1), 0.0).astype(BF)
        xta = jnp.where(upto_a_t, mul_t(wb[:half], q), 0.0).astype(BF)
        xtb = jnp.where(upto_b_t, mul_t(wb[half:], q[half:]), 0.0).astype(BF)
        lta = jnp.where(from_doc_t[:, half:], mul_t(wb[:half], wd[half:]), 0.0).astype(BF)
        dc00 = mul(xta, dsa)
        dc1 = mul(xtb, ds1).astype(BF)
        z1 = mul(t1, dc1)
        z10 = jnp.where(from_doc[half:], z1[:, :half], 0.0).astype(BF)
        z11 = jnp.where(strict_b, z1[:, half:], 0.0).astype(BF)
        z00 = mul(t0, (dc00 - mul(lta, z10)).astype(BF))
        z00 = jnp.where(strict_a[:half], z00, 0.0).astype(BF)
        za = jnp.concatenate([z00, z10], 0)
        z1 = jnp.concatenate([z10, z11], 1)
        dla = jnp.where(strict_a, mul_t(za, c00), 0.0).astype(BF)
        dlb = jnp.where(strict_b, mul_t(z1, c1), 0.0).astype(BF)
        dq0 = mul(ds0, k[:half]) - mul(dxa[:half], wb[:half])
        dq1 = mul(ds1, k) - mul(dxa[half:], wb[:half]) - mul(dxb, wb[half:])
        dk0 = mul(qt, dsa) - mul(wdt, za)
        dk1 = mul(qt[:, half:], ds1[:, half:]) - mul(wdt[:, half:], z11)
        y0 = mul(wdt, dla) - mul(qt, dxa)
        y1 = mul(wdt[:, half:], dlb) - mul(qt[:, half:], dxb)
        dv0 = mul(dot_[:, :half], p0) + mul(dot_[:, half:], p1[:, :half])
        dv1 = mul(dot_[:, half:], p1[:, half:])
        dw0 = mul(dla[:half], wb[:half]) - mul(z00, k[:half])
        dw1 = mul(dla[half:], wb[:half]) + mul(dlb, wb[half:]) - mul(z1, k)
        y = jnp.concatenate([y0, y1], 1).T
        dwd = beta * y + jnp.concatenate([dw0, dw1], 0)
        dbeta = jnp.sum(wdir * y, -1, keepdims=True)
        du = scale * (dwd - wdir * jnp.sum(wdir * dwd, -1, keepdims=True))
        width = heads * dim
        then = slice(width + h * dim, width + (h + 1) * dim)
        dqv_ref[:half, at] = dq0.astype(BF)
        dqv_ref[half:, at] = dq1.astype(BF)
        dqv_ref[:, then] = jnp.concatenate([dv0, dv1], 1).T.astype(BF)
        duk_ref[:, at] = du.astype(BF)
        duk_ref[:, then] = jnp.concatenate([dk0, dk1], 1).T.astype(BF)
        db_ref[:, h : h + 1] = (dbeta * beta * (1.0 - 0.5 * beta)).astype(BF)


def attn_forward(starts, q, k, v, u, braw):
    length, heads = braw.shape
    half = length // 2
    vm = pl.BlockSpec(memory_space=pltpu.VMEM)
    return pl.pallas_call(
        forward_kernel,
        in_specs=[pl.BlockSpec(memory_space=pltpu.SMEM)] + [vm] * 5,
        out_specs=[vm] * 4,
        out_shape=[
            jax.ShapeDtypeStruct(q.shape, BF),
            jax.ShapeDtypeStruct((heads, length, length), BF),
            jax.ShapeDtypeStruct((heads, length, length), BF),
            jax.ShapeDtypeStruct((heads, 2, half, half), BF),
        ],
        compiler_params=pltpu.CompilerParams(vmem_limit_bytes=48 * 2**20),
        name="attn_forward",
    )(starts, q, k, v, u, braw)


def attn_backward(starts, q, k, v, u, braw, do, p, c, t):
    length, heads = braw.shape
    vm = pl.BlockSpec(memory_space=pltpu.VMEM)
    return pl.pallas_call(
        backward_kernel,
        in_specs=[pl.BlockSpec(memory_space=pltpu.SMEM)] + [vm] * 9,
        out_specs=[vm] * 3,
        out_shape=[
            jax.ShapeDtypeStruct((length, 2 * q.shape[1]), BF),
            jax.ShapeDtypeStruct((length, 2 * q.shape[1]), BF),
            jax.ShapeDtypeStruct((length, heads), BF),
        ],
        compiler_params=pltpu.CompilerParams(vmem_limit_bytes=48 * 2**20),
        name="attn_backward",
    )(starts, q, k, v, u, braw, do, p, c, t)


def dot_rows(a, b):
    return lax.dot_general(a, b, (((0,), (0,)), ((), ())), preferred_element_type=F32)


def swap_wid(a):
    return lax.ppermute(a, "wid", [(0, 1), (1, 0)])


def swap_core(a):
    return lax.ppermute(a, "hid", [(0, 1), (1, 0), (2, 3), (3, 2)])


def swap_chip(a):
    return lax.ppermute(a, "hid", [(0, 2), (2, 0), (1, 3), (3, 1)])


def sum_rows(parts):
    n = lax.axis_size("rows")
    if n != 4:
        return [lax.psum(p, "rows") for p in parts]
    place = lax.axis_index("rows")
    inner = (place == 1) | (place == 2)
    done = []
    for p in parts:
        got = lax.ppermute(p, "rows", [(0, 1), (3, 2)])
        side = (p.astype(F32) + got.astype(F32)).astype(BF)
        got = lax.ppermute(side, "rows", [(1, 2), (2, 1)])
        whole = (side.astype(F32) + got.astype(F32)).astype(BF)
        got = lax.ppermute(whole, "rows", [(1, 0), (2, 3)])
        done.append(jnp.where(inner, whole, got))
    return done


def pick(pair, first):
    a, b = pair
    return jnp.where(first, a, b), jnp.where(first, b, a)


def on_device(
    inputs,
    starts,
    norm_one,
    w_query,
    w_key,
    w_value,
    w_house,
    strength_weight,
    b_beta,
    w_out,
    norm_two,
    gate_weight,
    up_weight,
    w_down,
    cotangent,
):
    micros, _, block, part = inputs.shape
    width = 2 * part
    length = 4 * block
    heads_cols = w_query.shape[1]
    wid = lax.axis_index("wid")
    hid = lax.axis_index("hid")
    core, chip = hid % 2, hid // 2
    core0, chip0, wid0 = core == 0, chip == 0, wid == 0

    def take(a, axis, index):
        return lax.dynamic_index_in_dim(a, index, axis, keepdims=False)

    x_far = swap_wid(take(inputs, 1, 1 - wid))
    w_uk = jnp.concatenate([w_house, w_key], 1)
    w_qv = jnp.concatenate([w_query, w_value], 1)
    uk_far = swap_wid(w_uk)
    qv_far = swap_wid(w_qv)
    sw_far = swap_wid(strength_weight)
    gains = jnp.stack([norm_one, norm_two])
    gains = jnp.concatenate([gains, swap_wid(gains)], 1)
    out_far = swap_wid(w_out)
    gate_far = swap_wid(gate_weight)
    up_far = swap_wid(up_weight)
    down_far = swap_wid(w_down)
    g_far = swap_wid(take(cotangent, 1, 1 - wid))
    row_starts = take(starts, 1, wid)

    def gather_chip(mine, far):
        mine = jnp.concatenate([mine, far], -1)
        a, b = pick((mine, swap_chip(mine)), chip0)
        return jnp.stack([a, b], 1).reshape(micros, 2 * block, width)

    def natural(mine, peer):
        cols = mine.shape[-1]
        a, b = pick((mine.reshape(2, block, cols), peer.reshape(2, block, cols)), core0)
        return jnp.stack([a, b], 1).reshape(length, cols)

    def split_cores(a):
        cols = a.shape[-1]
        a = a.reshape(2, 2, block, cols)
        return (
            take(a, 1, core).reshape(2 * block, cols),
            take(a, 1, 1 - core).reshape(2 * block, cols),
        )

    def both(a, own, far):
        return jnp.concatenate([mul(a, own), mul(a, far)], 1)

    def both_t(a, own, far):
        return jnp.concatenate([mul_t(a, own), mul_t(a, far)], 1)

    def over(a, own, far):
        return mul(a[:, :part], own) + mul(a[:, part:], far)

    def over_t(a, own, far):
        return mul_t(a[:, :part], own) + mul_t(a[:, part:], far)

    def chip_sum(keep, send):
        got = swap_core(send.astype(BF))
        return keep + got.astype(F32)

    def full_sum(keep, send):
        low = chip_sum(keep, send).astype(BF)
        return low.astype(F32) + swap_chip(low).astype(F32)

    def block_sum(keep, send):
        low = chip_sum(keep, send).reshape(2, block, width)
        got = swap_chip(take(low, 0, 1 - chip).astype(BF))
        return take(low, 0, chip) + got.astype(F32)

    def my_block(a):
        return take(a.reshape(2, block, a.shape[-1]), 0, chip)

    x_half = gather_chip(take(inputs, 1, wid), x_far).astype(F32)
    scale_one = lax.rsqrt(jnp.mean(x_half * x_half, -1, keepdims=True) + EPS)
    nm_half = (x_half * scale_one * gains[0]).astype(BF)
    nm_peer = swap_core(nm_half)
    nm = jnp.concatenate([natural(nm_half[m], nm_peer[m]) for m in range(micros)], 0)
    g_half = gather_chip(take(cotangent, 1, wid), g_far)
    g_peer = swap_core(g_half)

    uk = over(nm, w_uk, uk_far)
    braw = over(nm, strength_weight, sw_far) + b_beta
    qv = over(nm, w_qv, qv_far)
    house, keys = uk[:, :heads_cols], uk[:, heads_cols:].astype(BF)
    query, values = qv[:, :heads_cols].astype(BF), qv[:, heads_cols:].astype(BF)

    saved = []
    attn_keep, attn_send = [], []
    n2_all, mids, scales, acts, dgs, dus, outs = [], [], [], [], [], [], []
    for m in range(micros):
        at = slice(m * length, (m + 1) * length)
        args = (row_starts[m], query[at], keys[at], values[at], house[at], braw[at])
        attn, p, c, t = attn_forward(*args)
        saved.append((args, p, c, t))
        keep, send = split_cores(attn)
        attn_keep.append(keep)
        attn_send.append(send)
        mid = x_half[m] + full_sum(both(keep, w_out, out_far), both(send, w_out, out_far))
        scale_two = lax.rsqrt(jnp.mean(mid * mid, -1, keepdims=True) + EPS)
        n2 = (mid * scale_two * gains[1]).astype(BF)
        n2 = jnp.concatenate([n2, swap_core(n2)], 0)
        n2_all.append(n2)
        mids.append(mid)
        scales.append(scale_two)
    g_all = jnp.concatenate(
        [a for m in range(micros) for a in (g_half[m], g_peer[m])], 0
    )
    for m in range(micros):
        gm = jnp.concatenate([g_half[m], g_peer[m]], 0)
        d_act = over_t(gm, w_down, down_far)
        gate = over(n2_all[m], gate_weight, gate_far)
        upper = over(n2_all[m], up_weight, up_far)
        sigma = jax.nn.sigmoid(gate)
        swish = gate * sigma
        act = (swish * upper).astype(BF)
        acts.append(act)
        dgs.append((d_act * upper * sigma * (1.0 + gate * (1.0 - sigma))).astype(BF))
        dus.append((d_act * swish).astype(BF))
    n2_all = jnp.concatenate(n2_all, 0)
    act_all = jnp.concatenate(acts, 0)
    dg_all = jnp.concatenate(dgs, 0)
    du_all = jnp.concatenate(dus, 0)

    def wid_sum(own, far):
        return (own + swap_wid(far.astype(BF)).astype(F32)).astype(BF)

    def grad_rows(a, b):
        return wid_sum(dot_rows(a[:, :part], b), dot_rows(a[:, part:], b))

    def grad_cols(a, b):
        return wid_sum(dot_rows(a, b[:, :part]), dot_rows(a, b[:, part:]))

    down_low = grad_cols(act_all, g_all)
    gate_low = grad_rows(n2_all, dg_all)
    up_low = grad_rows(n2_all, du_all)

    half = 2 * block
    d_mids, d_branches = [], []
    gain_two = 0.0
    for m in range(micros):
        dg, du = dgs[m], dus[m]

        def back(s):
            return both_t(dg[s], gate_weight, gate_far) + both_t(du[s], up_weight, up_far)

        dn = full_sum(back(slice(0, half)), back(slice(half, None)))
        mid, scale = mids[m], scales[m]
        gain_two = gain_two + 0.5 * jnp.sum(dn * mid * scale, 0)
        inner = jnp.mean(mid * gains[1] * dn, -1, keepdims=True)
        d_mid = g_half[m].astype(F32) + scale * gains[1] * dn - mid * scale * scale * scale * inner
        low = d_mid.astype(BF)
        d_branches.append(jnp.concatenate([low, swap_core(low)], 0))
        d_mids.append(d_mid)

    for m in range(micros):
        feed = block_sum(
            both(acts[m][:half], w_down, down_far), both(acts[m][half:], w_down, down_far)
        )
        outs.append((my_block(mids[m]) + feed).astype(BF))

    db_all = jnp.concatenate(d_branches, 0)
    attn_all = jnp.concatenate(
        [a for m in range(micros) for a in (attn_keep[m], attn_send[m])], 0
    )
    out_low = grad_cols(attn_all, db_all)

    dqvs, duks, dbs, dxs = [], [], [], []
    gain_one = 0.0
    for m in range(micros):
        args, p, c, t = saved[m]
        d_attn = over_t(d_branches[m], w_out, out_far).astype(BF)
        d_attn = natural(d_attn[:half], d_attn[half:])
        dqv, duk, db = attn_backward(*args, d_attn, p, c, t)
        dqvs.append(dqv)
        duks.append(duk)
        dbs.append(db)
        pairs = (split_cores(dqv), split_cores(duk), split_cores(db))

        def back_one(n):
            return (
                both_t(pairs[0][n], w_qv, qv_far)
                + both_t(pairs[1][n], w_uk, uk_far)
                + both_t(pairs[2][n], strength_weight, sw_far)
            )

        dn = block_sum(back_one(0), back_one(1))
        x = my_block(x_half[m])
        scale = my_block(scale_one[m])
        gain_one = gain_one + jnp.sum(dn * x * scale, 0)
        inner = jnp.mean(x * gains[0] * dn, -1, keepdims=True)
        dxs.append(
            my_block(d_mids[m]) + scale * gains[0] * dn - x * scale * scale * scale * inner
        )
    dqv_all = jnp.concatenate(dqvs, 0)
    duk_all = jnp.concatenate(duks, 0)
    db_all = jnp.concatenate(dbs, 0)
    qv_low = grad_rows(nm, dqv_all)
    uk_low = grad_rows(nm, duk_all)

    down_low, gate_low, up_low, out_low, qv_low, uk_low = sum_rows(
        [down_low, gate_low, up_low, out_low, qv_low, uk_low]
    )
    strength = dot_rows(nm, db_all)
    bias = jnp.sum(db_all.astype(F32), 0)
    small = jnp.stack([gain_one, gain_two])
    small = small[:, :part] + swap_wid(small[:, part:])
    strength = strength[:part] + swap_wid(strength[part:])
    bias = bias + swap_wid(bias)
    strength, bias = lax.psum((strength, bias), "rows")
    small = lax.psum(small, ("rows", "hid"))

    def rows_back(values, kind):
        own = jnp.stack([v[:, :part] for v in values])
        far = swap_wid(jnp.stack([v[:, part:].astype(BF) for v in values])).astype(kind)
        a, b = pick((own, far), wid0)
        return jnp.stack([a, b], 1)

    def f(a):
        return a.astype(F32)

    return (
        rows_back(outs, BF),
        rows_back(dxs, F32),
        small[0],
        f(qv_low[:, :heads_cols]),
        f(uk_low[:, heads_cols:]),
        f(qv_low[:, heads_cols:]),
        f(uk_low[:, :heads_cols]),
        strength,
        bias,
        f(out_low),
        small[1],
        f(gate_low),
        f(up_low),
        f(down_low),
    )


def solution(mesh):
    tokens = P(None, "rows", "hid", "wid")
    tall, flat = P("wid", "hid"), P("hid", "wid")
    return jax.shard_map(
        on_device,
        mesh=mesh,
        in_specs=(
            tokens,
            P(None, "rows", None),
            P("wid"),
            tall,
            tall,
            tall,
            tall,
            tall,
            P("hid"),
            flat,
            P("wid"),
            tall,
            tall,
            flat,
            tokens,
        ),
        out_specs=(
            tokens,
            tokens,
            P("wid"),
            tall,
            tall,
            tall,
            tall,
            tall,
            P("hid"),
            flat,
            P("wid"),
            tall,
            tall,
            flat,
        ),
        check_vma=False,
    )
```

time: 2230 us -> 774 us (0.35)
  waiting for transfers between devices: 1250 us -> 264 us
  other arithmetic: 313 us -> 65.4 us
  matrix products: 420 us -> 197 us
  starting transfers between devices: 2.19 us -> 104 us
  local copies, waits for them, and re-layouts: 107 us -> 29.1 us
  blocking collectives: 106 us -> 66.2 us
  Pallas kernels: 12.3 us -> 38.6 us
    reduce_scatter x18 -> x0, waiting for transfers between devices: 619 us -> none  [the longest x4 216 us: project_sum(): lax.psum_scatter(first, 'wid', scatter_dimension=0, tiled=True)]
    all_gather x16 -> x0, waiting for transfers between devices: 357 us -> none  [the longest x4 109 us: project_grads(): lax.all_gather(first, 'wid', axis=0, tiled=True)]
    psum x1 -> x0, waiting for transfers between devices: 267 us -> none  [on_device(): lax.psum(totals[0].astype(jnp.bfloat16), 'rows').astype(jnp.float32)]
    ppermute x0 -> x63, waiting for transfers between devices: none -> 264 us  [the longest x6 131 us: sum_rows(): got = lax.ppermute(whole, 'rows', [(1, 0), (2, 3)])]
    another operation x11 -> x16, other arithmetic: 246 us -> 8.09 us  [the longest x4 4.2 us: gather_chip(): return jnp.stack([a, b], 1).reshape(micros, 2 * block, width)]
    dot_general x72 -> x91, matrix products: 337 us -> 197 us  [the longest x48 91.6 us: mul_t(): lax.dot_general(a, b, (((1,), (1,)), ((), ())), preferred_element_type=F32)]
    ppermute x0 -> x63, starting transfers between devices: none -> 104 us  [the longest x6 47.6 us: sum_rows(): got = lax.ppermute(p, 'rows', [(0, 1), (3, 2)])]
    another operation x42 -> x0, matrix products: 82.6 us -> none  [households(): jax.scipy.linalg.solve_triangular(system, right, lower=True, unit_diagona...]
  transfers between devices with their start and end apart: 35 -> 63, of which waited for: 32 -> 20; matrix products, arithmetic and copies ran while one was open for 21% -> 34% of each run, Pallas kernels for 0% -> 5%
where the time goes in v1:
time: 774 us; the launch traced here: 767 us
  waiting for transfers between devices  264 us (34%)
  matrix products  197 us (25%)
  starting transfers between devices  104 us (13%)
  blocking collectives  66.2 us (9%)
  other arithmetic  65.4 us (8%)
  Pallas kernels  38.6 us (5%)
  local copies, waits for them, and re-layouts  29.1 us (4%)
    ppermute x6, waiting for transfers between devices, sum_rows(): got = lax.ppermute(whole, 'rows', [(1, 0), (2, 3)])  131 us
    dot_general x48, matrix products, mul_t(): lax.dot_general(a, b, (((1,), (1,)), ((), ())), preferred_element_type=F32)  91.6 us
    ppermute x10, waiting for transfers between devices, swap_chip(): return lax.ppermute(a, 'hid', [(0, 2), (2, 0), (1, 3), (3, 1)])  70.2 us
    dot_general x30, matrix products, mul(): lax.dot_general(a, b, (((1,), (0,)), ((), ())), preferred_element_type=F32)  63 us
    ppermute x21, waiting for transfers between devices, swap_wid(): return lax.ppermute(a, 'wid', [(0, 1), (1, 0)])  48 us
    ppermute x6, starting transfers between devices, sum_rows(): got = lax.ppermute(p, 'rows', [(0, 1), (3, 2)])  47.6 us
    dot_general x13, matrix products, dot_rows(): lax.dot_general(a, b, (((0,), (0,)), ((), ())), preferred_element_type=F32)  42.3 us
    psum x1, blocking collectives, on_device(): small = lax.psum(small, ('rows', 'hid'))  38.3 us
  transfers between devices with their start and end apart: 63, of which 20 were waited for; matrix products, arithmetic and copies ran while one was open for 34% of the time, Pallas kernels for 5%

profile of v1, /device:TPU:0, one launch (start us, length us, event | category | flops | bytes accessed | tf_op | source)
XLA Modules:
  0.0 766.7 jit_solution(16675490022655995102)
XLA Ops:
  22.5 27.4 %collective-permute-done.22 = bf16[2,128,768]{2,1,0:T(8,128)(2,1)} collective-permute-done((bf16[2,128,768]{2,1,0:T(8,128)(2,1)}, bf16[2,128,768]{2,1,0:T(8,128)(2,1)}, u32[]{:S(2)}, u32[]{:S(2)}) %collective-permute-start.22) | collective-permute-done | bytes 393248 | tf_op jit(solution)/shard_map/ppermute | solution.py:260
  57.1 13.0 %collective-permute-done.23 = bf16[2,128,1536]{2,1,0:T(8,128)(2,1)S(1)} collective-permute-done((bf16[2,128,1536]{2,1,0:T(8,128)(2,1)S(1)}, bf16[2,128,1536]{2,1,0:T(8,128)(2,1)S(1)}, u32[]{:S(2)}, u32[]{:S(2)}) %collective-permute-start.23) | collective-permute-done | bytes 786464 | tf_op jit(solution)/shard_map/ppermute | solution.py:268
  98.3 10.6 %attn_forward.3 = (bf16[512,384]{1,0:T(8,128)(2,1)S(1)}, bf16[3,512,512]{2,1,0:T(8,128)(2,1)S(1)}, bf16[3,512,512]{2,1,0:T(8,128)(2,1)}, bf16[3,2,256,256]{3,2,1,0:T(8,128)(2,1)S(1)}) custom-call(s32[4]{0:T(128)S(1)} %get-tuple-element.198.starts_ref, bf16[512,384]{1,0:T(8,128)(2,1)S(1)} %get-tuple-element.144.q_ref, ...), custom_call_target="tpu_custom_call" | custom-call | tf_op jit(solution)/shard_map/attn_forward/pallas_call | solution.py:223
  113.7 10.2 %attn_forward.2 = (bf16[512,384]{1,0:T(8,128)(2,1)S(1)}, bf16[3,512,512]{2,1,0:T(8,128)(2,1)S(1)}, bf16[3,512,512]{2,1,0:T(8,128)(2,1)}, bf16[3,2,256,256]{3,2,1,0:T(8,128)(2,1)S(1)}) custom-call(s32[4]{0:T(128)S(1)} %get-tuple-element.197.starts_ref, bf16[512,384]{1,0:T(8,128)(2,1)S(1)} %get-tuple-element.145.q_ref, ...), custom_call_target="tpu_custom_call" | custom-call | tf_op jit(solution)/shard_map/attn_forward/pallas_call | solution.py:223
  139.4 14.0 %collective-permute-done.9 = bf16[256,1536]{1,0:T(8,128)(2,1)S(1)} collective-permute-done((bf16[256,1536]{1,0:T(8,128)(2,1)S(1)}, bf16[256,1536]{1,0:T(8,128)(2,1)S(1)}, u32[]{:S(2)}, u32[]{:S(2)}) %collective-permute-start.9) | collective-permute-done | bytes 786464 | tf_op jit(solution)/shard_map/ppermute | solution.py:268
  156.6 12.8 %collective-permute-done.17 = bf16[256,1536]{1,0:T(8,128)(2,1)S(1)} collective-permute-done((bf16[256,1536]{1,0:T(8,128)(2,1)S(1)}, bf16[256,1536]{1,0:T(8,128)(2,1)S(1)}, u32[]{:S(2)}, u32[]{:S(2)}) %collective-permute-start.17) | collective-permute-done | bytes 786464 | tf_op jit(solution)/shard_map/ppermute | solution.py:268
  180.1 8.0 %collective-permute-done.13 = bf16[1024,768]{1,0:T(8,128)(2,1)} collective-permute-done((bf16[1024,768]{1,0:T(8,128)(2,1)}, bf16[1024,768]{1,0:T(8,128)(2,1)}, u32[]{:S(2)}, u32[]{:S(2)}) %collective-permute-start.13) | collective-permute-done | bytes 1572896 | tf_op jit(solution)/shard_map/ppermute | solution.py:260
  220.4 16.0 %collective-permute-done.26 = bf16[256,1536]{1,0:T(8,128)(2,1)S(1)} collective-permute-done((bf16[256,1536]{1,0:T(8,128)(2,1)S(1)}, bf16[256,1536]{1,0:T(8,128)(2,1)S(1)}, u32[]{:S(2)}, u32[]{:S(2)}) %collective-permute-start.26) | collective-permute-done | bytes 786464 | tf_op jit(solution)/shard_map/ppermute | solution.py:268
  295.9 9.0 %attn_backward.2 = (bf16[512,768]{1,0:T(8,128)(2,1)S(1)}, bf16[512,768]{1,0:T(8,128)(2,1)S(1)}, bf16[512,3]{1,0:T(8,128)(2,1)S(1)}) custom-call(s32[4]{0:T(128)S(1)} %get-tuple-element.197.starts_ref, bf16[512,384]{1,0:T(8,128)(2,1)S(1)} %get-tuple-element.145.q_ref, bf16[512,384]{1,0:T(8,128)(2,1)S(1)} %get-tuple-element.146.k_ref, ...), custom_call_target="tpu_custom_call" | custom-call | tf_op jit(solution)/shard_map/attn_backward/pallas_call | solution.py:241
  342.5 8.3 %collective-permute-done.20 = bf16[128,1536]{1,0:T(8,128)(2,1)S(1)} collective-permute-done((bf16[128,1536]{1,0:T(8,128)(2,1)S(1)}, bf16[128,1536]{1,0:T(8,128)(2,1)S(1)}, u32[]{:S(2)}, u32[]{:S(2)}) %collective-permute-start.20) | collective-permute-done | bytes 393248 | tf_op jit(solution)/shard_map/ppermute | solution.py:268
  352.7 5.0 add_convert_fusion.2
  357.7 4.7 collective-permute-start.60
  372.0 8.5 %collective-permute-done.51 = bf16[768,1024]{1,0:T(8,128)(2,1)} collective-permute-done((bf16[768,1024]{1,0:T(8,128)(2,1)}, bf16[768,1024]{1,0:T(8,128)(2,1)}, u32[]{:S(2)}, u32[]{:S(2)}) %collective-permute-start.51) | collective-permute-done | bytes 1572896 | tf_op jit(solution)/shard_map/ppermute | solution.py:260
  385.0 4.9 collective-permute-start.52
  400.2 8.8 %attn_backward.3 = (bf16[512,768]{1,0:T(8,128)(2,1)S(1)}, bf16[512,768]{1,0:T(8,128)(2,1)S(1)}, bf16[512,3]{1,0:T(8,128)(2,1)S(1)}) custom-call(s32[4]{0:T(128)S(1)} %get-tuple-element.198.starts_ref, bf16[512,384]{1,0:T(8,128)(2,1)S(1)} %get-tuple-element.144.q_ref, bf16[512,384]{1,0:T(8,128)(2,1)S(1)} %get-tuple-element.147.k_ref, ...), custom_call_target="tpu_custom_call" | custom-call | tf_op jit(solution)/shard_map/attn_backward/pallas_call | solution.py:241
  446.7 27.9 %all-reduce = (f32[768,3]{0,1:T(4,128)}, f32[3]{0:T(128)}) all-reduce(f32[768,3]{0,1:T(4,128)} %slice_add_fusion, f32[3]{0:T(128)S(1)} %add.429), channel_id=1, replica_groups=mesh['rows'=4,'hid'=4,'wid'=2] {'rows'}, use_global_device_ids=true, to_apply=%region_12.13 | all-reduce | flops 2307 | bytes 18456 | tf_op jit(solution)/shard_map/psum | solution.py:519
  521.3 38.3 %psum.21 = f32[2,768]{1,0:T(2,128)S(1)} all-reduce(f32[2,768]{1,0:T(2,128)} %fusion.144), channel_id=1, replica_groups=mesh['rows'=4,'hid'=4,'wid'=2] {'rows','hid'}, use_global_device_ids=true, to_apply=%region_11.12 | all-reduce | flops 1536 | bytes 12288 | tf_op jit(solution)/shard_map/psum | solution.py:520
  560.3 29.4 %collective-permute-start.38 = (bf16[768,768]{1,0:T(8,128)(2,1)}, bf16[768,768]{1,0:T(8,128)(2,1)S(1)}, u32[]{:S(2)}, u32[]{:S(2)}) collective-permute-start(bf16[768,768]{1,0:T(8,128)(2,1)} %add_convert_fusion.15), channel_id=1, source_target_pairs={{0,8},{24,16},{1,9},{25,17},{2,10},{26,18},{3,11},{27,19},{4,12},{... | collective-permute-start | bytes 3538952 | tf_op jit(solution)/shard_map/ppermute | solution.py:279
  601.3 14.1 %collective-permute-done.38 = bf16[768,768]{1,0:T(8,128)(2,1)S(1)} collective-permute-done((bf16[768,768]{1,0:T(8,128)(2,1)}, bf16[768,768]{1,0:T(8,128)(2,1)S(1)}, u32[]{:S(2)}, u32[]{:S(2)}) %collective-permute-start.38) | collective-permute-done | bytes 1179680 | tf_op jit(solution)/shard_map/ppermute | solution.py:279
  626.9 22.0 %collective-permute-done.62 = bf16[1024,768]{1,0:T(8,128)(2,1)S(1)} collective-permute-done((bf16[1024,768]{1,0:T(8,128)(2,1)S(1)}, bf16[1024,768]{1,0:T(8,128)(2,1)S(1)}, u32[]{:S(2)}, u32[]{:S(2)}) %collective-permute-start.62) | collective-permute-done | bytes 1572896 | tf_op jit(solution)/shard_map/ppermute | solution.py:283
  650.8 31.8 %collective-permute-done.58 = bf16[768,1024]{1,0:T(8,128)(2,1)S(1)} collective-permute-done((bf16[768,1024]{1,0:T(8,128)(2,1)S(1)}, bf16[768,1024]{1,0:T(8,128)(2,1)S(1)}, u32[]{:S(2)}, u32[]{:S(2)}) %collective-permute-start.58) | collective-permute-done | bytes 1572896 | tf_op jit(solution)/shard_map/ppermute | solution.py:283
  684.5 31.8 %collective-permute-done.54 = bf16[768,1024]{1,0:T(8,128)(2,1)S(1)} collective-permute-done((bf16[768,1024]{1,0:T(8,128)(2,1)S(1)}, bf16[768,1024]{1,0:T(8,128)(2,1)S(1)}, u32[]{:S(2)}, u32[]{:S(2)}) %collective-permute-start.54) | collective-permute-done | bytes 1572896 | tf_op jit(solution)/shard_map/ppermute | solution.py:283
  718.2 23.4 %collective-permute-done.44 = bf16[768,768]{1,0:T(8,128)(2,1)S(1)} collective-permute-done((bf16[768,768]{1,0:T(8,128)(2,1)S(1)}, bf16[768,768]{1,0:T(8,128)(2,1)S(1)}, u32[]{:S(2)}, u32[]{:S(2)}) %collective-permute-start.44) | collective-permute-done | bytes 1179680 | tf_op jit(solution)/shard_map/ppermute | solution.py:283
  743.3 21.5 %collective-permute-done.40 = bf16[768,768]{1,0:T(8,128)(2,1)S(1)} collective-permute-done((bf16[768,768]{1,0:T(8,128)(2,1)S(1)}, bf16[768,768]{1,0:T(8,128)(2,1)S(1)}, u32[]{:S(2)}, u32[]{:S(2)}) %collective-permute-start.40) | collective-permute-done | bytes 1179680 | tf_op jit(solution)/shard_map/ppermute | solution.py:283
  (581 shorter events, 361.9 us)
Async XLA Ops:
  5.8 77.0 %collective-permute-start.6 = (bf16[768,3]{0,1:T(4,128)(2,1)S(1)}, bf16[768,3]{0,1:T(4,128)(2,1)S(1)}, u32[]{:S(2)}, u32[]{:S(2)}) collective-permute-start(bf16[768,3]{0,1:T(4,128)(2,1)S(1)} %copy-done.108), channel_id=1, source_target_pairs={{0,1},{1,0},{2,3},{3,2},{4,5},{5,4},{6,7},{7,6},{8,9},{9,8},{10,11... | collective-permute-start | bytes 13832 | tf_op jit(solution)/shard_map/ppermute | solution.py:260
  8.0 80.8 %collective-permute-start.5 = (bf16[768,768]{1,0:T(8,128)(2,1)S(1)}, bf16[768,768]{1,0:T(8,128)(2,1)S(1)}, u32[]{:S(2)}, u32[]{:S(2)}) collective-permute-start(bf16[768,768]{1,0:T(8,128)(2,1)S(1)} %constant_dynamic-update-slice_fusion.2), channel_id=1, source_target_pairs={{0,1},{1,0},{2,3},{3,2},{4,5},{5,4},{6,7},{7,6},{8,9},{9,8},{10,11... | collective-permute-start | bytes 3538952 | tf_op jit(solution)/shard_map/ppermute | solution.py:260
  20.9 73.5 %collective-permute-start.4 = (bf16[768,768]{1,0:T(8,128)(2,1)}, bf16[768,768]{1,0:T(8,128)(2,1)}, u32[]{:S(2)}, u32[]{:S(2)}) collective-permute-start(bf16[768,768]{1,0:T(8,128)(2,1)} %constant_dynamic-update-slice_fusion), channel_id=1, source_target_pairs={{0,1},{1,0},{2,3},{3,2},{4,5},{5,4},{6,7},{7,6},{8,9},{9,8},{10,11... | collective-permute-start | bytes 3538952 | tf_op jit(solution)/shard_map/ppermute | solution.py:260
  49.9 60.9 %collective-permute-start.7 = (bf16[384,768]{1,0:T(8,128)(2,1)}, bf16[384,768]{1,0:T(8,128)(2,1)}, u32[]{:S(2)}, u32[]{:S(2)}) collective-permute-start(bf16[384,768]{1,0:T(8,128)(2,1)} %param.24), channel_id=1, source_target_pairs={{0,1},{1,0},{2,3},{3,2},{4,5},{5,4},{6,7},{7,6},{8,9},{9,8},{10,11... | collective-permute-start | bytes 1769480 | tf_op jit(solution)/shard_map/ppermute | solution.py:260
  76.6 93.2 %collective-permute-start.12 = (bf16[768,1024]{1,0:T(8,128)(2,1)}, bf16[768,1024]{1,0:T(8,128)(2,1)}, u32[]{:S(2)}, u32[]{:S(2)}) collective-permute-start(bf16[768,1024]{1,0:T(8,128)(2,1)} %param.27), channel_id=1, source_target_pairs={{0,1},{1,0},{2,3},{3,2},{4,5},{5,4},{6,7},{7,6},{8,9},{9,8},{10,11... | collective-permute-start | bytes 4718600 | tf_op jit(solution)/shard_map/ppermute | solution.py:260
  82.9 90.0 %collective-permute-start.11 = (bf16[768,1024]{1,0:T(8,128)(2,1)}, bf16[768,1024]{1,0:T(8,128)(2,1)}, u32[]{:S(2)}, u32[]{:S(2)}) collective-permute-start(bf16[768,1024]{1,0:T(8,128)(2,1)} %param.26), channel_id=1, source_target_pairs={{0,1},{1,0},{2,3},{3,2},{4,5},{5,4},{6,7},{7,6},{8,9},{9,8},{10,11... | collective-permute-start | bytes 4718600 | tf_op jit(solution)/shard_map/ppermute | solution.py:260
  88.8 99.3 %collective-permute-start.13 = (bf16[1024,768]{1,0:T(8,128)(2,1)}, bf16[1024,768]{1,0:T(8,128)(2,1)}, u32[]{:S(2)}, u32[]{:S(2)}) collective-permute-start(bf16[1024,768]{1,0:T(8,128)(2,1)} %param.28), channel_id=1, source_target_pairs={{0,1},{1,0},{2,3},{3,2},{4,5},{5,4},{6,7},{7,6},{8,9},{9,8},{10,11... | collective-permute-start | bytes 4718600 | tf_op jit(solution)/shard_map/ppermute | solution.py:260
  275.6 75.9 %collective-permute-start.59 = (bf16[1024,768]{1,0:T(8,128)(2,1)}, bf16[1024,768]{1,0:T(8,128)(2,1)}, u32[]{:S(2)}, u32[]{:S(2)}) collective-permute-start(bf16[1024,768]{1,0:T(8,128)(2,1)} %convolution_convert_fusion), channel_id=1, source_target_pairs={{0,1},{1,0},{2,3},{3,2},{4,5},{5,4},{6,7},{7,6},{8,9},{9,8},{10,11... | collective-permute-start | bytes 4718600 | tf_op jit(solution)/shard_map/ppermute | solution.py:260
  277.3 85.1 %collective-permute-start.55 = (bf16[768,1024]{1,0:T(8,128)(2,1)}, bf16[768,1024]{1,0:T(8,128)(2,1)}, u32[]{:S(2)}, u32[]{:S(2)}) collective-permute-start(bf16[768,1024]{1,0:T(8,128)(2,1)} %convolution_convert_fusion.1), channel_id=1, source_target_pairs={{0,1},{1,0},{2,3},{3,2},{4,5},{5,4},{6,7},{7,6},{8,9},{9,8},{10,11... | collective-permute-start | bytes 4718600 | tf_op jit(solution)/shard_map/ppermute | solution.py:260
  277.6 102.9 %collective-permute-start.51 = (bf16[768,1024]{1,0:T(8,128)(2,1)}, bf16[768,1024]{1,0:T(8,128)(2,1)}, u32[]{:S(2)}, u32[]{:S(2)}) collective-permute-start(bf16[768,1024]{1,0:T(8,128)(2,1)} %convolution_convert_fusion.2), channel_id=1, source_target_pairs={{0,1},{1,0},{2,3},{3,2},{4,5},{5,4},{6,7},{7,6},{8,9},{9,8},{10,11... | collective-permute-start | bytes 4718600 | tf_op jit(solution)/shard_map/ppermute | solution.py:260
  284.4 55.9 %collective-permute-start.30 = (bf16[256,1536]{1,0:T(8,128)(2,1)}, bf16[256,1536]{1,0:T(8,128)(2,1)}, u32[]{:S(2)}, u32[]{:S(2)}) collective-permute-start(bf16[256,1536]{1,0:T(8,128)(2,1)} %fusion.25), channel_id=1, source_target_pairs={{0,2},{2,0},{4,6},{6,4},{1,3},{3,1},{5,7},{7,5},{8,10},{10,8},{12,... | collective-permute-start | bytes 2359304 | tf_op jit(solution)/shard_map/ppermute | solution.py:264
  357.7 119.5 %collective-permute-start.60 = (bf16[1024,768]{1,0:T(8,128)(2,1)}, bf16[1024,768]{1,0:T(8,128)(2,1)}, u32[]{:S(2)}, u32[]{:S(2)}) collective-permute-start(bf16[1024,768]{1,0:T(8,128)(2,1)} %add_convert_fusion.2), channel_id=1, source_target_pairs={{0,8},{24,16},{1,9},{25,17},{2,10},{26,18},{3,11},{27,19},{4,12},{... | collective-permute-start | bytes 4718600 | tf_op jit(solution)/shard_map/ppermute | solution.py:279
  366.8 114.0 %collective-permute-start.56 = (bf16[768,1024]{1,0:T(8,128)(2,1)}, bf16[768,1024]{1,0:T(8,128)(2,1)}, u32[]{:S(2)}, u32[]{:S(2)}) collective-permute-start(bf16[768,1024]{1,0:T(8,128)(2,1)} %add_convert_fusion.5), channel_id=1, source_target_pairs={{0,8},{24,16},{1,9},{25,17},{2,10},{26,18},{3,11},{27,19},{4,12},{... | collective-permute-start | bytes 4718600 | tf_op jit(solution)/shard_map/ppermute | solution.py:279
  385.0 98.9 %collective-permute-start.52 = (bf16[768,1024]{1,0:T(8,128)(2,1)}, bf16[768,1024]{1,0:T(8,128)(2,1)}, u32[]{:S(2)}, u32[]{:S(2)}) collective-permute-start(bf16[768,1024]{1,0:T(8,128)(2,1)} %add_convert_fusion.8), channel_id=1, source_target_pairs={{0,8},{24,16},{1,9},{25,17},{2,10},{26,18},{3,11},{27,19},{4,12},{... | collective-permute-start | bytes 4718600 | tf_op jit(solution)/shard_map/ppermute | solution.py:279
  394.2 80.4 %collective-permute-start.47 = (bf16[384,768]{1,0:T(8,128)(2,1)}, bf16[384,768]{1,0:T(8,128)(2,1)}, u32[]{:S(2)}, u32[]{:S(2)}) collective-permute-start(bf16[384,768]{1,0:T(8,128)(2,1)} %fusion.42), channel_id=1, source_target_pairs={{0,1},{1,0},{2,3},{3,2},{4,5},{5,4},{6,7},{7,6},{8,9},{9,8},{10,11... | collective-permute-start | bytes 1769480 | tf_op jit(solution)/shard_map/ppermute | solution.py:260
  488.1 106.2 %collective-permute-start.61 = (bf16[1024,768]{1,0:T(8,128)(2,1)}, bf16[1024,768]{1,0:T(8,128)(2,1)}, u32[]{:S(2)}, u32[]{:S(2)}) collective-permute-start(bf16[1024,768]{1,0:T(8,128)(2,1)} %add_convert_fusion.1), channel_id=1, source_target_pairs={{8,16},{16,8},{9,17},{17,9},{10,18},{18,10},{11,19},{19,11},{12,20... | collective-permute-start | bytes 4718600 | tf_op jit(solution)/shard_map/ppermute | solution.py:281
  490.6 125.9 %collective-permute-start.57 = (bf16[768,1024]{1,0:T(8,128)(2,1)S(1)}, bf16[768,1024]{1,0:T(8,128)(2,1)}, u32[]{:S(2)}, u32[]{:S(2)}) collective-permute-start(bf16[768,1024]{1,0:T(8,128)(2,1)S(1)} %add_convert_fusion.4), channel_id=1, source_target_pairs={{8,16},{16,8},{9,17},{17,9},{10,18},{18,10},{11,19},{19,11},{12,20... | collective-permute-start | bytes 4718600 | tf_op jit(solution)/shard_map/ppermute | solution.py:281
  505.0 92.9 %collective-permute-start.42 = (bf16[768,768]{1,0:T(8,128)(2,1)}, bf16[768,768]{1,0:T(8,128)(2,1)}, u32[]{:S(2)}, u32[]{:S(2)}) collective-permute-start(bf16[768,768]{1,0:T(8,128)(2,1)} %add_convert_fusion.12), channel_id=1, source_target_pairs={{0,8},{24,16},{1,9},{25,17},{2,10},{26,18},{3,11},{27,19},{4,12},{... | collective-permute-start | bytes 3538952 | tf_op jit(solution)/shard_map/ppermute | solution.py:279
  519.3 72.9 %collective-permute-start.49 = (bf16[384,768]{1,0:T(8,128)(2,1)}, bf16[384,768]{1,0:T(8,128)(2,1)}, u32[]{:S(2)}, u32[]{:S(2)}) collective-permute-start(bf16[384,768]{1,0:T(8,128)(2,1)} %add_convert_fusion.17), channel_id=1, source_target_pairs={{8,16},{16,8},{9,17},{17,9},{10,18},{18,10},{11,19},{19,11},{12,20... | collective-permute-start | bytes 1769480 | tf_op jit(solution)/shard_map/ppermute | solution.py:281
  560.3 55.1 %collective-permute-start.38 = (bf16[768,768]{1,0:T(8,128)(2,1)}, bf16[768,768]{1,0:T(8,128)(2,1)S(1)}, u32[]{:S(2)}, u32[]{:S(2)}) collective-permute-start(bf16[768,768]{1,0:T(8,128)(2,1)} %add_convert_fusion.15), channel_id=1, source_target_pairs={{0,8},{24,16},{1,9},{25,17},{2,10},{26,18},{3,11},{27,19},{4,12},{... | collective-permute-start | bytes 3538952 | tf_op jit(solution)/shard_map/ppermute | solution.py:279
  619.3 63.4 %collective-permute-start.58 = (bf16[768,1024]{1,0:T(8,128)(2,1)S(1)}, bf16[768,1024]{1,0:T(8,128)(2,1)S(1)}, u32[]{:S(2)}, u32[]{:S(2)}) collective-permute-start(bf16[768,1024]{1,0:T(8,128)(2,1)S(1)} %add_convert_fusion.3), channel_id=1, source_target_pairs={{8,0},{16,24},{9,1},{17,25},{10,2},{18,26},{11,3},{19,27},{12,4},{... | collective-permute-start | bytes 4718600 | tf_op jit(solution)/shard_map/ppermute | solution.py:283
  621.3 95.1 %collective-permute-start.54 = (bf16[768,1024]{1,0:T(8,128)(2,1)S(1)}, bf16[768,1024]{1,0:T(8,128)(2,1)S(1)}, u32[]{:S(2)}, u32[]{:S(2)}) collective-permute-start(bf16[768,1024]{1,0:T(8,128)(2,1)S(1)} %add_convert_fusion.6), channel_id=1, source_target_pairs={{8,0},{16,24},{9,1},{17,25},{10,2},{18,26},{11,3},{19,27},{12,4},{... | collective-permute-start | bytes 4718600 | tf_op jit(solution)/shard_map/ppermute | solution.py:283
  624.0 117.6 %collective-permute-start.44 = (bf16[768,768]{1,0:T(8,128)(2,1)S(1)}, bf16[768,768]{1,0:T(8,128)(2,1)S(1)}, u32[]{:S(2)}, u32[]{:S(2)}) collective-permute-start(bf16[768,768]{1,0:T(8,128)(2,1)S(1)} %add_convert_fusion.10), channel_id=1, source_target_pairs={{8,0},{16,24},{9,1},{17,25},{10,2},{18,26},{11,3},{19,27},{12,4},{... | collective-permute-start | bytes 3538952 | tf_op jit(solution)/shard_map/ppermute | solution.py:283
  625.6 139.2 %collective-permute-start.40 = (bf16[768,768]{1,0:T(8,128)(2,1)S(1)}, bf16[768,768]{1,0:T(8,128)(2,1)S(1)}, u32[]{:S(2)}, u32[]{:S(2)}) collective-permute-start(bf16[768,768]{1,0:T(8,128)(2,1)S(1)} %add_convert_fusion.13), channel_id=1, source_target_pairs={{8,0},{16,24},{9,1},{17,25},{10,2},{18,26},{11,3},{19,27},{12,4},{... | collective-permute-start | bytes 3538952 | tf_op jit(solution)/shard_map/ppermute | solution.py:283
  (161 other events, 2585.6 us)

commit v2 on v1

v2 whole, which is shorter than its diff:
```python
import jax
import jax.numpy as jnp
from jax import lax
from jax.experimental import pallas as pl
from jax.experimental.pallas import tpu as pltpu
from jax.sharding import PartitionSpec as P

EPS = 1e-06
F32 = jnp.float32
BF = jnp.bfloat16


def mul(a, b):
    return lax.dot_general(a, b, (((1,), (0,)), ((), ())), preferred_element_type=F32)


def mul_t(a, b):
    return lax.dot_general(a, b, (((1,), (1,)), ((), ())), preferred_element_type=F32)


def parts_of(a):
    high = a.astype(BF)
    return high, (a - high.astype(F32)).astype(BF)


def mul_fine(a, b):
    ah, al = parts_of(a)
    bh, bl = parts_of(b)
    return mul(jnp.concatenate([ah, al], 1), jnp.concatenate([bh, bh], 0)) + mul(ah, bl)


def grid_of(rows, cols, row0, col0):
    return (
        lax.broadcasted_iota(jnp.int32, (rows, cols), 0) + row0,
        lax.broadcasted_iota(jnp.int32, (rows, cols), 1) + col0,
    )


def first_of(place, starts_ref):
    begin = jnp.zeros_like(place)
    for n in range(starts_ref.shape[0]):
        begin = jnp.where(place >= starts_ref[n], starts_ref[n], begin)
    return begin


def directions(u, braw):
    scale = lax.rsqrt(jnp.sum(u * u, -1, keepdims=True) + EPS)
    wdir = u * scale
    beta = 2.0 * jax.nn.sigmoid(braw)
    return scale, wdir, beta


def unit_inverses(tiles):
    size = tiles[0].shape[0]
    row, col = grid_of(size, size, 0, 0)
    eye = jnp.where(row == col, 1.0, 0.0)
    near = (row // 8) == (col // 8)
    base = [jnp.where(near, n, 0.0) for n in tiles]
    two = [mul_fine(n, n) for n in base]
    three = [mul_fine(n, m) for n, m in zip(base, two)]
    four = [mul_fine(m, m) for m in two]
    low = [eye + a + b + c for a, b, c in zip(base, two, three)]
    done = [p + mul_fine(p, f) for p, f in zip(low, four)]
    span = 8
    while span < size:
        cross = ((row // (2 * span)) == (col // (2 * span))) & ((row // span) != (col // span))
        part = [mul_fine(jnp.where(cross, n, 0.0), d) for n, d in zip(tiles, done)]
        done = [d + mul_fine(d, p) for d, p in zip(done, part)]
        span *= 2
    return done


def solve_kernel(
    starts_ref,
    core_ref,
    nm_ref,
    np_ref,
    wu0_ref,
    wu1_ref,
    wk0_ref,
    wk1_ref,
    bias_ref,
    k_ref,
    u_ref,
    b_ref,
    c_ref,
    t_ref,
):
    length, cols = k_ref.shape
    heads = b_ref.shape[1]
    part = wu0_ref.shape[0]
    core = core_ref[0]
    block = nm_ref.shape[0] // 2
    for src, side in ((nm_ref, core), (np_ref, 1 - core)):
        a0, a1 = src[:, :part], src[:, part:]
        uk = mul(a0, wu0_ref[...]) + mul(a1, wu1_ref[...])
        keys = mul(a0, wk0_ref[...]) + mul(a1, wk1_ref[...])
        for n in range(2):
            there = pl.ds(pl.multiple_of((2 * n + side) * block, block), block)
            here = slice(n * block, (n + 1) * block)
            u_ref[there, :] = uk[here, :cols]
            b_ref[there, :] = uk[here, cols : cols + heads] + bias_ref[...]
            k_ref[there, :] = keys[here].astype(BF)
    dim = cols // heads
    half, tile = length // 2, length // 4
    row, col = grid_of(length, half, 0, 0)
    row1, col1 = grid_of(half, half, half, half)
    begin = first_of(lax.broadcasted_iota(jnp.int32, (length, 1), 0), starts_ref)
    strict_a = (col >= begin) & (col < row)
    strict_b = (col1 >= begin[half:]) & (col1 < row1)
    state = []
    tiles = []
    for h in range(heads):
        at = slice(h * dim, (h + 1) * dim)
        _, wdir, beta = directions(u_ref[:, at], b_ref[:, h : h + 1])
        wd, wb = wdir.astype(BF), (wdir * beta).astype(BF)
        la = jnp.where(strict_a, mul_t(wd, wb[:half]), 0.0)
        lb = jnp.where(strict_b, mul_t(wd[half:], wb[half:]), 0.0)
        state.append((wd, la, lb))
        tiles += [-la[:tile, :tile], -la[tile:half, tile:], -lb[:tile, :tile], -lb[tile:, tile:]]
    done = unit_inverses(tiles)
    for h in range(heads):
        at = slice(h * dim, (h + 1) * dim)
        wd, la, lb = state[h]
        whole = []
        for n, lower in enumerate((la[:half], lb)):
            d0, d1 = done[4 * h + 2 * n], done[4 * h + 2 * n + 1]
            d10 = -mul_fine(d1, mul_fine(lower[tile:, :tile], d0))
            t = jnp.concatenate(
                [jnp.concatenate([d0, jnp.zeros_like(d0)], 1), jnp.concatenate([d10, d1], 1)], 0
            )
            t_ref[h, n] = t.T.astype(BF)
            whole.append(t.astype(BF))
        k = k_ref[:, at]
        ra = jnp.where(strict_a, mul_t(wd, k[:half]), 0.0)
        rb = jnp.where(strict_b, mul_t(wd[half:], k[half:]), 0.0)
        c00 = mul(whole[0], ra[:half].astype(BF)).astype(BF)
        g10 = ra[half:] - mul(la[half:].astype(BF), c00)
        c1 = mul(whole[1], jnp.concatenate([g10, rb], 1).astype(BF)).astype(BF)
        c_ref[h, :half, :half] = c00
        c_ref[h, half:, :] = c1


def forward_kernel(
    starts_ref,
    core_ref,
    nm_ref,
    np_ref,
    qv0_ref,
    qv1_ref,
    wo0_ref,
    wo1_ref,
    k_ref,
    u_ref,
    b_ref,
    c_ref,
    q_ref,
    v_ref,
    o_ref,
    p_ref,
    keep_ref,
    send_ref,
):
    length, cols = q_ref.shape
    heads = b_ref.shape[1]
    part = qv0_ref.shape[0]
    core = core_ref[0]
    block = nm_ref.shape[0] // 2
    for src, side in ((nm_ref, core), (np_ref, 1 - core)):
        qv = mul(src[:, :part], qv0_ref[...]) + mul(src[:, part:], qv1_ref[...])
        for n in range(2):
            there = pl.ds(pl.multiple_of((2 * n + side) * block, block), block)
            here = slice(n * block, (n + 1) * block)
            q_ref[there, :] = qv[here, :cols].astype(BF)
            v_ref[there, :] = qv[here, cols:].astype(BF)
    dim = cols // heads
    half = length // 2
    soft = dim ** -0.5
    row, col = grid_of(length, half, 0, 0)
    row1, col1 = grid_of(half, half, half, half)
    begin = first_of(lax.broadcasted_iota(jnp.int32, (length, 1), 0), starts_ref)
    from_doc = col >= begin
    upto_a = from_doc & (col <= row)
    upto_b = (col1 >= begin[half:]) & (col1 <= row1)
    for h in range(heads):
        at = slice(h * dim, (h + 1) * dim)
        _, wdir, beta = directions(u_ref[:, at], b_ref[:, h : h + 1])
        wb = (wdir * beta).astype(BF)
        q, k, v = q_ref[:, at], k_ref[:, at], v_ref[:, at]
        c00, c1 = c_ref[h, :half, :half], c_ref[h, half:, :]
        xa = jnp.where(upto_a, mul_t(q, wb[:half]), 0.0).astype(BF)
        xb = jnp.where(upto_b, mul_t(q[half:], wb[half:]), 0.0).astype(BF)
        sa = mul_t(q, k[:half]) - mul(xa, c00)
        s0 = jnp.where(upto_a[:half], sa[:half], -1e30)
        low = mul(xb, c1)
        s10 = jnp.where(from_doc[half:], sa[half:] - low[:, :half], -1e30)
        s11 = jnp.where(upto_b, mul_t(q[half:], k[half:]) - low[:, half:], -1e30)
        top = jnp.max(s0, -1, keepdims=True)
        w = jnp.exp((s0 - top) * soft)
        w = (w * (1.0 / jnp.sum(w, -1, keepdims=True))).astype(BF)
        p_ref[h, :half, :half] = w
        o_ref[:half, at] = mul(w, v[:half]).astype(BF)
        s1 = jnp.concatenate([s10, s11], 1)
        top = jnp.max(s1, -1, keepdims=True)
        w = jnp.exp((s1 - top) * soft)
        w = (w * (1.0 / jnp.sum(w, -1, keepdims=True))).astype(BF)
        p_ref[h, half:, :] = w
        o_ref[half:, at] = mul(w, v).astype(BF)
    for n in range(2):
        here = slice(n * block, (n + 1) * block)
        for dst, side in ((send_ref, 1 - core), (keep_ref, core)):
            o = o_ref[pl.ds(pl.multiple_of((2 * n + side) * block, block), block), :]
            dst[here, :part] = mul(o, wo0_ref[...]).astype(dst.dtype)
            dst[here, part:] = mul(o, wo1_ref[...]).astype(dst.dtype)


def backward_kernel(
    starts_ref,
    core_ref,
    k_ref,
    u_ref,
    b_ref,
    c_ref,
    t_ref,
    q_ref,
    v_ref,
    p_ref,
    dm_ref,
    dp_ref,
    wo0_ref,
    wo1_ref,
    wu0_ref,
    wu1_ref,
    wk0_ref,
    wk1_ref,
    qv0_ref,
    qv1_ref,
    nm_ref,
    np_ref,
    duk_out,
    dqv_out,
    keep_ref,
    send_ref,
    gain_ref,
    do_ref,
    duk_ref,
    dqv_ref,
):
    part = wu0_ref.shape[0]
    wide = duk_ref.shape[1]
    near = wu0_ref.shape[1]
    core = core_ref[0]
    block = dm_ref.shape[0] // 2
    for src, side in ((dm_ref, core), (dp_ref, 1 - core)):
        d = mul_t(src[:, :part], wo0_ref[...]) + mul_t(src[:, part:], wo1_ref[...])
        for n in range(2):
            there = pl.ds(pl.multiple_of((2 * n + side) * block, block), block)
            do_ref[there, :] = d[n * block : (n + 1) * block].astype(BF)
    length = q_ref.shape[0]
    heads = b_ref.shape[1]
    dim = q_ref.shape[1] // heads
    half = length // 2
    soft = dim ** -0.5
    row, col = grid_of(length, half, 0, 0)
    row1, col1 = grid_of(half, half, half, half)
    begin = first_of(lax.broadcasted_iota(jnp.int32, (length, 1), 0), starts_ref)
    from_doc = col >= begin
    strict_a = from_doc & (col < row)
    upto_a = from_doc & (col <= row)
    strict_b = (col1 >= begin[half:]) & (col1 < row1)
    upto_b = (col1 >= begin[half:]) & (col1 <= row1)
    early, late = grid_of(half, length, 0, 0)
    begin_t = first_of(lax.broadcasted_iota(jnp.int32, (1, length), 1), starts_ref)
    from_doc_t = early >= begin_t
    upto_a_t = from_doc_t & (early <= late)
    early1, late1 = grid_of(half, half, half, half)
    upto_b_t = (early1 >= begin_t[:, half:]) & (early1 <= late1)
    dbraws = []
    for h in range(heads):
        at = slice(h * dim, (h + 1) * dim)
        scale, wdir, beta = directions(u_ref[:, at], b_ref[:, h : h + 1])
        wd, wb = wdir.astype(BF), (wdir * beta).astype(BF)
        q, k, v, do = q_ref[:, at], k_ref[:, at], v_ref[:, at], do_ref[:, at]
        qt, wdt, dot_ = q.T, wd.T, do.T
        p0, p1 = p_ref[h, :half, :half], p_ref[h, half:, :]
        c00, c1 = c_ref[h, :half, :half], c_ref[h, half:, :]
        t0, t1 = t_ref[h, 0], t_ref[h, 1]
        p0f, p1f = p0.astype(F32), p1.astype(F32)
        dp0 = mul_t(do[:half], v[:half])
        dp1 = mul_t(do[half:], v)
        ds0 = p0f * (dp0 - jnp.sum(p0f * dp0, -1, keepdims=True)) * soft
        ds1 = p1f * (dp1 - jnp.sum(p1f * dp1, -1, keepdims=True)) * soft
        ds0, ds1 = ds0.astype(BF), ds1.astype(BF)
        dsa = jnp.concatenate([ds0, ds1[:, :half]], 0)
        dxa = jnp.where(upto_a, mul_t(dsa, c00), 0.0).astype(BF)
        dxb = jnp.where(upto_b, mul_t(ds1, c1), 0.0).astype(BF)
        xta = jnp.where(upto_a_t, mul_t(wb[:half], q), 0.0).astype(BF)
        xtb = jnp.where(upto_b_t, mul_t(wb[half:], q[half:]), 0.0).astype(BF)
        lta = jnp.where(from_doc_t[:, half:], mul_t(wb[:half], wd[half:]), 0.0).astype(BF)
        dc00 = mul(xta, dsa)
        dc1 = mul(xtb, ds1).astype(BF)
        z1 = mul(t1, dc1)
        z10 = jnp.where(from_doc[half:], z1[:, :half], 0.0).astype(BF)
        z11 = jnp.where(strict_b, z1[:, half:], 0.0).astype(BF)
        z00 = mul(t0, (dc00 - mul(lta, z10)).astype(BF))
        z00 = jnp.where(strict_a[:half], z00, 0.0).astype(BF)
        za = jnp.concatenate([z00, z10], 0)
        z1 = jnp.concatenate([z10, z11], 1)
        dla = jnp.where(strict_a, mul_t(za, c00), 0.0).astype(BF)
        dlb = jnp.where(strict_b, mul_t(z1, c1), 0.0).astype(BF)
        dq0 = mul(ds0, k[:half]) - mul(dxa[:half], wb[:half])
        dq1 = mul(ds1, k) - mul(dxa[half:], wb[:half]) - mul(dxb, wb[half:])
        dk0 = mul(qt, dsa) - mul(wdt, za)
        dk1 = mul(qt[:, half:], ds1[:, half:]) - mul(wdt[:, half:], z11)
        y0 = mul(wdt, dla) - mul(qt, dxa)
        y1 = mul(wdt[:, half:], dlb) - mul(qt[:, half:], dxb)
        dv0 = mul(dot_[:, :half], p0) + mul(dot_[:, half:], p1[:, :half])
        dv1 = mul(dot_[:, half:], p1[:, half:])
        dw0 = mul(dla[:half], wb[:half]) - mul(z00, k[:half])
        dw1 = mul(dla[half:], wb[:half]) + mul(dlb, wb[half:]) - mul(z1, k)
        y = jnp.concatenate([y0, y1], 1).T
        dwd = beta * y + jnp.concatenate([dw0, dw1], 0)
        dbeta = jnp.sum(wdir * y, -1, keepdims=True)
        du = scale * (dwd - wdir * jnp.sum(wdir * dwd, -1, keepdims=True))
        dqv_ref[:half, at] = dq0.astype(BF)
        dqv_ref[half:, at] = dq1.astype(BF)
        dqv_ref[:, (heads + h) * dim : (heads + h + 1) * dim] = (
            jnp.concatenate([dv0, dv1], 1).T.astype(BF)
        )
        duk_ref[:, at] = du.astype(BF)
        behind = wide - heads * dim
        duk_ref[:, behind + h * dim : behind + (h + 1) * dim] = (
            jnp.concatenate([dk0, dk1], 1).T.astype(BF)
        )
        dbraws.append(dbeta * beta * (1.0 - 0.5 * beta))
    lane = lax.broadcasted_iota(jnp.int32, (length, wide - 2 * heads * dim), 1)
    last = jnp.zeros(lane.shape, F32)
    for h in range(heads):
        last = jnp.where(lane == h, dbraws[h], last)
    duk_ref[:, heads * dim : wide - heads * dim] = last.astype(BF)
    gain = [0.0, 0.0]
    for dst, norm, side, base in (
        (send_ref, np_ref, 1 - core, 2 * block),
        (keep_ref, nm_ref, core, 0),
    ):
        for n in range(2):
            there = pl.ds(pl.multiple_of((2 * n + side) * block, block), block)
            here = slice(base + n * block, base + (n + 1) * block)
            duk, dqv = duk_ref[there, :], dqv_ref[there, :]
            duk_out[here, :] = duk
            dqv_out[here, :] = dqv
            rows = slice(n * block, (n + 1) * block)
            du, dk = duk[:, :near], duk[:, near:]
            for i, (cut, wu, wk, qv) in enumerate(
                (
                    (slice(0, part), wu0_ref, wk0_ref, qv0_ref),
                    (slice(part, 2 * part), wu1_ref, wk1_ref, qv1_ref),
                )
            ):
                dn = mul_t(du, wu[...]) + mul_t(dk, wk[...]) + mul_t(dqv, qv[...])
                dst[rows, cut] = dn.astype(dst.dtype)
                gain[i] += jnp.sum(dn * norm[rows, cut].astype(F32), 0, keepdims=True)
    gain_ref[:, :part] = gain[0]
    gain_ref[:, part:] = gain[1]


def vmem(n):
    return [pl.BlockSpec(memory_space=pltpu.VMEM)] * n


def smem(n):
    return [pl.BlockSpec(memory_space=pltpu.SMEM)] * n


def shape_of(*dims, kind=BF):
    return jax.ShapeDtypeStruct(dims, kind)


def params(mib=48):
    return pltpu.CompilerParams(vmem_limit_bytes=mib * 2**20)


def cost(us):
    return pl.CostEstimate(flops=int(us * 3e8), bytes_accessed=1000, transcendentals=0)


def attn_solve(starts, core, nm, np_, wu0, wu1, wk0, wk1, bias):
    length, heads = 2 * nm.shape[0], bias.shape[1]
    cols = wk0.shape[1]
    half = length // 2
    return pl.pallas_call(
        solve_kernel,
        in_specs=smem(2) + vmem(7),
        out_specs=vmem(5),
        out_shape=[
            shape_of(length, cols),
            shape_of(length, cols, kind=F32),
            shape_of(length, heads, kind=F32),
            shape_of(heads, length, length),
            shape_of(heads, 2, half, half),
        ],
        compiler_params=params(),
        cost_estimate=cost(12),
        name="attn_solve",
    )(starts, core, nm, np_, wu0, wu1, wk0, wk1, bias)


def attn_forward(starts, core, nm, np_, qv0, qv1, wo0, wo1, k, u, braw, c):
    length, cols = k.shape
    half, width, heads = length // 2, nm.shape[1], braw.shape[1]
    return pl.pallas_call(
        forward_kernel,
        in_specs=smem(2) + vmem(10),
        out_specs=vmem(6),
        out_shape=[
            shape_of(length, cols),
            shape_of(length, cols),
            shape_of(length, cols),
            shape_of(heads, length, length),
            shape_of(half, width, kind=F32),
            shape_of(half, width),
        ],
        compiler_params=params(),
        cost_estimate=cost(9),
        name="attn_forward",
    )(starts, core, nm, np_, qv0, qv1, wo0, wo1, k, u, braw, c)


def attn_backward(starts, core, saved, dm, dp, *weights_and_norms):
    length, cols = saved[0].shape
    half, width = length // 2, dm.shape[1]
    near, far = weights_and_norms[2].shape[1], weights_and_norms[4].shape[1]
    return pl.pallas_call(
        backward_kernel,
        in_specs=smem(2) + vmem(20),
        out_specs=vmem(5),
        out_shape=[
            shape_of(length, near + far),
            shape_of(length, 2 * cols),
            shape_of(half, width, kind=F32),
            shape_of(half, width),
            shape_of(1, width, kind=F32),
        ],
        scratch_shapes=[
            pltpu.VMEM((length, cols), BF),
            pltpu.VMEM((length, near + far), BF),
            pltpu.VMEM((length, 2 * cols), BF),
        ],
        compiler_params=params(),
        cost_estimate=cost(21),
        name="attn_backward",
    )(starts, core, *saved, dm, dp, *weights_and_norms)


def feed_kernel(a_ref, w0_ref, w1_ref, keep_ref, send_ref):
    rows = a_ref.shape[0] // 2
    part = w0_ref.shape[1]
    for dst, at in ((send_ref, slice(rows, None)), (keep_ref, slice(0, rows))):
        dst[0, :, :part] = mul(a_ref[at, :], w0_ref[...]).astype(dst.dtype)
        dst[0, :, part:] = mul(a_ref[at, :], w1_ref[...]).astype(dst.dtype)


def ffn_feed(act, wd0, wd1):
    hidden, part = wd0.shape
    micros, rows = 2, act.shape[0] // 4
    weight = pl.BlockSpec((hidden, part), lambda m: (0, 0))
    out = pl.BlockSpec((1, rows, 2 * part), lambda m: (m, 0, 0))
    return pl.pallas_call(
        feed_kernel,
        grid=(micros,),
        in_specs=[pl.BlockSpec((2 * rows, hidden), lambda m: (m, 0)), weight, weight],
        out_specs=[out, out],
        out_shape=[
            shape_of(micros, rows, 2 * part, kind=F32),
            shape_of(micros, rows, 2 * part),
        ],
        compiler_params=params(),
        cost_estimate=cost(6),
        name="ffn_feed",
    )(act, wd0, wd1)


def ffn_grad_kernel(*refs):
    a, b = refs[:4], refs[4:6]
    own_ref, far_ref, turned = refs[6:]
    rows = a[0].shape[0]
    part = own_ref.shape[0]

    @pl.when(pl.program_id(0) == 0)
    def _():
        for p in range(4):
            turned[:, p * rows : (p + 1) * rows] = a[p][...].T

    out = mul(turned[:, : 2 * rows], b[0][...]) + mul(turned[:, 2 * rows :], b[1][...])
    own_ref[...] = out[:part]
    far_ref[...] = out[part:].astype(BF)


def ffn_grad(a, b, tile=256):
    rows, width = a[0].shape
    hidden = b[0].shape[1]
    whole = pl.BlockSpec((rows, width), lambda i: (0, 0))
    cols = pl.BlockSpec((2 * rows, tile), lambda i: (0, i))
    out = pl.BlockSpec((width // 2, tile), lambda i: (0, i))
    return pl.pallas_call(
        ffn_grad_kernel,
        grid=(hidden // tile,),
        in_specs=[whole] * 4 + [cols] * 2,
        out_specs=[out, out],
        out_shape=[shape_of(width // 2, hidden, kind=F32), shape_of(width // 2, hidden)],
        scratch_shapes=[pltpu.VMEM((width, 4 * rows), BF)],
        compiler_params=params(),
        cost_estimate=cost(6),
        name="ffn_grad",
    )(*a, *b)


def attn_grad_kernel(core_ref, *refs):
    a, d, dqv, duk, attn = refs[:4], refs[4:8], refs[8:10], refs[10:12], refs[12:14]
    extra, own, far = refs[14:16], refs[16:18], refs[18:20]
    turned, turned_d, placed = refs[20:]
    rows = a[0].shape[0]
    block = rows // 2
    part = own[0].shape[0]
    cols = attn[0].shape[1]
    for p in range(4):
        here = slice(p * rows, (p + 1) * rows)
        turned[:, here] = a[p][...].T
        turned_d[:, here] = d[p][...].T
        side = core_ref[0] if p % 2 == 0 else 1 - core_ref[0]
        for n in range(2):
            there = pl.ds(pl.multiple_of((2 * n + side) * block, block), block)
            placed[p * rows + n * block : p * rows + (n + 1) * block, :] = attn[p // 2][there, :]
    ends = [0]
    for o in own:
        ends.append(ends[-1] + o.shape[1])
    pieces = [(cols, cols, 128, duk, 0)]
    at = cols + 128
    for src, begin, size in ((dqv, 0, 2 * cols), (duk, cols + 128, cols), (duk, 0, cols)):
        while size:
            i = max(n for n in range(len(own)) if ends[n] <= at)
            n = min(size, ends[i + 1] - at)
            pieces.append((at - ends[i], begin, n, src, i))
            at, begin, size = at + n, begin + n, size - n
    for side, dsts in ((1, far), (0, own)):
        half = slice(side * part, (side + 1) * part)
        dsts[0][:, :cols] = mul(turned_d[half, :], placed[...]).astype(dsts[0].dtype)
        for to, begin, n, src, i in pieces:
            out = mul(turned[half, : 2 * rows], src[0][:, begin : begin + n])
            out = out + mul(turned[half, 2 * rows :], src[1][:, begin : begin + n])
            if i == 0 and to == cols:
                out = out + extra[side][...]
            dsts[i][:, to : to + n] = out.astype(dsts[i].dtype)


def attn_grad(core, a, d, dqv, duk, attn, extra):
    rows, width = a[0].shape
    part, cols = width // 2, attn[0].shape[1]
    wide = cols + 128
    sizes = (2 * wide,) * 2
    out = pl.pallas_call(
        attn_grad_kernel,
        in_specs=smem(1) + vmem(16),
        out_specs=vmem(4),
        out_shape=[shape_of(part, n, kind=F32) for n in sizes] + [shape_of(part, n) for n in sizes],
        scratch_shapes=[
            pltpu.VMEM((width, 4 * rows), BF),
            pltpu.VMEM((width, 4 * rows), BF),
            pltpu.VMEM((4 * rows, cols), BF),
        ],
        compiler_params=params(),
        cost_estimate=cost(14),
        name="attn_grad",
    )(core, *a, *d, *dqv, *duk, *attn, *extra)
    return list(zip(out[:2], out[2:]))


def up_kernel(*refs):
    n2, g = refs[:4], refs[4:8]
    wg0, wg1, wu0, wu1, one_ref, two_ref, act_ref, own_ref, far_ref = refs[8:]
    part = wg0.shape[0]
    rows = n2[0].shape[0]
    total = 0.0
    for p in range(4):
        a0, a1 = n2[p][:, :part], n2[p][:, part:]
        gate = mul(a0, wg0[...]) + mul(a1, wg1[...])
        upper = mul(a0, wu0[...]) + mul(a1, wu1[...])
        sigma = jax.nn.sigmoid(gate)
        swish = gate * sigma
        act = (swish * upper).astype(BF)
        at = slice(p * rows, (p + 1) * rows)
        one_ref[at, :] = (upper * sigma * (1.0 + gate * (1.0 - sigma))).astype(BF)
        two_ref[at, :] = swish.astype(BF)
        act_ref[at, :] = act
        total = total + mul(act.T, g[p][...])
    own_ref[...] = total[:, :part]
    far_ref[...] = total[:, part:].astype(BF)


def ffn_up(n2, g, wg0, wg1, wu0, wu1, tile=256):
    rows, width = n2[0].shape
    part, hidden = wg0.shape
    whole = pl.BlockSpec((rows, width), lambda i: (0, 0))
    cols = pl.BlockSpec((part, tile), lambda i: (0, i))
    tall = pl.BlockSpec((4 * rows, tile), lambda i: (0, i))
    flat = pl.BlockSpec((tile, part), lambda i: (i, 0))
    return pl.pallas_call(
        up_kernel,
        grid=(hidden // tile,),
        in_specs=[whole] * 8 + [cols] * 4,
        out_specs=[tall] * 3 + [flat] * 2,
        out_shape=[shape_of(4 * rows, hidden)] * 3
        + [shape_of(hidden, part, kind=F32), shape_of(hidden, part)],
        compiler_params=params(),
        cost_estimate=cost(16),
        name="ffn_up",
    )(*n2, *g, wg0, wg1, wu0, wu1)


def down_kernel(*refs):
    g, one_ref, two_ref = refs[:2], refs[2], refs[3]
    wd0, wd1, wg0, wg1, wu0, wu1, dg_ref, du_ref, keep_ref, send_ref, acc = refs[4:]
    part = wg0.shape[0]
    rows = g[0].shape[0]
    step = pl.program_id(0)

    for p in range(2):
        d = mul_t(g[p][:, :part], wd0[...]) + mul_t(g[p][:, part:], wd1[...])
        at = slice(p * rows, (p + 1) * rows)
        dg = (d * one_ref[at, :].astype(F32)).astype(BF)
        du = (d * two_ref[at, :].astype(F32)).astype(BF)
        dg_ref[at, :] = dg
        du_ref[at, :] = du
        new0 = mul_t(dg, wg0[...]) + mul_t(du, wu0[...])
        new1 = mul_t(dg, wg1[...]) + mul_t(du, wu1[...])

        @pl.when(step == 0)
        def _():
            acc[at, :part] = new0
            acc[at, part:] = new1

        @pl.when(step > 0)
        def _():
            acc[at, :part] += new0
            acc[at, part:] += new1

    @pl.when(step == pl.num_programs(0) - 1)
    def _():
        keep_ref[...] = acc[:rows, :]
        send_ref[...] = acc[rows:, :].astype(BF)


def ffn_down(m, g, one, two, wd0, wd1, wg0, wg1, wu0, wu1, tile=256):
    rows, width = g[0].shape
    part, hidden = wg0.shape
    whole = pl.BlockSpec((rows, width), lambda i: (0, 0))
    cols = pl.BlockSpec((part, tile), lambda i: (0, i))
    flat = pl.BlockSpec((tile, part), lambda i: (i, 0))
    pick_m = pl.BlockSpec((2 * rows, tile), lambda i: (m, i))
    tall = pl.BlockSpec((2 * rows, tile), lambda i: (0, i))
    return pl.pallas_call(
        down_kernel,
        grid=(hidden // tile,),
        in_specs=[whole] * 2 + [pick_m] * 2 + [flat] * 2 + [cols] * 4,
        out_specs=[tall] * 2 + [whole] * 2,
        out_shape=[shape_of(2 * rows, hidden)] * 2
        + [shape_of(rows, width, kind=F32), shape_of(rows, width)],
        scratch_shapes=[pltpu.VMEM((2 * rows, width), F32)],
        compiler_params=params(),
        cost_estimate=cost(13),
        name="ffn_down",
    )(*g, one, two, wd0, wd1, wg0, wg1, wu0, wu1)


def swap_wid(a):
    return lax.ppermute(a, "wid", [(0, 1), (1, 0)])


def swap_core(a):
    return lax.ppermute(a, "hid", [(0, 1), (1, 0), (2, 3), (3, 2)])


def swap_chip(a):
    return lax.ppermute(a, "hid", [(0, 2), (2, 0), (1, 3), (3, 1)])


def tie(a, *others):
    return lax.optimization_barrier((a, *others))[0]


class RowSum:
    def __init__(self, a):
        self.value = a
        self.line = lax.axis_size("rows") == 4
        self.stage = 0

    def send(self):
        self.stage += 1
        if self.line and self.stage <= 3:
            moves = {1: [(0, 1), (3, 2)], 2: [(1, 2), (2, 1)], 3: [(1, 0), (2, 3)]}
            self.got = lax.ppermute(self.value, "rows", moves[self.stage])

    def take(self, then):
        if not self.line:
            if self.stage == 3:
                self.value = lax.psum(then(self.value), "rows").astype(F32)
        elif self.stage < 3:
            self.value = (self.value.astype(F32) + then(self.got).astype(F32)).astype(BF)
        else:
            place = lax.axis_index("rows")
            inner = (place == 1) | (place == 2)
            self.value = jnp.where(inner, self.value, then(self.got)).astype(F32)


def pick(pair, first):
    a, b = pair
    return jnp.where(first, a, b), jnp.where(first, b, a)

ORDER = (
    "fd0", "low0", "fd1", "low1", "gF", "dL", "dmid0", "ab0", "gL", "dM",
    "dmid1", "uF", "ab1", "dW", "gM", "aF", "uL", "vL", "aL", "bL",
    "uM", "gW", "dE", "vM", "feed", "cL", "eL", "aM", "uW", "gE",
    "bM", "vW", "uE", "flow", "cM", "vE", "aW", "eM", "dlow", "bW",
    "aE", "outs", "cW", "bE", "dxs", "eW", "s1", "cE", "s2", "outsf",
    "s3", "dxsf", "eE",
)


def on_device(
    inputs,
    starts,
    norm_one,
    w_query,
    w_key,
    w_value,
    w_house,
    strength_weight,
    b_beta,
    w_out,
    norm_two,
    gate_weight,
    up_weight,
    w_down,
    cotangent,
):
    micros, _, block, part = inputs.shape
    width = 2 * part
    half = 2 * block
    cols = w_query.shape[1]
    heads = strength_weight.shape[1]
    wid = lax.axis_index("wid")
    hid = lax.axis_index("hid")
    core, chip = hid % 2, hid // 2
    chip0, wid0 = chip == 0, wid == 0
    core_arg = core.astype(jnp.int32).reshape(1)

    def take(a, axis, index):
        return lax.dynamic_index_in_dim(a, index, axis, keepdims=False)

    def assisted(w, *before):
        size = w.shape[0] // lax.axis_size("rows")
        share = lax.dynamic_slice_in_dim(w, lax.axis_index("rows") * size, size)
        got = swap_wid(tie(share, *before))
        return lax.all_gather(got, "rows", axis=0, tiled=True), got

    x_far = swap_wid(take(inputs, 1, 1 - wid))
    gains = jnp.stack([norm_one, norm_two])
    gains_far = swap_wid(gains)
    gains = jnp.concatenate([gains, gains_far], 1)
    w_u = jnp.concatenate([w_house, strength_weight, jnp.zeros((part, 128 - heads), BF)], 1)
    w_qv = jnp.concatenate([w_query, w_value], 1)
    u_far = swap_wid(tie(w_u, x_far))
    k_far = swap_wid(tie(w_key, x_far))
    up_far, up_share = assisted(up_weight, u_far)
    down_far, down_share = assisted(w_down, k_far)
    qv_far = swap_wid(tie(w_qv, u_far))
    g_far = swap_wid(tie(take(cotangent, 1, 1 - wid), k_far))
    out_far = swap_wid(tie(w_out, k_far))
    row_starts = take(starts, 1, wid)

    def gather_chip(mine, far):
        mine = jnp.concatenate([mine, far], -1)
        a, b = pick((mine, swap_chip(mine)), chip0)
        return jnp.stack([a, b], 1).reshape(micros, half, width)

    def chip_sum(keep, send):
        return keep + swap_core(send).astype(F32)

    def my_block(a):
        return take(a.reshape(2, block, a.shape[-1]), 0, chip)

    x_half = tie(gather_chip(take(inputs, 1, wid), x_far), u_far).astype(F32)
    scale_one = lax.rsqrt(jnp.mean(x_half * x_half, -1, keepdims=True) + EPS)
    nm_half = (x_half * scale_one * gains[0]).astype(BF)
    nm_half = tie(nm_half, k_far)
    nm_peer = swap_core(nm_half)
    saved, attns, mids, scales, n2_parts = [], [], [], [], []
    uk_w = (w_u, u_far, w_key, k_far)
    for m in range(micros):
        nm = nm_half[m] if m == 0 else tie(nm_half[m], saved[0][0])
        saved.append(attn_solve(row_starts[m], core_arg, nm, nm_peer[m], *uk_w, b_beta[None]))
    g_half = gather_chip(tie(take(cotangent, 1, wid), saved[-1][0]), g_far)
    def finish_mid(m, low, got):
        mid = x_half[m] + low.astype(F32) + got.astype(F32)
        scale_two = lax.rsqrt(jnp.mean(mid * mid, -1, keepdims=True) + EPS)
        n2 = (mid * scale_two * gains[1]).astype(BF)
        n2_parts.extend([n2, swap_core(n2)])
        mids.append(mid)
        scales.append(scale_two)

    low = saved[1][0]
    for m in range(micros):
        k, u, braw, c, t = saved[m]
        nm = tie(nm_half[m], low)
        q, v, attn, p, keep, send = attn_forward(
            row_starts[m], core_arg, nm, nm_peer[m], w_qv, qv_far, w_out, out_far, k, u, braw, c
        )
        saved[m] = (*saved[m], q, v, p)
        attns.append(attn)
        got = swap_core(send)
        if m == 1:
            finish_mid(0, low, tie(chip_got, keep))
            got = tie(got, n2_parts[0])
        low = (keep + got.astype(F32)).astype(BF)
        chip_got = swap_chip(low)
    finish_mid(1, low, chip_got)
    g_peer = swap_core(tie(g_half, low))
    g_parts = [a for m in range(micros) for a in (g_half[m], g_peer[m])]
    gate_far = swap_wid(tie(gate_weight, saved[1][0]))
    ffn_w = (gate_weight, gate_far, up_weight, up_far)
    one, two, act, down_own, down_far_part = ffn_up(n2_parts, g_parts, *ffn_w)
    ready = {"d": (down_own, swap_wid(down_far_part), slice(None))}

    last = [act]

    def then(a):
        return tie(a, last[0])

    def mark(a):
        last[0] = a
        return a

    s = {}
    steps = {}

    def stack_m(name):
        return jnp.concatenate([s[name + "0"], s[name + "1"]], 0)

    def row_steps(m, tag):
        def ffn_back():
            gm = (then(g_parts[2 * m]), g_parts[2 * m + 1])
            dg, du, keep, send = ffn_down(m, gm, one, two, w_down, down_far, *ffn_w)
            s["dg" + tag], s["du" + tag], s["nk" + tag] = mark(dg), du, keep
            s["ng" + tag] = swap_core(send)

        def low():
            s["nl" + tag] = mark((s["nk" + tag] + then(s["ng" + tag]).astype(F32)).astype(BF))
            s["nx" + tag] = swap_chip(s["nl" + tag])

        def d_mid():
            mid, scale = mids[m], scales[m]
            dn = s["nl" + tag].astype(F32) + then(s["nx" + tag]).astype(F32)
            inner = jnp.mean(mid * gains[1] * dn, -1, keepdims=True)
            d = g_half[m].astype(F32) + scale * gains[1] * dn
            d = d - mid * scale * scale * scale * inner
            s["d" + tag] = d
            s["g2" + tag] = 0.5 * jnp.sum(dn * mid * scale, 0)
            s["dl" + tag] = mark(d.astype(BF))
            s["dp" + tag] = swap_core(s["dl" + tag])

        def attn_back():
            duk, dqv, keep, send, s["g1" + tag] = attn_backward(
                row_starts[m],
                core_arg,
                saved[m],
                then(s["dl" + tag]),
                s["dp" + tag],
                w_out,
                out_far,
                *uk_w,
                w_qv,
                qv_far,
                nm_half[m],
                nm_peer[m],
            )
            s["duk" + tag], s["dqv" + tag], s["ak" + tag] = mark(duk), dqv, keep
            s["ag" + tag] = swap_core(send)

        steps["fd" + tag] = ffn_back
        steps["low" + tag] = low
        steps["dmid" + tag] = d_mid
        steps["ab" + tag] = attn_back

    for m in range(micros):
        row_steps(m, str(m))

    def grad_steps(name):
        state = {}

        def low():
            own, near, part_of = ready[name]
            near = then(near)[:, part_of].astype(F32)
            state["sum"] = RowSum(mark((own[:, part_of] + near).astype(BF)))
            state["sum"].send()

        def more():
            state["sum"].take(then)
            mark(state["sum"].value)
            state["sum"].send()

        def end():
            more()
            s[name] = state["sum"].value

        steps[name + "L"] = low
        steps[name + "M"] = more
        steps[name + "W"] = more
        steps[name + "E"] = end

    for name in "dguvabce":
        grad_steps(name)

    def put_ready(names, own, near):
        size = own.shape[1] // len(names)
        for n, name in enumerate(names):
            ready[name] = (own, near, slice(n * size, (n + 1) * size))

    def ffn_grad_step(name, of):
        def step():
            norms = (then(n2_parts[0]), *n2_parts[1:])
            b = (s[of + "0"], s[of + "1"])
            own, far = ffn_grad(norms, b)
            put_ready(name, own, swap_wid(mark(far)))

        return step

    steps["gF"] = ffn_grad_step("g", "dg")
    steps["uF"] = ffn_grad_step("uv", "du")

    def feed_step():
        keep, send = ffn_feed(then(act), w_down, down_far)
        mark(keep)
        for m in range(micros):
            s[f"fk{m}"], s[f"fg{m}"] = keep[m], swap_core(send[m])

    steps["feed"] = feed_step

    def attn_grad_step():
        duk = [s["duk0"], s["duk1"]]
        bias = sum(jnp.sum(a[:, cols : cols + heads].astype(F32), 0) for a in duk)
        scales = jnp.stack([(s["g10"] + s["g11"])[0] / gains[0], s["g20"] + s["g21"]], 1)
        column = lax.broadcasted_iota(jnp.int32, (width, 128), 1)
        row = lax.broadcasted_iota(jnp.int32, (width, 128), 0) % part
        extra = jnp.where(column == 2 * heads, scales[:, :1], 0.0)
        extra = extra + jnp.where(column == 2 * heads + 1, scales[:, 1:], 0.0)
        bias = jnp.pad(bias[None], ((0, 0), (heads, 128 - 2 * heads)))
        extra = extra + jnp.where(row == 0, bias, 0.0)
        norms = [a for m in range(micros) for a in (nm_half[m], nm_peer[m])]
        norms[0] = then(norms[0])
        dqv = [s["dqv0"], s["dqv1"]]
        db = [s["dl0"], s["dp0"], s["dl1"], s["dp1"]]
        pairs = attn_grad(core_arg, norms, db, dqv, duk, attns, (extra[:part], extra[part:]))
        mark(pairs[0][1])
        for names, (own, far) in zip(("ab", "ce"), pairs):
            put_ready(names, own, swap_wid(far))

    steps["aF"] = attn_grad_step

    def own_blocks(a):
        return jnp.stack([my_block(m) for m in a])

    def block_low(keep, got, name):
        def step():
            low = [s[keep + t] + then(s[got + t]).astype(F32) for t in ("0", "1")]
            low = jnp.stack(low).reshape(micros, 2, block, width)
            s[name + "l"] = take(low, 1, chip)
            s[name + "x"] = swap_chip(mark(take(low, 1, 1 - chip).astype(BF)))

        return step

    def rows_back(values, kind, name):
        own = values[..., :part].astype(kind)
        far = swap_wid(mark(values[..., part:].astype(BF)))

        def finish():
            a, b = pick((own, then(far).astype(kind)), wid0)
            s[name] = mark(jnp.stack([a, b], 1))

        steps[name + "f"] = finish

    def out_step():
        rows_back(own_blocks(mids) + s["fl"] + then(s["fx"]).astype(F32), BF, "outs")

    def dx_step():
        dn = s["al"] + then(s["ax"]).astype(F32)
        x, scale = own_blocks(x_half), own_blocks(scale_one)
        inner = jnp.mean(x * gains[0] * dn, -1, keepdims=True)
        dx = own_blocks([s["d0"], s["d1"]]) + scale * gains[0] * dn
        rows_back(dx - x * scale * scale * scale * inner, F32, "dxs")

    def small_core():
        s["few"] = then(s["a"])[:, cols + 2 * heads : cols + 2 * heads + 2]
        s["few_got"] = swap_core(s["few"])

    def small_chip():
        s["few"] = mark(s["few"] + then(s["few_got"]))
        s["few_got"] = swap_chip(s["few"])

    def small_end():
        s["small"] = mark(s["few"] + then(s["few_got"]))

    steps["s1"], steps["s2"], steps["s3"] = small_core, small_chip, small_end
    steps["flow"] = block_low("fk", "fg", "f")
    steps["dlow"] = block_low("ak", "ag", "a")
    steps["outs"] = out_step
    steps["dxs"] = dx_step
    for name in ORDER:
        steps[name]()
    outs, dxs = s["outs"], s["dxs"]
    g_down, g_gate, g_up = s["d"], s["g"], jnp.concatenate([s["u"], s["v"]], 1)
    g_out = s["a"][:, :cols].T
    strengths = s["a"][:, cols:]
    chunks = (s["b"], s["c"], s["e"])
    wide = cols + 128

    def columns(begin):
        out = []
        done = 0
        while done < cols:
            at = begin + done
            n = min(cols - done, wide - at % wide)
            out.append(chunks[at // wide][:, at % wide : at % wide + n])
            done += n
        return jnp.concatenate(out, 1)

    g_q, g_v, g_k, g_u = [columns(n * cols) for n in range(4)]
    return (
        outs,
        dxs,
        s["small"][:, 0],
        g_q,
        g_k,
        g_v,
        g_u,
        strengths[:, :heads],
        strengths[0, heads : 2 * heads],
        g_out,
        s["small"][:, 1],
        g_gate,
        g_up,
        g_down,
    )


def solution(mesh):
    tokens = P(None, "rows", "hid", "wid")
    tall, flat = P("wid", "hid"), P("hid", "wid")
    specs = (P("wid"), tall, tall, tall, tall, tall, P("hid"), flat, P("wid"), tall, tall, flat)
    return jax.shard_map(
        on_device,
        mesh=mesh,
        in_specs=(tokens, P(None, "rows", None), *specs, tokens),
        out_specs=(tokens, tokens, *specs),
        check_vma=False,
    )
```

time: 774 us -> 603 us (0.78)
  matrix products: 197 us -> 0 us
  Pallas kernels: 38.6 us -> 160 us
  blocking collectives: 66.2 us -> 0 us
  waiting for transfers between devices: 264 us -> 203 us
  starting transfers between devices: 104 us -> 80.6 us
  local copies, waits for them, and re-layouts: 29.1 us -> 48 us
  other arithmetic: 65.4 us -> 83.6 us
  between operations: 3.33 us -> 16.2 us
    dot_general x91 -> x0, matrix products: 197 us -> none  [the longest x48 91.6 us: mul_t(): lax.dot_general(a, b, (((1,), (1,)), ((), ())), preferred_element_type=F32)]
    pallas_call x4 -> x13, Pallas kernels: 38.6 us -> 160 us  [the longest x2 40 us: attn_backward(): pl.pallas_call(backward_kernel, in_specs=smem(2) + vmem(20), out_specs=vm...]
    psum x2 -> x0, blocking collectives: 66.2 us -> none  [the longest x1 38.3 us: on_device(): small = lax.psum(small, ('rows', 'hid'))]
    ppermute x18 -> x24, waiting for transfers between devices: 145 us -> 86.7 us  [send(): self.got = lax.ppermute(self.value, 'rows', moves[self.stage])]
    ppermute x10 -> x9, waiting for transfers between devices: 70.2 us -> 30.3 us  [swap_chip(): return lax.ppermute(a, 'hid', [(0, 2), (2, 0), (1, 3), (3, 1)])]
    ppermute x21 -> x17, waiting for transfers between devices: 48 us -> 83.9 us  [swap_wid(): return lax.ppermute(a, 'wid', [(0, 1), (1, 0)])]
    convert_element_type x32 -> x43, other arithmetic: 40 us -> 55.3 us  [the longest x16 17.5 us: take(): (self.value.astype(F32) + then(self.got).astype(F32)).astype(BF)]
    ppermute x18 -> x24, starting transfers between devices: 63.1 us -> 51.3 us  [send(): self.got = lax.ppermute(self.value, 'rows', moves[self.stage])]
  transfers between devices with their start and end apart: 63 -> 67, of which waited for: 20 -> 24; matrix products, arithmetic and copies ran while one was open for 34% -> 17% of each run, Pallas kernels for 5% -> 23%
where the time goes in v2:
time: 603 us; the launch traced here: 592 us
  waiting for transfers between devices  203 us (34%)
  Pallas kernels  160 us (27%)
  other arithmetic  83.6 us (14%)
  starting transfers between devices  80.6 us (13%)
  local copies, waits for them, and re-layouts  48 us (8%)
  between operations  16.2 us (3%)
    ppermute x24, waiting for transfers between devices, send(): self.got = lax.ppermute(self.value, 'rows', moves[self.stage])  86.7 us
    ppermute x17, waiting for transfers between devices, swap_wid(): return lax.ppermute(a, 'wid', [(0, 1), (1, 0)])  83.9 us
    ppermute x24, starting transfers between devices, send(): self.got = lax.ppermute(self.value, 'rows', moves[self.stage])  51.3 us
    pallas_call x2, Pallas kernels, attn_backward(): pl.pallas_call(backward_kernel, in_specs=smem(2) + vmem(20), out_specs=vm...  40 us
    ppermute x9, waiting for transfers between devices, swap_chip(): return lax.ppermute(a, 'hid', [(0, 2), (2, 0), (1, 3), (3, 1)])  30.3 us
    pallas_call x2, Pallas kernels, ffn_down(): pl.pallas_call(down_kernel, grid=(hidden // tile,), in_specs=[whole] * 2...  27.2 us
    unnamed x240, local copies, waits for them, and re-layouts  23.7 us
    pallas_call x2, Pallas kernels, attn_solve(): pl.pallas_call(solve_kernel, in_specs=smem(2) + vmem(7), out_specs=vmem(5...  23.5 us
  transfers between devices with their start and end apart: 67, of which 24 were waited for; matrix products, arithmetic and copies ran while one was open for 17% of the time, Pallas kernels for 23%

profile of v2, /device:TPU:0, one launch (start us, length us, event | category | flops | bytes accessed | tf_op | source)
XLA Modules:
  0.0 591.9 jit_solution(12170711009687679679)
XLA Ops:
  11.5 9.1 %collective-permute-done = bf16[2,128,768]{2,1,0:T(8,128)(2,1)S(1)} collective-permute-done((bf16[2,128,768]{2,1,0:T(8,128)(2,1)S(1)}, bf16[2,128,768]{2,1,0:T(8,128)(2,1)S(1)}, u32[]{:S(2)}, u32[]{:S(2)}) %collective-permute-start) | collective-permute-done | bytes 393248 | tf_op jit(solution)/shard_map/ppermute | solution.py:676
  29.2 11.4 %collective-permute-done.1 = bf16[2,128,1536]{2,1,0:T(8,128)(2,1)} collective-permute-done((bf16[2,128,1536]{2,1,0:T(8,128)(2,1)}, bf16[2,128,1536]{2,1,0:T(8,128)(2,1)}, u32[]{:S(2)}, u32[]{:S(2)}) %collective-permute-start.1) | collective-permute-done | bytes 786464 | tf_op jit(solution)/shard_map/ppermute | solution.py:684
  65.2 11.5 %attn_solve.2 = (bf16[512,384]{1,0:T(8,128)(2,1)S(1)}, f32[512,384]{1,0:T(8,128)S(1)}, f32[512,3]{1,0:T(8,128)S(1)}, bf16[3,512,512]{2,1,0:T(8,128)(2,1)}, bf16[3,2,256,256]{3,2,1,0:T(8,128)(2,1)S(1)}) custom-call(s32[4]{0:T(128)S(1)} %get-tuple-element.345.starts_ref, s32[1]{0:T(128)} %bitcast.7.core_ref, ...), custom_call_target="tpu_custom_call" | custom-call | flops 3600000000 | bytes 1000 | tf_op jit(solution)/shard_map/attn_solve/pallas_call | solution.py:391
  76.7 12.0 %attn_solve.3 = (bf16[512,384]{1,0:T(8,128)(2,1)S(1)}, f32[512,384]{1,0:T(8,128)S(1)}, f32[512,3]{1,0:T(8,128)S(1)}, bf16[3,512,512]{2,1,0:T(8,128)(2,1)}, bf16[3,2,256,256]{3,2,1,0:T(8,128)(2,1)S(1)}) custom-call(s32[4]{0:T(128)S(1)} %get-tuple-element.344.starts_ref, s32[1]{0:T(128)} %bitcast.7.core_ref, ...), custom_call_target="tpu_custom_call" | custom-call | flops 3600000000 | bytes 1000 | tf_op jit(solution)/shard_map/attn_solve/pallas_call | solution.py:391
  89.7 10.5 %collective-permute-done.6.qv1_ref = bf16[768,768]{1,0:T(8,128)(2,1)S(1)} collective-permute-done((bf16[768,768]{1,0:T(8,128)(2,1)S(1)}, bf16[768,768]{1,0:T(8,128)(2,1)S(1)}, u32[]{:S(2)}, u32[]{:S(2)}) %collective-permute-start.6) | collective-permute-done | bytes 1179680 | tf_op jit(solution)/shard_map/ppermute | solution.py:676
  101.2 8.7 %attn_forward.2 = (bf16[512,384]{1,0:T(8,128)(2,1)S(1)}, bf16[512,384]{1,0:T(8,128)(2,1)S(1)}, bf16[512,384]{1,0:T(8,128)(2,1)S(1)}, bf16[3,512,512]{2,1,0:T(8,1...) custom-call(s32[4]{0:T(128)S(1)} %get-tuple-element.345.starts_ref, s32[1]{0:T(128)} %bitcast.7.core_ref, ...), custom_call_target="tpu_custom_call" | custom-call | flops 2700000000 | bytes 1000 | tf_op jit(solution)/shard_map/attn_forward/pallas_call | solution.py:411
  138.7 8.8 %attn_forward.3 = (bf16[512,384]{1,0:T(8,128)(2,1)S(1)}, bf16[512,384]{1,0:T(8,128)(2,1)S(1)}, bf16[512,384]{1,0:T(8,128)(2,1)S(1)}, bf16[3,512,512]{2,1,0:T(8,1...) custom-call(s32[4]{0:T(128)S(1)} %get-tuple-element.344.starts_ref, s32[1]{0:T(128)} %bitcast.7.core_ref, ...), custom_call_target="tpu_custom_call" | custom-call | flops 2700000000 | bytes 1000 | tf_op jit(solution)/shard_map/attn_forward/pallas_call | solution.py:411
  158.0 15.1 %collective-permute-done.11 = bf16[256,1536]{1,0:T(8,128)(2,1)} collective-permute-done((bf16[256,1536]{1,0:T(8,128)(2,1)}, bf16[256,1536]{1,0:T(8,128)(2,1)}, u32[]{:S(2)}, u32[]{:S(2)}) %collective-permute-start.11) | collective-permute-done | bytes 786464 | tf_op jit(solution)/shard_map/ppermute | solution.py:684
  179.6 13.7 %collective-permute-done.17.refs_9_.refs_7_ = bf16[768,1024]{1,0:T(8,128)(2,1)} collective-permute-done((bf16[768,1024]{1,0:T(8,128)(2,1)}, bf16[768,1024]{1,0:T(8,128)(2,1)}, u32[]{:S(2)}, u32[]{:S(2)}) %collective-permute-start.17) | collective-permute-done | bytes 1572896 | tf_op jit(solution)/shard_map/ppermute | solution.py:676
  193.4 16.9 %ffn_up.1 = (bf16[1024,1024]{1,0:T(8,128)(2,1)}, bf16[1024,1024]{1,0:T(8,128)(2,1)}, bf16[1024,1024]{1,0:T(8,128)(2,1)}, f32[1024,768]{1,0:T(8,128)}, bf16[1024,768]{1,0:T(8,128)(2,1)}) custom-call(bf16[256,1536]{1,0:T(8,128)(2,1)S(1)} %multiply_convert_fusion.2.refs_0_, bf16[256,1536]{1,0:T(8,128)(2,1)} %collective-permute-done.12.refs_1_, ...), custom_call_target="tpu_custom_call" | custom-call | flops 4800000000 | bytes 1000 | tf_op jit(solution)/shard_map/ffn_up/pallas_call | solution.py:607
  210.3 13.1 %ffn_down.2 = (bf16[512,1024]{1,0:T(8,128)(2,1)S(1)}, bf16[512,1024]{1,0:T(8,128)(2,1)S(1)}, f32[256,1536]{1,0:T(8,128)S(1)}, bf16[256,1536]{1,0:T(8,128)(2,1)S(1)}) custom-call(bf16[256,1536]{1,0:T(8,128)(2,1)S(1)} %bitcast.125, bf16[256,1536]{1,0:T(8,128)(2,1)S(1)} %get-tuple-element.323.refs_5_.refs_1_, bf16[1024,1024]{1,0:T(8,128)(2,1)} %get-tuple-element.171.refs_2_, ...), custom_call_target="tpu_custom_call" | custom-call | flops 3900000000 | bytes 1000 | tf_op jit(solution)/shard_map/ffn_down/pallas_call | solution.py:661
  228.9 14.0 %ffn_down.3 = (bf16[512,1024]{1,0:T(8,128)(2,1)S(1)}, bf16[512,1024]{1,0:T(8,128)(2,1)S(1)}, f32[256,1536]{1,0:T(8,128)S(1)}, bf16[256,1536]{1,0:T(8,128)(2,1)}) custom-call(bf16[256,1536]{1,0:T(8,128)(2,1)S(1)} %bitcast.123, bf16[256,1536]{1,0:T(8,128)(2,1)S(1)} %copy-done.2, bf16[1024,1024]{1,0:T(8,128)(2,1)} %get-tuple-element.171.refs_2_, ...), custom_call_target="tpu_custom_call" | custom-call | flops 3900000000 | bytes 1000 | tf_op jit(solution)/shard_map/ffn_down/pallas_call | solution.py:661
  249.5 7.8 %ffn_grad.2 = (f32[768,1024]{1,0:T(8,128)}, bf16[768,1024]{1,0:T(8,128)(2,1)}) custom-call(bf16[256,1536]{1,0:T(8,128)(2,1)S(1)} %copy-done.13, bf16[256,1536]{1,0:T(8,128)(2,1)} %collective-permute-done.12.refs_1_, bf16[256,1536]{1,0:T(8,128)(2,1)} %multiply_convert_fusion.1.refs_2_, bf16[256,1536]{1,0:T(8,128)(2,1)} %collective-permute-done.13.refs_3_, ...), custom_call_target="tpu_custom_call" | custom-call | flops 1800000000 | bytes 1000 | tf_op jit(solution)/shard_map/ffn_grad/pallas_call | solution.py:505
  276.2 20.0 %attn_backward.2 = (bf16[512,896]{1,0:T(8,128)(2,1)}, bf16[512,768]{1,0:T(8,128)(2,1)S(1)}, f32[256,1536]{1,0:T(8,128)}, bf16[256,1536]{1,0:T(8,128)(2,1)S(1)}, f32[1,1536]{1,0:T(1,128)S(1)}) custom-call(s32[4]{0:T(128)S(1)} %get-tuple-element.345.starts_ref, s32[1]{0:T(128)} %bitcast.7.core_ref, bf16[512,384]{1,0:T(8,128)(2,1)S(1)} %copy-done.47, ...), custom_call_target="tpu_custom_call" | custom-call | flops 6300000256 | bytes 1000 | tf_op jit(solution)/shard_map/attn_backward/pallas_call | solution.py:433
  317.8 7.8 %ffn_grad.3 = (f32[768,1024]{1,0:T(8,128)}, bf16[768,1024]{1,0:T(8,128)(2,1)}) custom-call(bf16[256,1536]{1,0:T(8,128)(2,1)S(1)} %copy-done.13, bf16[256,1536]{1,0:T(8,128)(2,1)} %collective-permute-done.12.refs_1_, bf16[256,1536]{1,0:T(8,128)(2,1)} %multiply_convert_fusion.1.refs_2_, bf16[256,1536]{1,0:T(8,128)(2,1)} %collective-permute-done.13.refs_3_, ...), custom_call_target="tpu_custom_call" | custom-call | flops 1800000000 | bytes 1000 | tf_op jit(solution)/shard_map/ffn_grad/pallas_call | solution.py:505
  327.2 20.0 %attn_backward.3 = (bf16[512,896]{1,0:T(8,128)(2,1)}, bf16[512,768]{1,0:T(8,128)(2,1)S(1)}, f32[256,1536]{1,0:T(8,128)}, bf16[256,1536]{1,0:T(8,128)(2,1)S(1)}, f32[1,1536]{1,0:T(1,128)S(1)}) custom-call(s32[4]{0:T(128)S(1)} %get-tuple-element.344.starts_ref, s32[1]{0:T(128)} %bitcast.7.core_ref, bf16[512,384]{1,0:T(8,128)(2,1)S(1)} %copy-done.43, ...), custom_call_target="tpu_custom_call" | custom-call | flops 6300000256 | bytes 1000 | tf_op jit(solution)/shard_map/attn_backward/pallas_call | solution.py:433
  355.4 13.3 %attn_grad.1 = (f32[768,1024]{1,0:T(8,128)}, f32[768,1024]{1,0:T(8,128)}, bf16[768,1024]{1,0:T(8,128)(2,1)}, bf16[768,1024]{1,0:T(8,128)(2,1)}) custom-call(s32[1]{0:T(128)} %bitcast.7.core_ref, bf16[256,1536]{1,0:T(8,128)(2,1)S(1)} %copy-done.7, bf16[256,1536]{1,0:T(8,128)(2,1)S(1)} %copy-done.11, bf16[256,1536]{1,0:T(8,128)(2,1)S(1)} %copy-done.5, ...), custom_call_target="tpu_custom_call" | custom-call | flops 4200000000 | bytes 1000 | tf_op jit(solution)/shard_map/attn_grad/pallas_call | solution.py:561
  382.2 22.7 %collective-permute-done.36 = bf16[768,1024]{1,0:T(8,128)(2,1)S(1)} collective-permute-done((bf16[768,1024]{1,0:T(8,128)(2,1)}, bf16[768,1024]{1,0:T(8,128)(2,1)S(1)}, u32[]{:S(2)}, u32[]{:S(2)}) %collective-permute-start.36) | collective-permute-done | bytes 1572896 | tf_op jit(solution)/shard_map/ppermute | solution.py:676
  418.9 10.3 %collective-permute-done.32 = bf16[768,512]{1,0:T(8,128)(2,1)S(1)} collective-permute-done((bf16[768,512]{1,0:T(8,128)(2,1)S(1)}, bf16[768,512]{1,0:T(8,128)(2,1)S(1)}, u32[]{:S(2)}, u32[]{:S(2)}) %collective-permute-start.32) | collective-permute-done | bytes 786464 | tf_op jit(solution)/shard_map/ppermute | solution.py:701
  451.4 12.4 %collective-permute-done.44 = bf16[768,1024]{1,0:T(8,128)(2,1)} collective-permute-done((bf16[768,1024]{1,0:T(8,128)(2,1)S(1)}, bf16[768,1024]{1,0:T(8,128)(2,1)}, u32[]{:S(2)}, u32[]{:S(2)}) %collective-permute-start.44) | collective-permute-done | bytes 1572896 | tf_op jit(solution)/shard_map/ppermute | solution.py:701
  469.4 9.2 %collective-permute-done.41 = bf16[768,512]{1,0:T(8,128)(2,1)S(1)} collective-permute-done((bf16[768,512]{1,0:T(8,128)(2,1)S(1)}, bf16[768,512]{1,0:T(8,128)(2,1)S(1)}, u32[]{:S(2)}, u32[]{:S(2)}) %collective-permute-start.41) | collective-permute-done | bytes 786464 | tf_op jit(solution)/shard_map/ppermute | solution.py:701
  482.9 10.5 %collective-permute-done.49 = bf16[768,512]{1,0:T(8,128)(2,1)S(1)} collective-permute-done((bf16[768,512]{1,0:T(8,128)(2,1)S(1)}, bf16[768,512]{1,0:T(8,128)(2,1)S(1)}, u32[]{:S(2)}, u32[]{:S(2)}) %collective-permute-start.49) | collective-permute-done | bytes 786464 | tf_op jit(solution)/shard_map/ppermute | solution.py:701
  515.1 14.8 %collective-permute-done.50 = bf16[768,512]{1,0:T(8,128)(2,1)S(1)} collective-permute-done((bf16[768,512]{1,0:T(8,128)(2,1)S(1)}, bf16[768,512]{1,0:T(8,128)(2,1)S(1)}, u32[]{:S(2)}, u32[]{:S(2)}) %collective-permute-start.50) | collective-permute-done | bytes 786464 | tf_op jit(solution)/shard_map/ppermute | solution.py:701
  534.7 17.5 %collective-permute-done.58 = bf16[768,512]{1,0:T(8,128)(2,1)S(1)} collective-permute-done((bf16[768,512]{1,0:T(8,128)(2,1)S(1)}, bf16[768,512]{1,0:T(8,128)(2,1)S(1)}, u32[]{:S(2)}, u32[]{:S(2)}) %collective-permute-start.58) | collective-permute-done | bytes 786464 | tf_op jit(solution)/shard_map/ppermute | solution.py:701
  (495 shorter events, 264.6 us)
Async XLA Ops:
  7.2 172.5 %all-gather.3.cloned.1.call-start = ((), (), s32[]{:S(2)}) async-start(), calls=%async_computation | async-start | bytes 1966080 | tf_op jit(solution)/shard_map/all_gather | solution.py:764
  60.9 39.3 %collective-permute-start.6 = (bf16[768,768]{1,0:T(8,128)(2,1)S(1)}, bf16[768,768]{1,0:T(8,128)(2,1)S(1)}, u32[]{:S(2)}, u32[]{:S(2)}) collective-permute-start(bf16[768,768]{1,0:T(8,128)(2,1)S(1)} %constant_dynamic-update-slice_fusion.qv0_ref), channel_id=1, source_target_pairs={{0,1},{1,0},{2,3},{3,2},{4,5},{5,4},{6,7},{7,6},{8,9},{9,8},{10,11... | collective-permute-start | bytes 3538952 | tf_op jit(solution)/shard_map/ppermute | solution.py:676
  121.7 34.5 %collective-permute-start.19 = (bf16[256,768]{1,0:T(8,128)(2,1)}, bf16[256,768]{1,0:T(8,128)(2,1)}, u32[]{:S(2)}, u32[]{:S(2)}) collective-permute-start(bf16[256,768]{1,0:T(8,128)(2,1)} %constant_dynamic-slice_fusion.7), channel_id=1, source_target_pairs={{0,1},{1,0},{2,3},{3,2},{4,5},{5,4},{6,7},{7,6},{8,9},{9,8},{10,11... | collective-permute-start | bytes 1179656 | tf_op jit(solution)/shard_map/ppermute | solution.py:676
  126.6 83.7 %all-gather.5.cloned.1.call-start = ((), (), s32[]{:S(2)}) async-start(), calls=%async_computation.1 | async-start | bytes 1966080 | tf_op jit(solution)/shard_map/all_gather | solution.py:764
  156.2 37.2 %collective-permute-start.17 = (bf16[768,1024]{1,0:T(8,128)(2,1)}, bf16[768,1024]{1,0:T(8,128)(2,1)}, u32[]{:S(2)}, u32[]{:S(2)}) collective-permute-start(bf16[768,1024]{1,0:T(8,128)(2,1)} %refs_6_.3), channel_id=1, source_target_pairs={{0,1},{1,0},{2,3},{3,2},{4,5},{5,4},{6,7},{7,6},{8,9},{9,8},{10,11... | collective-permute-start | bytes 4718600 | tf_op jit(solution)/shard_map/ppermute | solution.py:676
  157.7 35.6 %collective-permute-start.12 = (bf16[256,1536]{1,0:T(8,128)(2,1)S(1)}, bf16[256,1536]{1,0:T(8,128)(2,1)}, u32[]{:S(2)}, u32[]{:S(2)}) collective-permute-start(bf16[256,1536]{1,0:T(8,128)(2,1)S(1)} %multiply_convert_fusion.2.refs_0_), channel_id=1, source_target_pairs={{0,2},{2,0},{4,6},{6,4},{1,3},{3,1},{5,7},{7,5},{8,10},{10,8},{12,... | collective-permute-start | bytes 2359304 | tf_op jit(solution)/shard_map/ppermute | solution.py:680
  225.4 37.5 %collective-permute-start.23 = (bf16[1024,768]{1,0:T(8,128)(2,1)}, bf16[1024,768]{1,0:T(8,128)(2,1)}, u32[]{:S(2)}, u32[]{:S(2)}) collective-permute-start(bf16[1024,768]{1,0:T(8,128)(2,1)} %get-tuple-element.184), channel_id=1, source_target_pairs={{0,1},{1,0},{2,3},{3,2},{4,5},{5,4},{6,7},{7,6},{8,9},{9,8},{10,11... | collective-permute-start | bytes 4718600 | tf_op jit(solution)/shard_map/ppermute | solution.py:676
  257.3 39.0 %collective-permute-start.25 = (bf16[768,1024]{1,0:T(8,128)(2,1)}, bf16[768,1024]{1,0:T(8,128)(2,1)}, u32[]{:S(2)}, u32[]{:S(2)}) collective-permute-start(bf16[768,1024]{1,0:T(8,128)(2,1)} %get-tuple-element.186), channel_id=1, source_target_pairs={{0,1},{1,0},{2,3},{3,2},{4,5},{5,4},{6,7},{7,6},{8,9},{9,8},{10,11... | collective-permute-start | bytes 4718600 | tf_op jit(solution)/shard_map/ppermute | solution.py:676
  264.8 36.6 %collective-permute-start.24 = (bf16[1024,768]{1,0:T(8,128)(2,1)S(1)}, bf16[1024,768]{1,0:T(8,128)(2,1)}, u32[]{:S(2)}, u32[]{:S(2)}) collective-permute-start(bf16[1024,768]{1,0:T(8,128)(2,1)S(1)} %add_convert_fusion.5), channel_id=1, source_target_pairs={{0,8},{24,16},{1,9},{25,17},{2,10},{26,18},{3,11},{27,19},{4,12},{... | collective-permute-start | bytes 4718600 | tf_op jit(solution)/shard_map/ppermute | solution.py:701
  308.7 41.3 %collective-permute-start.30 = (bf16[1024,768]{1,0:T(8,128)(2,1)}, bf16[1024,768]{1,0:T(8,128)(2,1)}, u32[]{:S(2)}, u32[]{:S(2)}) collective-permute-start(bf16[1024,768]{1,0:T(8,128)(2,1)} %add_convert_fusion.3), channel_id=1, source_target_pairs={{8,16},{16,8},{9,17},{17,9},{10,18},{18,10},{11,19},{19,11},{12,20... | collective-permute-start | bytes 4718600 | tf_op jit(solution)/shard_map/ppermute | solution.py:701
  310.5 41.9 %collective-permute-start.29 = (bf16[768,1024]{1,0:T(8,128)(2,1)}, bf16[768,1024]{1,0:T(8,128)(2,1)}, u32[]{:S(2)}, u32[]{:S(2)}) collective-permute-start(bf16[768,1024]{1,0:T(8,128)(2,1)} %add_convert_fusion.4), channel_id=1, source_target_pairs={{0,8},{24,16},{1,9},{25,17},{2,10},{26,18},{3,11},{27,19},{4,12},{... | collective-permute-start | bytes 4718600 | tf_op jit(solution)/shard_map/ppermute | solution.py:701
  325.6 48.3 %collective-permute-start.28 = (bf16[768,1024]{1,0:T(8,128)(2,1)}, bf16[768,1024]{1,0:T(8,128)(2,1)}, u32[]{:S(2)}, u32[]{:S(2)}) collective-permute-start(bf16[768,1024]{1,0:T(8,128)(2,1)} %get-tuple-element.203), channel_id=1, source_target_pairs={{0,1},{1,0},{2,3},{3,2},{4,5},{5,4},{6,7},{7,6},{8,9},{9,8},{10,11... | collective-permute-start | bytes 4718600 | tf_op jit(solution)/shard_map/ppermute | solution.py:676
  368.7 36.1 %collective-permute-start.36 = (bf16[768,1024]{1,0:T(8,128)(2,1)}, bf16[768,1024]{1,0:T(8,128)(2,1)S(1)}, u32[]{:S(2)}, u32[]{:S(2)}) collective-permute-start(bf16[768,1024]{1,0:T(8,128)(2,1)} %get-tuple-element.219), channel_id=1, source_target_pairs={{0,1},{1,0},{2,3},{3,2},{4,5},{5,4},{6,7},{7,6},{8,9},{9,8},{10,11... | collective-permute-start | bytes 4718600 | tf_op jit(solution)/shard_map/ppermute | solution.py:676
  369.4 138.8 %collective-permute-start.52 = (bf16[256,1536]{1,0:T(8,128)(2,1)S(1)}, bf16[256,1536]{1,0:T(8,128)(2,1)}, u32[]{:S(2)}, u32[]{:S(2)}) collective-permute-start(bf16[256,1536]{1,0:T(8,128)(2,1)S(1)} %get-tuple-element.248), channel_id=1, source_target_pairs={{0,2},{2,0},{4,6},{6,4},{1,3},{3,1},{5,7},{7,5},{8,10},{10,8},{12,... | collective-permute-start | bytes 2359304 | tf_op jit(solution)/shard_map/ppermute | solution.py:680
  369.5 42.9 %collective-permute-start.34 = (bf16[768,1024]{1,0:T(8,128)(2,1)S(1)}, bf16[768,1024]{1,0:T(8,128)(2,1)S(1)}, u32[]{:S(2)}, u32[]{:S(2)}) collective-permute-start(bf16[768,1024]{1,0:T(8,128)(2,1)S(1)} %add_convert_fusion.1), channel_id=1, source_target_pairs={{8,16},{16,8},{9,17},{17,9},{10,18},{18,10},{11,19},{19,11},{12,20... | collective-permute-start | bytes 4718600 | tf_op jit(solution)/shard_map/ppermute | solution.py:701
  372.4 43.0 %collective-permute-start.33 = (bf16[1024,768]{1,0:T(8,128)(2,1)S(1)}, bf16[1024,768]{1,0:T(8,128)(2,1)S(1)}, u32[]{:S(2)}, u32[]{:S(2)}) collective-permute-start(bf16[1024,768]{1,0:T(8,128)(2,1)S(1)} %add_convert_fusion.2), channel_id=1, source_target_pairs={{8,0},{16,24},{9,1},{17,25},{10,2},{18,26},{11,3},{19,27},{12,4},{... | collective-permute-start | bytes 4718600 | tf_op jit(solution)/shard_map/ppermute | solution.py:701
  404.9 35.3 %collective-permute-start.40 = (bf16[768,1024]{1,0:T(8,128)(2,1)}, bf16[768,1024]{1,0:T(8,128)(2,1)}, u32[]{:S(2)}, u32[]{:S(2)}) collective-permute-start(bf16[768,1024]{1,0:T(8,128)(2,1)} %get-tuple-element.233), channel_id=1, source_target_pairs={{0,1},{1,0},{2,3},{3,2},{4,5},{5,4},{6,7},{7,6},{8,9},{9,8},{10,11... | collective-permute-start | bytes 4718600 | tf_op jit(solution)/shard_map/ppermute | solution.py:676
  415.5 34.3 %collective-permute-start.38 = (bf16[768,512]{1,0:T(8,128)(2,1)}, bf16[768,512]{1,0:T(8,128)(2,1)}, u32[]{:S(2)}, u32[]{:S(2)}) collective-permute-start(bf16[768,512]{1,0:T(8,128)(2,1)} %add_convert_fusion.19), channel_id=1, source_target_pairs={{8,16},{16,8},{9,17},{17,9},{10,18},{18,10},{11,19},{19,11},{12,20... | collective-permute-start | bytes 2359304 | tf_op jit(solution)/shard_map/ppermute | solution.py:701
  429.2 34.6 %collective-permute-start.44 = (bf16[768,1024]{1,0:T(8,128)(2,1)S(1)}, bf16[768,1024]{1,0:T(8,128)(2,1)}, u32[]{:S(2)}, u32[]{:S(2)}) collective-permute-start(bf16[768,1024]{1,0:T(8,128)(2,1)S(1)} %add_convert_fusion), channel_id=1, source_target_pairs={{8,0},{16,24},{9,1},{17,25},{10,2},{18,26},{11,3},{19,27},{12,4},{... | collective-permute-start | bytes 4718600 | tf_op jit(solution)/shard_map/ppermute | solution.py:701
  468.6 40.9 %collective-permute-start.54 = (bf16[256,1536]{1,0:T(8,128)(2,1)S(1)}, bf16[256,1536]{1,0:T(8,128)(2,1)S(1)}, u32[]{:S(2)}, u32[]{:S(2)}) collective-permute-start(bf16[256,1536]{1,0:T(8,128)(2,1)S(1)} %get-tuple-element.252), channel_id=1, source_target_pairs={{0,2},{2,0},{4,6},{6,4},{1,3},{3,1},{5,7},{7,5},{8,10},{10,8},{12,... | collective-permute-start | bytes 2359304 | tf_op jit(solution)/shard_map/ppermute | solution.py:680
  509.5 46.8 %collective-permute-start.56 = (bf16[768,512]{1,0:T(8,128)(2,1)S(1)}, bf16[768,512]{1,0:T(8,128)(2,1)S(1)}, u32[]{:S(2)}, u32[]{:S(2)}) collective-permute-start(bf16[768,512]{1,0:T(8,128)(2,1)S(1)} %add_convert_fusion.9), channel_id=1, source_target_pairs={{8,16},{16,8},{9,17},{17,9},{10,18},{18,10},{11,19},{19,11},{12,20... | collective-permute-start | bytes 2359304 | tf_op jit(solution)/shard_map/ppermute | solution.py:701
  512.2 40.1 %collective-permute-start.57 = (bf16[2,128,1536]{2,1,0:T(8,128)(2,1)S(1)}, bf16[2,128,1536]{2,1,0:T(8,128)(2,1)S(1)}, u32[]{:S(2)}, u32[]{:S(2)}) collective-permute-start(bf16[2,128,1536]{2,1,0:T(8,128)(2,1)S(1)} %fusion.18), channel_id=1, source_target_pairs={{0,4},{4,0},{2,6},{6,2},{1,5},{5,1},{3,7},{7,3},{8,12},{12,8},{10,... | collective-permute-start | bytes 2359304 | tf_op jit(solution)/shard_map/ppermute | solution.py:684
  531.8 39.0 %collective-permute-start.55 = (bf16[2,128,768]{2,1,0:T(8,128)(2,1)S(1)}, bf16[2,128,768]{2,1,0:T(8,128)(2,1)}, u32[]{:S(2)}, u32[]{:S(2)}) collective-permute-start(bf16[2,128,768]{2,1,0:T(8,128)(2,1)S(1)} %slice.253), channel_id=1, source_target_pairs={{0,1},{1,0},{2,3},{3,2},{4,5},{5,4},{6,7},{7,6},{8,9},{9,8},{10,11... | collective-permute-start | bytes 1179656 | tf_op jit(solution)/shard_map/ppermute | solution.py:676
  533.4 34.1 %collective-permute-start.61 = (bf16[768,512]{1,0:T(8,128)(2,1)}, bf16[768,512]{1,0:T(8,128)(2,1)}, u32[]{:S(2)}, u32[]{:S(2)}) collective-permute-start(bf16[768,512]{1,0:T(8,128)(2,1)} %add_convert_fusion.7), channel_id=1, source_target_pairs={{8,0},{16,24},{9,1},{17,25},{10,2},{18,26},{11,3},{19,27},{12,4},{... | collective-permute-start | bytes 2359304 | tf_op jit(solution)/shard_map/ppermute | solution.py:701
  (162 other events, 1857.3 us)
Sparse Core Ops, SparseCore 0:
  126.7 37.4 all-gather.2
  165.7 35.9 all-gather.4

commit v3 on v2

--- a/solution.py
+++ b/solution.py
@@ -492,7 +492,7 @@
             turned[:, p * rows : (p + 1) * rows] = a[p][...].T
 
     out = mul(turned[:, : 2 * rows], b[0][...]) + mul(turned[:, 2 * rows :], b[1][...])
-    own_ref[...] = out[:part]
+    own_ref[...] = out[:part].astype(BF)
     far_ref[...] = out[part:].astype(BF)
 
 
@@ -507,7 +507,7 @@
         grid=(hidden // tile,),
         in_specs=[whole] * 4 + [cols] * 2,
         out_specs=[out, out],
-        out_shape=[shape_of(width // 2, hidden, kind=F32), shape_of(width // 2, hidden)],
+        out_shape=[shape_of(width // 2, hidden)] * 2,
         scratch_shapes=[pltpu.VMEM((width, 4 * rows), BF)],
         compiler_params=params(),
         cost_estimate=cost(6),
@@ -562,7 +562,7 @@
         attn_grad_kernel,
         in_specs=smem(1) + vmem(16),
         out_specs=vmem(4),
-        out_shape=[shape_of(part, n, kind=F32) for n in sizes] + [shape_of(part, n) for n in sizes],
+        out_shape=[shape_of(part, n) for n in sizes * 2],
         scratch_shapes=[
             pltpu.VMEM((width, 4 * rows), BF),
             pltpu.VMEM((width, 4 * rows), BF),
@@ -593,7 +593,7 @@
         two_ref[at, :] = swish.astype(BF)
         act_ref[at, :] = act
         total = total + mul(act.T, g[p][...])
-    own_ref[...] = total[:, :part]
+    own_ref[...] = total[:, :part].astype(BF)
     far_ref[...] = total[:, part:].astype(BF)
 
 
@@ -610,7 +610,7 @@
         in_specs=[whole] * 8 + [cols] * 4,
         out_specs=[tall] * 3 + [flat] * 2,
         out_shape=[shape_of(4 * rows, hidden)] * 3
-        + [shape_of(hidden, part, kind=F32), shape_of(hidden, part)],
+        + [shape_of(hidden, part)] * 2,
         compiler_params=params(),
         cost_estimate=cost(16),
         name="ffn_up",
@@ -900,7 +900,7 @@
         def low():
             own, near, part_of = ready[name]
             near = then(near)[:, part_of].astype(F32)
-            state["sum"] = RowSum(mark((own[:, part_of] + near).astype(BF)))
+            state["sum"] = RowSum(mark((own[:, part_of].astype(F32) + near).astype(BF)))
             state["sum"].send()
 
         def more():

time: 603 us -> 607 us (level)
  waiting for transfers between devices: 203 us -> 212 us
    ppermute x24, waiting for transfers between devices: 86.7 us -> 92.9 us  [send(): self.got = lax.ppermute(self.value, 'rows', moves[self.stage])]
    unnamed x240 -> x244, local copies, waits for them, and re-layouts: 23.7 us -> 24.5 us
where the time goes in v3:
time: 607 us; the launch traced here: 595 us
  waiting for transfers between devices  212 us (35%)
  Pallas kernels  159 us (26%)
  other arithmetic  81 us (13%)
  starting transfers between devices  77.3 us (13%)
  local copies, waits for them, and re-layouts  48.9 us (8%)
  between operations  16.3 us (3%)
    ppermute x24, waiting for transfers between devices, send(): self.got = lax.ppermute(self.value, 'rows', moves[self.stage])  92.9 us
    ppermute x17, waiting for transfers between devices, swap_wid(): return lax.ppermute(a, 'wid', [(0, 1), (1, 0)])  86 us
    ppermute x24, starting transfers between devices, send(): self.got = lax.ppermute(self.value, 'rows', moves[self.stage])  48.3 us
    pallas_call x2, Pallas kernels, attn_backward(): pl.pallas_call(backward_kernel, in_specs=smem(2) + vmem(20), out_specs=vm...  40 us
    ppermute x9, waiting for transfers between devices, swap_chip(): return lax.ppermute(a, 'hid', [(0, 2), (2, 0), (1, 3), (3, 1)])  30.6 us
    pallas_call x2, Pallas kernels, ffn_down(): pl.pallas_call(down_kernel, grid=(hidden // tile,), in_specs=[whole] * 2...  27.2 us
    unnamed x244, local copies, waits for them, and re-layouts  24.5 us
    pallas_call x2, Pallas kernels, attn_solve(): pl.pallas_call(solve_kernel, in_specs=smem(2) + vmem(7), out_specs=vmem(5...  23.5 us
  transfers between devices with their start and end apart: 67, of which 24 were waited for; matrix products, arithmetic and copies ran while one was open for 17% of the time, Pallas kernels for 23%

profile of v3, /device:TPU:0, one launch (start us, length us, event | category | flops | bytes accessed | tf_op | source)
XLA Modules:
  0.0 595.1 jit_solution(2947962529283766984)
XLA Ops:
  11.5 9.1 %collective-permute-done = bf16[2,128,768]{2,1,0:T(8,128)(2,1)S(1)} collective-permute-done((bf16[2,128,768]{2,1,0:T(8,128)(2,1)S(1)}, bf16[2,128,768]{2,1,0:T(8,128)(2,1)S(1)}, u32[]{:S(2)}, u32[]{:S(2)}) %collective-permute-start) | collective-permute-done | bytes 393248 | tf_op jit(solution)/shard_map/ppermute | solution.py:676
  29.2 11.4 %collective-permute-done.1 = bf16[2,128,1536]{2,1,0:T(8,128)(2,1)} collective-permute-done((bf16[2,128,1536]{2,1,0:T(8,128)(2,1)}, bf16[2,128,1536]{2,1,0:T(8,128)(2,1)}, u32[]{:S(2)}, u32[]{:S(2)}) %collective-permute-start.1) | collective-permute-done | bytes 786464 | tf_op jit(solution)/shard_map/ppermute | solution.py:684
  65.2 11.5 %attn_solve.2 = (bf16[512,384]{1,0:T(8,128)(2,1)S(1)}, f32[512,384]{1,0:T(8,128)S(1)}, f32[512,3]{1,0:T(8,128)S(1)}, bf16[3,512,512]{2,1,0:T(8,128)(2,1)}, bf16[3,2,256,256]{3,2,1,0:T(8,128)(2,1)S(1)}) custom-call(s32[4]{0:T(128)S(1)} %get-tuple-element.345.starts_ref, s32[1]{0:T(128)} %bitcast.7.core_ref, ...), custom_call_target="tpu_custom_call" | custom-call | flops 3600000000 | bytes 1000 | tf_op jit(solution)/shard_map/attn_solve/pallas_call | solution.py:391
  76.7 12.0 %attn_solve.3 = (bf16[512,384]{1,0:T(8,128)(2,1)S(1)}, f32[512,384]{1,0:T(8,128)S(1)}, f32[512,3]{1,0:T(8,128)S(1)}, bf16[3,512,512]{2,1,0:T(8,128)(2,1)}, bf16[3,2,256,256]{3,2,1,0:T(8,128)(2,1)S(1)}) custom-call(s32[4]{0:T(128)S(1)} %get-tuple-element.344.starts_ref, s32[1]{0:T(128)} %bitcast.7.core_ref, ...), custom_call_target="tpu_custom_call" | custom-call | flops 3600000000 | bytes 1000 | tf_op jit(solution)/shard_map/attn_solve/pallas_call | solution.py:391
  89.7 10.6 %collective-permute-done.6.qv1_ref = bf16[768,768]{1,0:T(8,128)(2,1)S(1)} collective-permute-done((bf16[768,768]{1,0:T(8,128)(2,1)S(1)}, bf16[768,768]{1,0:T(8,128)(2,1)S(1)}, u32[]{:S(2)}, u32[]{:S(2)}) %collective-permute-start.6) | collective-permute-done | bytes 1179680 | tf_op jit(solution)/shard_map/ppermute | solution.py:676
  101.2 8.7 %attn_forward.2 = (bf16[512,384]{1,0:T(8,128)(2,1)S(1)}, bf16[512,384]{1,0:T(8,128)(2,1)S(1)}, bf16[512,384]{1,0:T(8,128)(2,1)S(1)}, bf16[3,512,512]{2,1,0:T(8,1...) custom-call(s32[4]{0:T(128)S(1)} %get-tuple-element.345.starts_ref, s32[1]{0:T(128)} %bitcast.7.core_ref, ...), custom_call_target="tpu_custom_call" | custom-call | flops 2700000000 | bytes 1000 | tf_op jit(solution)/shard_map/attn_forward/pallas_call | solution.py:411
  138.7 8.8 %attn_forward.3 = (bf16[512,384]{1,0:T(8,128)(2,1)S(1)}, bf16[512,384]{1,0:T(8,128)(2,1)S(1)}, bf16[512,384]{1,0:T(8,128)(2,1)S(1)}, bf16[3,512,512]{2,1,0:T(8,1...) custom-call(s32[4]{0:T(128)S(1)} %get-tuple-element.344.starts_ref, s32[1]{0:T(128)} %bitcast.7.core_ref, ...), custom_call_target="tpu_custom_call" | custom-call | flops 2700000000 | bytes 1000 | tf_op jit(solution)/shard_map/attn_forward/pallas_call | solution.py:411
  157.9 15.1 %collective-permute-done.11 = bf16[256,1536]{1,0:T(8,128)(2,1)} collective-permute-done((bf16[256,1536]{1,0:T(8,128)(2,1)}, bf16[256,1536]{1,0:T(8,128)(2,1)}, u32[]{:S(2)}, u32[]{:S(2)}) %collective-permute-start.11) | collective-permute-done | bytes 786464 | tf_op jit(solution)/shard_map/ppermute | solution.py:684
  179.6 13.7 %collective-permute-done.17.refs_9_.refs_7_ = bf16[768,1024]{1,0:T(8,128)(2,1)} collective-permute-done((bf16[768,1024]{1,0:T(8,128)(2,1)}, bf16[768,1024]{1,0:T(8,128)(2,1)}, u32[]{:S(2)}, u32[]{:S(2)}) %collective-permute-start.17) | collective-permute-done | bytes 1572896 | tf_op jit(solution)/shard_map/ppermute | solution.py:676
  193.3 16.9 %ffn_up.1 = (bf16[1024,1024]{1,0:T(8,128)(2,1)}, bf16[1024,1024]{1,0:T(8,128)(2,1)}, bf16[1024,1024]{1,0:T(8,128)(2,1)}, bf16[1024,768]{1,0:T(8,128)(2,1)}, bf16[1024,768]{1,0:T(8,128)(2,1)}) custom-call(bf16[256,1536]{1,0:T(8,128)(2,1)S(1)} %multiply_convert_fusion.2.refs_0_, bf16[256,1536]{1,0:T(8,128)(2,1)} %collective-permute-done.12.refs_1_, ...), custom_call_target="tpu_custom_call" | custom-call | flops 4800000000 | bytes 1000 | tf_op jit(solution)/shard_map/ffn_up/pallas_call | solution.py:607
  210.2 13.1 %ffn_down.2 = (bf16[512,1024]{1,0:T(8,128)(2,1)S(1)}, bf16[512,1024]{1,0:T(8,128)(2,1)S(1)}, f32[256,1536]{1,0:T(8,128)S(1)}, bf16[256,1536]{1,0:T(8,128)(2,1)S(1)}) custom-call(bf16[256,1536]{1,0:T(8,128)(2,1)S(1)} %bitcast.125, bf16[256,1536]{1,0:T(8,128)(2,1)S(1)} %get-tuple-element.323.refs_5_.refs_1_, bf16[1024,1024]{1,0:T(8,128)(2,1)} %get-tuple-element.171.refs_2_, ...), custom_call_target="tpu_custom_call" | custom-call | flops 3900000000 | bytes 1000 | tf_op jit(solution)/shard_map/ffn_down/pallas_call | solution.py:661
  228.8 14.0 %ffn_down.3 = (bf16[512,1024]{1,0:T(8,128)(2,1)S(1)}, bf16[512,1024]{1,0:T(8,128)(2,1)S(1)}, f32[256,1536]{1,0:T(8,128)S(1)}, bf16[256,1536]{1,0:T(8,128)(2,1)}) custom-call(bf16[256,1536]{1,0:T(8,128)(2,1)S(1)} %bitcast.123, bf16[256,1536]{1,0:T(8,128)(2,1)S(1)} %copy-done.2, bf16[1024,1024]{1,0:T(8,128)(2,1)} %get-tuple-element.171.refs_2_, ...), custom_call_target="tpu_custom_call" | custom-call | flops 3900000000 | bytes 1000 | tf_op jit(solution)/shard_map/ffn_down/pallas_call | solution.py:661
  249.5 7.7 %ffn_grad.2 = (bf16[768,1024]{1,0:T(8,128)(2,1)}, bf16[768,1024]{1,0:T(8,128)(2,1)}) custom-call(bf16[256,1536]{1,0:T(8,128)(2,1)S(1)} %copy-done.13, bf16[256,1536]{1,0:T(8,128)(2,1)} %collective-permute-done.12.refs_1_, bf16[256,1536]{1,0:T(8,128)(2,1)} %multiply_convert_fusion.1.refs_2_, bf16[256,1536]{1,0:T(8,128)(2,1)} %collective-permute-done.13.refs_3_, ...), custom_call_target="tpu_custom_call" | custom-call | flops 1800000000 | bytes 1000 | tf_op jit(solution)/shard_map/ffn_grad/pallas_call | solution.py:505
  277.3 20.1 %attn_backward.2 = (bf16[512,896]{1,0:T(8,128)(2,1)}, bf16[512,768]{1,0:T(8,128)(2,1)S(1)}, f32[256,1536]{1,0:T(8,128)}, bf16[256,1536]{1,0:T(8,128)(2,1)S(1)}, f32[1,1536]{1,0:T(1,128)S(1)}) custom-call(s32[4]{0:T(128)S(1)} %get-tuple-element.345.starts_ref, s32[1]{0:T(128)} %bitcast.7.core_ref, bf16[512,384]{1,0:T(8,128)(2,1)S(1)} %copy-done.47, ...), custom_call_target="tpu_custom_call" | custom-call | flops 6300000256 | bytes 1000 | tf_op jit(solution)/shard_map/attn_backward/pallas_call | solution.py:433
  323.0 7.7 %ffn_grad.3 = (bf16[768,1024]{1,0:T(8,128)(2,1)}, bf16[768,1024]{1,0:T(8,128)(2,1)}) custom-call(bf16[256,1536]{1,0:T(8,128)(2,1)S(1)} %copy-done.13, bf16[256,1536]{1,0:T(8,128)(2,1)} %collective-permute-done.12.refs_1_, bf16[256,1536]{1,0:T(8,128)(2,1)} %multiply_convert_fusion.1.refs_2_, bf16[256,1536]{1,0:T(8,128)(2,1)} %collective-permute-done.13.refs_3_, ...), custom_call_target="tpu_custom_call" | custom-call | flops 1800000000 | bytes 1000 | tf_op jit(solution)/shard_map/ffn_grad/pallas_call | solution.py:505
  332.3 20.0 %attn_backward.3 = (bf16[512,896]{1,0:T(8,128)(2,1)}, bf16[512,768]{1,0:T(8,128)(2,1)S(1)}, f32[256,1536]{1,0:T(8,128)}, bf16[256,1536]{1,0:T(8,128)(2,1)S(1)}, f32[1,1536]{1,0:T(1,128)S(1)}) custom-call(s32[4]{0:T(128)S(1)} %get-tuple-element.344.starts_ref, s32[1]{0:T(128)} %bitcast.7.core_ref, bf16[512,384]{1,0:T(8,128)(2,1)S(1)} %copy-done.43, ...), custom_call_target="tpu_custom_call" | custom-call | flops 6300000256 | bytes 1000 | tf_op jit(solution)/shard_map/attn_backward/pallas_call | solution.py:433
  360.1 12.9 %attn_grad.1 = (bf16[768,1024]{1,0:T(8,128)(2,1)}, bf16[768,1024]{1,0:T(8,128)(2,1)}, bf16[768,1024]{1,0:T(8,128)(2,1)}, bf16[768,1024]{1,0:T(8,128)(2,1)}) custom-call(s32[1]{0:T(128)} %bitcast.7.core_ref, bf16[256,1536]{1,0:T(8,128)(2,1)S(1)} %copy-done.7, bf16[256,1536]{1,0:T(8,128)(2,1)S(1)} %copy-done.11, bf16[256,1536]{1,0:T(8,128)(2,1)S(1)} %copy-done.5, ...), custom_call_target="tpu_custom_call" | custom-call | flops 4200000000 | bytes 1000 | tf_op jit(solution)/shard_map/attn_grad/pallas_call | solution.py:561
  386.2 22.8 %collective-permute-done.36 = bf16[768,1024]{1,0:T(8,128)(2,1)S(1)} collective-permute-done((bf16[768,1024]{1,0:T(8,128)(2,1)}, bf16[768,1024]{1,0:T(8,128)(2,1)S(1)}, u32[]{:S(2)}, u32[]{:S(2)}) %collective-permute-start.36) | collective-permute-done | bytes 1572896 | tf_op jit(solution)/shard_map/ppermute | solution.py:676
  421.0 11.2 %collective-permute-done.32 = bf16[768,512]{1,0:T(8,128)(2,1)S(1)} collective-permute-done((bf16[768,512]{1,0:T(8,128)(2,1)S(1)}, bf16[768,512]{1,0:T(8,128)(2,1)S(1)}, u32[]{:S(2)}, u32[]{:S(2)}) %collective-permute-start.32) | collective-permute-done | bytes 786464 | tf_op jit(solution)/shard_map/ppermute | solution.py:701
  453.8 13.0 %collective-permute-done.44 = bf16[768,1024]{1,0:T(8,128)(2,1)} collective-permute-done((bf16[768,1024]{1,0:T(8,128)(2,1)S(1)}, bf16[768,1024]{1,0:T(8,128)(2,1)}, u32[]{:S(2)}, u32[]{:S(2)}) %collective-permute-start.44) | collective-permute-done | bytes 1572896 | tf_op jit(solution)/shard_map/ppermute | solution.py:701
  472.4 8.8 %collective-permute-done.41 = bf16[768,512]{1,0:T(8,128)(2,1)S(1)} collective-permute-done((bf16[768,512]{1,0:T(8,128)(2,1)S(1)}, bf16[768,512]{1,0:T(8,128)(2,1)S(1)}, u32[]{:S(2)}, u32[]{:S(2)}) %collective-permute-start.41) | collective-permute-done | bytes 786464 | tf_op jit(solution)/shard_map/ppermute | solution.py:701
  485.5 10.5 %collective-permute-done.49 = bf16[768,512]{1,0:T(8,128)(2,1)S(1)} collective-permute-done((bf16[768,512]{1,0:T(8,128)(2,1)S(1)}, bf16[768,512]{1,0:T(8,128)(2,1)S(1)}, u32[]{:S(2)}, u32[]{:S(2)}) %collective-permute-start.49) | collective-permute-done | bytes 786464 | tf_op jit(solution)/shard_map/ppermute | solution.py:701
  517.5 16.1 %collective-permute-done.50 = bf16[768,512]{1,0:T(8,128)(2,1)S(1)} collective-permute-done((bf16[768,512]{1,0:T(8,128)(2,1)S(1)}, bf16[768,512]{1,0:T(8,128)(2,1)S(1)}, u32[]{:S(2)}, u32[]{:S(2)}) %collective-permute-start.50) | collective-permute-done | bytes 786464 | tf_op jit(solution)/shard_map/ppermute | solution.py:701
  539.4 16.6 %collective-permute-done.58 = bf16[768,512]{1,0:T(8,128)(2,1)S(1)} collective-permute-done((bf16[768,512]{1,0:T(8,128)(2,1)S(1)}, bf16[768,512]{1,0:T(8,128)(2,1)S(1)}, u32[]{:S(2)}, u32[]{:S(2)}) %collective-permute-start.58) | collective-permute-done | bytes 786464 | tf_op jit(solution)/shard_map/ppermute | solution.py:701
  (499 shorter events, 266.5 us)
Async XLA Ops:
  7.2 172.4 %all-gather.3.cloned.1.call-start = ((), (), s32[]{:S(2)}) async-start(), calls=%async_computation | async-start | bytes 1966080 | tf_op jit(solution)/shard_map/all_gather | solution.py:764
  60.9 39.3 %collective-permute-start.6 = (bf16[768,768]{1,0:T(8,128)(2,1)S(1)}, bf16[768,768]{1,0:T(8,128)(2,1)S(1)}, u32[]{:S(2)}, u32[]{:S(2)}) collective-permute-start(bf16[768,768]{1,0:T(8,128)(2,1)S(1)} %constant_dynamic-update-slice_fusion.qv0_ref), channel_id=1, source_target_pairs={{0,1},{1,0},{2,3},{3,2},{4,5},{5,4},{6,7},{7,6},{8,9},{9,8},{10,11... | collective-permute-start | bytes 3538952 | tf_op jit(solution)/shard_map/ppermute | solution.py:676
  121.6 34.5 %collective-permute-start.19 = (bf16[256,768]{1,0:T(8,128)(2,1)}, bf16[256,768]{1,0:T(8,128)(2,1)}, u32[]{:S(2)}, u32[]{:S(2)}) collective-permute-start(bf16[256,768]{1,0:T(8,128)(2,1)} %constant_dynamic-slice_fusion.7), channel_id=1, source_target_pairs={{0,1},{1,0},{2,3},{3,2},{4,5},{5,4},{6,7},{7,6},{8,9},{9,8},{10,11... | collective-permute-start | bytes 1179656 | tf_op jit(solution)/shard_map/ppermute | solution.py:676
  126.5 83.7 %all-gather.5.cloned.1.call-start = ((), (), s32[]{:S(2)}) async-start(), calls=%async_computation.1 | async-start | bytes 1966080 | tf_op jit(solution)/shard_map/all_gather | solution.py:764
  156.1 37.2 %collective-permute-start.17 = (bf16[768,1024]{1,0:T(8,128)(2,1)}, bf16[768,1024]{1,0:T(8,128)(2,1)}, u32[]{:S(2)}, u32[]{:S(2)}) collective-permute-start(bf16[768,1024]{1,0:T(8,128)(2,1)} %refs_6_.3), channel_id=1, source_target_pairs={{0,1},{1,0},{2,3},{3,2},{4,5},{5,4},{6,7},{7,6},{8,9},{9,8},{10,11... | collective-permute-start | bytes 4718600 | tf_op jit(solution)/shard_map/ppermute | solution.py:676
  157.7 35.6 %collective-permute-start.12 = (bf16[256,1536]{1,0:T(8,128)(2,1)S(1)}, bf16[256,1536]{1,0:T(8,128)(2,1)}, u32[]{:S(2)}, u32[]{:S(2)}) collective-permute-start(bf16[256,1536]{1,0:T(8,128)(2,1)S(1)} %multiply_convert_fusion.2.refs_0_), channel_id=1, source_target_pairs={{0,2},{2,0},{4,6},{6,4},{1,3},{3,1},{5,7},{7,5},{8,10},{10,8},{12,... | collective-permute-start | bytes 2359304 | tf_op jit(solution)/shard_map/ppermute | solution.py:680
  225.3 37.5 %collective-permute-start.23 = (bf16[1024,768]{1,0:T(8,128)(2,1)}, bf16[1024,768]{1,0:T(8,128)(2,1)}, u32[]{:S(2)}, u32[]{:S(2)}) collective-permute-start(bf16[1024,768]{1,0:T(8,128)(2,1)} %get-tuple-element.184), channel_id=1, source_target_pairs={{0,1},{1,0},{2,3},{3,2},{4,5},{5,4},{6,7},{7,6},{8,9},{9,8},{10,11... | collective-permute-start | bytes 4718600 | tf_op jit(solution)/shard_map/ppermute | solution.py:676
  257.2 40.2 %collective-permute-start.25 = (bf16[768,1024]{1,0:T(8,128)(2,1)}, bf16[768,1024]{1,0:T(8,128)(2,1)S(1)}, u32[]{:S(2)}, u32[]{:S(2)}) collective-permute-start(bf16[768,1024]{1,0:T(8,128)(2,1)} %get-tuple-element.186), channel_id=1, source_target_pairs={{0,1},{1,0},{2,3},{3,2},{4,5},{5,4},{6,7},{7,6},{8,9},{9,8},{10,11... | collective-permute-start | bytes 4718600 | tf_op jit(solution)/shard_map/ppermute | solution.py:676
  268.6 38.1 %collective-permute-start.24 = (bf16[1024,768]{1,0:T(8,128)(2,1)}, bf16[1024,768]{1,0:T(8,128)(2,1)}, u32[]{:S(2)}, u32[]{:S(2)}) collective-permute-start(bf16[1024,768]{1,0:T(8,128)(2,1)} %add_convert_fusion.5), channel_id=1, source_target_pairs={{0,8},{24,16},{1,9},{25,17},{2,10},{26,18},{3,11},{27,19},{4,12},{... | collective-permute-start | bytes 4718600 | tf_op jit(solution)/shard_map/ppermute | solution.py:701
  275.8 34.3 %collective-permute-start.22 = (bf16[256,1536]{1,0:T(8,128)(2,1)S(1)}, bf16[256,1536]{1,0:T(8,128)(2,1)S(1)}, u32[]{:S(2)}, u32[]{:S(2)}) collective-permute-start(bf16[256,1536]{1,0:T(8,128)(2,1)S(1)} %add_convert_fusion.24), channel_id=1, source_target_pairs={{0,4},{4,0},{2,6},{6,2},{1,5},{5,1},{3,7},{7,3},{8,12},{12,8},{10,... | collective-permute-start | bytes 2359304 | tf_op jit(solution)/shard_map/ppermute | solution.py:684
  313.9 41.2 %collective-permute-start.30 = (bf16[1024,768]{1,0:T(8,128)(2,1)}, bf16[1024,768]{1,0:T(8,128)(2,1)}, u32[]{:S(2)}, u32[]{:S(2)}) collective-permute-start(bf16[1024,768]{1,0:T(8,128)(2,1)} %add_convert_fusion.3), channel_id=1, source_target_pairs={{8,16},{16,8},{9,17},{17,9},{10,18},{18,10},{11,19},{19,11},{12,20... | collective-permute-start | bytes 4718600 | tf_op jit(solution)/shard_map/ppermute | solution.py:701
  315.8 41.7 %collective-permute-start.29 = (bf16[768,1024]{1,0:T(8,128)(2,1)S(1)}, bf16[768,1024]{1,0:T(8,128)(2,1)}, u32[]{:S(2)}, u32[]{:S(2)}) collective-permute-start(bf16[768,1024]{1,0:T(8,128)(2,1)S(1)} %add_convert_fusion.4), channel_id=1, source_target_pairs={{0,8},{24,16},{1,9},{25,17},{2,10},{26,18},{3,11},{27,19},{4,12},{... | collective-permute-start | bytes 4718600 | tf_op jit(solution)/shard_map/ppermute | solution.py:701
  330.7 47.3 %collective-permute-start.28 = (bf16[768,1024]{1,0:T(8,128)(2,1)}, bf16[768,1024]{1,0:T(8,128)(2,1)}, u32[]{:S(2)}, u32[]{:S(2)}) collective-permute-start(bf16[768,1024]{1,0:T(8,128)(2,1)} %get-tuple-element.203), channel_id=1, source_target_pairs={{0,1},{1,0},{2,3},{3,2},{4,5},{5,4},{6,7},{7,6},{8,9},{9,8},{10,11... | collective-permute-start | bytes 4718600 | tf_op jit(solution)/shard_map/ppermute | solution.py:676
  373.0 36.0 %collective-permute-start.36 = (bf16[768,1024]{1,0:T(8,128)(2,1)}, bf16[768,1024]{1,0:T(8,128)(2,1)S(1)}, u32[]{:S(2)}, u32[]{:S(2)}) collective-permute-start(bf16[768,1024]{1,0:T(8,128)(2,1)} %get-tuple-element.219), channel_id=1, source_target_pairs={{0,1},{1,0},{2,3},{3,2},{4,5},{5,4},{6,7},{7,6},{8,9},{9,8},{10,11... | collective-permute-start | bytes 4718600 | tf_op jit(solution)/shard_map/ppermute | solution.py:676
  373.7 137.0 %collective-permute-start.52 = (bf16[256,1536]{1,0:T(8,128)(2,1)S(1)}, bf16[256,1536]{1,0:T(8,128)(2,1)}, u32[]{:S(2)}, u32[]{:S(2)}) collective-permute-start(bf16[256,1536]{1,0:T(8,128)(2,1)S(1)} %get-tuple-element.248), channel_id=1, source_target_pairs={{0,2},{2,0},{4,6},{6,4},{1,3},{3,1},{5,7},{7,5},{8,10},{10,8},{12,... | collective-permute-start | bytes 2359304 | tf_op jit(solution)/shard_map/ppermute | solution.py:680
  373.8 41.5 %collective-permute-start.34 = (bf16[768,1024]{1,0:T(8,128)(2,1)S(1)}, bf16[768,1024]{1,0:T(8,128)(2,1)S(1)}, u32[]{:S(2)}, u32[]{:S(2)}) collective-permute-start(bf16[768,1024]{1,0:T(8,128)(2,1)S(1)} %add_convert_fusion.1), channel_id=1, source_target_pairs={{8,16},{16,8},{9,17},{17,9},{10,18},{18,10},{11,19},{19,11},{12,20... | collective-permute-start | bytes 4718600 | tf_op jit(solution)/shard_map/ppermute | solution.py:701
  376.7 41.7 %collective-permute-start.33 = (bf16[1024,768]{1,0:T(8,128)(2,1)S(1)}, bf16[1024,768]{1,0:T(8,128)(2,1)S(1)}, u32[]{:S(2)}, u32[]{:S(2)}) collective-permute-start(bf16[1024,768]{1,0:T(8,128)(2,1)S(1)} %add_convert_fusion.2), channel_id=1, source_target_pairs={{8,0},{16,24},{9,1},{17,25},{10,2},{18,26},{11,3},{19,27},{12,4},{... | collective-permute-start | bytes 4718600 | tf_op jit(solution)/shard_map/ppermute | solution.py:701
  409.0 35.2 %collective-permute-start.40 = (bf16[768,1024]{1,0:T(8,128)(2,1)}, bf16[768,1024]{1,0:T(8,128)(2,1)}, u32[]{:S(2)}, u32[]{:S(2)}) collective-permute-start(bf16[768,1024]{1,0:T(8,128)(2,1)} %get-tuple-element.233), channel_id=1, source_target_pairs={{0,1},{1,0},{2,3},{3,2},{4,5},{5,4},{6,7},{7,6},{8,9},{9,8},{10,11... | collective-permute-start | bytes 4718600 | tf_op jit(solution)/shard_map/ppermute | solution.py:676
  432.2 34.6 %collective-permute-start.44 = (bf16[768,1024]{1,0:T(8,128)(2,1)S(1)}, bf16[768,1024]{1,0:T(8,128)(2,1)}, u32[]{:S(2)}, u32[]{:S(2)}) collective-permute-start(bf16[768,1024]{1,0:T(8,128)(2,1)S(1)} %add_convert_fusion), channel_id=1, source_target_pairs={{8,0},{16,24},{9,1},{17,25},{10,2},{18,26},{11,3},{19,27},{12,4},{... | collective-permute-start | bytes 4718600 | tf_op jit(solution)/shard_map/ppermute | solution.py:701
  471.6 40.5 %collective-permute-start.54 = (bf16[256,1536]{1,0:T(8,128)(2,1)S(1)}, bf16[256,1536]{1,0:T(8,128)(2,1)S(1)}, u32[]{:S(2)}, u32[]{:S(2)}) collective-permute-start(bf16[256,1536]{1,0:T(8,128)(2,1)S(1)} %get-tuple-element.252), channel_id=1, source_target_pairs={{0,2},{2,0},{4,6},{6,4},{1,3},{3,1},{5,7},{7,5},{8,10},{10,8},{12,... | collective-permute-start | bytes 2359304 | tf_op jit(solution)/shard_map/ppermute | solution.py:680
  501.5 33.6 %collective-permute-start.46 = (bf16[2,128,1536]{2,1,0:T(8,128)(2,1)S(1)}, bf16[2,128,1536]{2,1,0:T(8,128)(2,1)S(1)}, u32[]{:S(2)}, u32[]{:S(2)}) collective-permute-start(bf16[2,128,1536]{2,1,0:T(8,128)(2,1)S(1)} %fusion.17), channel_id=1, source_target_pairs={{0,4},{4,0},{2,6},{6,2},{1,5},{5,1},{3,7},{7,3},{8,12},{12,8},{10,... | collective-permute-start | bytes 2359304 | tf_op jit(solution)/shard_map/ppermute | solution.py:684
  512.1 48.1 %collective-permute-start.56 = (bf16[768,512]{1,0:T(8,128)(2,1)S(1)}, bf16[768,512]{1,0:T(8,128)(2,1)S(1)}, u32[]{:S(2)}, u32[]{:S(2)}) collective-permute-start(bf16[768,512]{1,0:T(8,128)(2,1)S(1)} %add_convert_fusion.9), channel_id=1, source_target_pairs={{8,16},{16,8},{9,17},{17,9},{10,18},{18,10},{11,19},{19,11},{12,20... | collective-permute-start | bytes 2359304 | tf_op jit(solution)/shard_map/ppermute | solution.py:701
  514.8 41.4 %collective-permute-start.57 = (bf16[2,128,1536]{2,1,0:T(8,128)(2,1)S(1)}, bf16[2,128,1536]{2,1,0:T(8,128)(2,1)S(1)}, u32[]{:S(2)}, u32[]{:S(2)}) collective-permute-start(bf16[2,128,1536]{2,1,0:T(8,128)(2,1)S(1)} %fusion.18), channel_id=1, source_target_pairs={{0,4},{4,0},{2,6},{6,2},{1,5},{5,1},{3,7},{7,3},{8,12},{12,8},{10,... | collective-permute-start | bytes 2359304 | tf_op jit(solution)/shard_map/ppermute | solution.py:684
  536.5 37.1 %collective-permute-start.55 = (bf16[2,128,768]{2,1,0:T(8,128)(2,1)}, bf16[2,128,768]{2,1,0:T(8,128)(2,1)}, u32[]{:S(2)}, u32[]{:S(2)}) collective-permute-start(bf16[2,128,768]{2,1,0:T(8,128)(2,1)} %slice.253), channel_id=1, source_target_pairs={{0,1},{1,0},{2,3},{3,2},{4,5},{5,4},{6,7},{7,6},{8,9},{9,8},{10,11... | collective-permute-start | bytes 1179656 | tf_op jit(solution)/shard_map/ppermute | solution.py:676
  (164 other events, 1914.8 us)
Sparse Core Ops, SparseCore 0:
  126.7 37.4 all-gather.2
  165.7 35.9 all-gather.4
